TPU v7x, 128 devices: a whole 4x4x4 slice. The times are simulated.
128 devices in a mesh: ns: 8 (over y, core), ew: 16 (over z, x).
Axes of the slice: x: 4, y: 4, z: 4, core: 2. Of those that a mesh axis runs over, the one named last changes fastest.
Arguments:
- fields: bfloat16 [64, 64, 2048], P(None, 'ns', 'ew'), may hold values from -6 to 6
- w_in: bfloat16 [64, 192], replicated, may hold values from -0.75 to 0.75
- conv_first: bfloat16 [3, 3, 192, 192], replicated, may hold values from -0.15625 to 0.15625
- conv_second: bfloat16 [3, 3, 192, 192], replicated, may hold values from -0.15625 to 0.15625
- w_out: bfloat16 [192, 6], replicated, may hold values from -0.4375 to 0.4375
- slot_cells: int32 [128, 4, 16384], P(('ns', 'ew')), may hold values from 0 to 1023
- slot_weights: float32 [128, 4, 16384], P(('ns', 'ew')), may hold values from 0 to 1
- slot_count: int32 [128, 128], P(('ns', 'ew')), may hold values from 0 to 128, as said below
- recv_obs: int32 [128, 16384], P(('ns', 'ew')), may hold values from 0 to 2047
- targets: float32 [6, 262144], P(None, ('ns', 'ew')), may hold values from -6 to 6
Outputs:
- station_pred: float32 [6, 262144], P(None, ('ns', 'ew'))
- loss: float32 [], replicated
- grad_first: float32 [3, 3, 192, 192], replicated
- grad_second: float32 [3, 3, 192, 192], replicated
- grad_in: float32 [64, 192], replicated
- grad_out: float32 [192, 6], replicated
- grad_fields: float32 [64, 64, 2048], P(None, 'ns', 'ew')
Inputs may be any that keep to these rules, and one draw needn't show every extreme that they name: `slot_cells`: local cell numbers of a tile, row-major. `slot_count`: every row has a column equal to 128.
All inputs are finite; a program needn't handle non-finite values.
Results may differ from a plain program's by a relative error of at most 0.008.
Values may be sent and summed in bfloat16 or wider, within the bound.
No kernel may reach another device: no remote copies, remote signals or barrier semaphores. Data moves between devices by JAX's collectives and lax.ppermute only.
A program may use at most 64 MiB of HBM per device.

v0:
```python
import functools

import jax
import jax.numpy as jnp
from jax import lax
from jax.experimental import pallas as pl
from jax.experimental.pallas import tpu as pltpu
from jax.sharding import PartitionSpec as P

BF = jnp.bfloat16
F32 = jnp.float32
CAP = 128
TH, TW = 8, 128
ROW = 144
N12, N10, N8 = 12 * ROW, 10 * ROW, 8 * ROW
CP = 256
AXES = ("ns", "ew")
PIECE = 48
NT = (((1,), (1,)), ((), ()))
TN = (((0,), (0,)), ((), ()))
PARAMS = pltpu.CompilerParams(vmem_limit_bytes=60 * 1024 * 1024)


def dot(x, y, dims=(((1,), (0,)), ((), ()))):
    return lax.dot_general(x, y, dims, preferred_element_type=F32)


def taps(cat, weight, first, count, order):
    total = None
    for a in range(3):
        start = (a if order > 0 else 2 - a) * ROW + first
        term = dot(cat[start : start + count, :], weight[a])
        total = term if total is None else total + term
    return total


def pick(table_row, index):
    return jnp.take_along_axis(
        jnp.broadcast_to(table_row, (8, 128)), index, axis=1, mode="promise_in_bounds"
    )


def forward_kernel(
    flags, ft, win, w1, w2, wo, cells, wts, cnt, out, xcat, acat, gp, h2b_out, hs, as_, fs, pf
):
    zero8 = jnp.zeros((8, CP), F32)
    hs[0:8, :] = zero8
    hs[N12 + 8 : N12 + 16, :] = zero8
    as_[0:8, :] = zero8
    as_[N10 + 8 : N10 + 16, :] = zero8
    hs[8 : N12 + 8, :] = dot(ft[...], win[...])
    for b in range(3):
        xcat[:, b * CP : (b + 1) * CP] = hs[7 + b : 7 + b + N12, :].astype(BF)
    col = lax.broadcasted_iota(jnp.int32, (ROW, CP), 0)
    col_mask = jnp.where(col == 1, flags[2], jnp.where(col == 130, flags[3], 1.0))
    root = 0.7978845608028654
    for part in range(5):
        z2 = taps(xcat, w1, part * 2 * ROW, 2 * ROW, 1)
        for q in range(2):
            r = part * 2 + q
            z = z2[q * ROW : (q + 1) * ROW]
            mask = col_mask
            if r == 0:
                mask = col_mask * flags[0]
            if r == 9:
                mask = col_mask * flags[1]
            zz = z * z
            t = jnp.tanh(root * z * (1.0 + 0.044715 * zz))
            half = 0.5 * (1.0 + t)
            slope = half + 0.5 * z * (1.0 - t * t) * (root * (1.0 + 3 * 0.044715 * zz))
            as_[8 + r * ROW : 8 + (r + 1) * ROW, :] = z * half * mask
            gp[r * ROW : (r + 1) * ROW, :] = slope * mask
    for b in range(3):
        acat[:, b * CP : (b + 1) * CP] = as_[7 + b : 7 + b + N10, :].astype(BF)
    for part in range(4):
        at = part * 2 * ROW
        h2 = hs[8 + 2 * ROW + at : 8 + 4 * ROW + at, :] + taps(acat, w2, at, 2 * ROW, 1)
        h2b_out[at : at + 2 * ROW, :] = h2.astype(BF)
    field = dot(wo[...], h2b_out[...], NT)
    for r in range(8):
        fs[r * 8 : (r + 1) * 8, :] = field[0:8, r * ROW + 2 : r * ROW + 2 + TW]
    pf[...] = jnp.zeros_like(pf)
    lane = lax.broadcasted_iota(jnp.int32, (8, 128), 1)

    def owners(ob, carry):
        rows = pl.ds(pl.multiple_of(ob * 8, 8), 8)
        live = lane < cnt[rows, 0:1]
        index = [cells[k, rows, :] for k in range(4)]
        low = [i & 127 for i in index]
        high = [i >> 7 for i in index]
        weight = [jnp.where(live, wts[k, rows, :], 0.0) for k in range(4)]
        for v in range(6):
            got = [jnp.zeros((8, 128), F32)] * 4
            for r in range(8):
                row = fs[r * 8 + v : r * 8 + v + 1, :]
                got = [
                    jnp.where(high[k] == r, pick(row, low[k]), got[k]) for k in range(4)
                ]
            value = sum(weight[k] * got[k] for k in range(4))
            pf[pl.ds(ob * 64 + v, 8, stride=8), :] = value
        return carry

    lax.fori_loop(0, 16, owners, 0)
    out[...] = pf[...].astype(BF)


def one_hot_rows(low_row, iotas):
    spread = jnp.broadcast_to(low_row, (16, 128)).astype(BF)
    one, zero = jnp.ones((16, 128), BF), jnp.zeros((16, 128), BF)
    return [jnp.where(spread == i, one, zero) for i in iotas]


def low_iotas():
    base = lax.broadcasted_iota(jnp.int32, (16, 128), 0)
    return [(base + 16 * m).astype(F32).astype(BF) for m in range(8)]


def owner_kernel(recv, obs, target, pred, loss, out, left, right, rs, gf):
    iotas = low_iotas()

    def collect(tb, carry):
        block = recv[pl.ds(pl.multiple_of(tb * 64, 64), 64), :].astype(F32)
        index = obs[pl.ds(pl.multiple_of(tb * 8, 8), 8), :]
        low = (index & 127).astype(F32)
        high = index >> 7
        for i in range(8):
            at = pl.ds(pl.multiple_of(tb * 1024 + i * 128, 128), 128)
            mine = jnp.broadcast_to(high[i : i + 1], (8, 128))
            value = block[i * 8 : i * 8 + 8]
            for h in range(8):
                two = [jnp.where(mine == 2 * h + e, value, 0.0) for e in range(2)]
                left[h * 16 : h * 16 + 16, at] = jnp.concatenate(two, 0).astype(BF)
            for m, hot in enumerate(one_hot_rows(low[i : i + 1], iotas)):
                right[m * 16 : m * 16 + 16, at] = hot
        return carry

    lax.fori_loop(0, 16, collect, 0)
    total = dot(left[...], right[...], NT)
    scale = 1.0 / (6 * 2048)
    squares = jnp.zeros((6, 128), F32)
    for h in range(16):
        at = slice(h * 128, h * 128 + 128)
        mine = total[h * 8 : h * 8 + 6]
        pred[:, at] = mine
        resid = mine - target[:, at]
        squares = squares + resid * resid
        rs[h * 8 : h * 8 + 6, :] = resid * scale
    loss[...] = jnp.full((16, 128), jnp.sum(squares) * (0.5 * scale), F32)
    gf[...] = jnp.zeros_like(gf)

    def choose(tb, carry):
        index = obs[pl.ds(pl.multiple_of(tb * 8, 8), 8), :]
        low, high = index & 127, index >> 7
        got = [jnp.zeros((8, 128), F32)] * 6
        for h in range(16):
            here = high == h
            got = [
                jnp.where(here, pick(rs[h * 8 + v : h * 8 + v + 1, :], low), got[v])
                for v in range(6)
            ]
        for v in range(6):
            gf[pl.ds(tb * 64 + v, 8, stride=8), :] = got[v]
        return carry

    lax.fori_loop(0, 16, choose, 0)
    out[...] = gf[...].astype(BF)


def spread_kernel(grad, cells, wts, cnt, out, left, right):
    iotas = low_iotas()
    out[...] = jnp.zeros_like(out)
    lane = lax.broadcasted_iota(jnp.int32, (8, 128), 1)

    def owners(ob, carry):
        rows = pl.ds(pl.multiple_of(ob * 8, 8), 8)
        live = lane < cnt[rows, 0:1]
        block = grad[pl.ds(pl.multiple_of(ob * 64, 64), 64), :].astype(F32)
        for k in range(4):
            index = cells[k, rows, :]
            low = (index & 127).astype(F32)
            high = index >> 7
            weight = jnp.where(live, wts[k, rows, :], 0.0)
            for i in range(8):
                at = slice((k * 8 + i) * 128, (k * 8 + i) * 128 + 128)
                mine = jnp.broadcast_to(high[i : i + 1], (8, 128))
                value = block[i * 8 : i * 8 + 8] * jnp.broadcast_to(weight[i : i + 1], (8, 128))
                for h in range(4):
                    two = [jnp.where(mine == 2 * h + e, value, 0.0) for e in range(2)]
                    left[h * 16 : h * 16 + 16, at] = jnp.concatenate(two, 0).astype(BF)
                for m, hot in enumerate(one_hot_rows(low[i : i + 1], iotas)):
                    right[m * 16 : m * 16 + 16, at] = hot
        out[...] += dot(left[...], right[...], NT)
        return carry

    lax.fori_loop(0, 16, owners, 0)


def backward_kernel(
    gfn, ft, xcat, acat, gp, h2b, w2t, w1t, win, wo, loss, pay, gfields, gs, g2cat, zs, gzcat, own
):
    zero8 = jnp.zeros((8, CP), F32)
    gs[0:8, :] = zero8
    gs[N12 + 8 : N12 + 16, :] = zero8
    zs[0:8, :] = zero8
    zs[N10 + 8 : N10 + 16, :] = zero8
    x = gfn[...]
    x_hi = x.astype(BF)
    x_lo = (x - x_hi.astype(F32)).astype(BF)
    gs[8 : N12 + 8, :] = dot(x_hi, wo[...]) + dot(x_lo, wo[...])
    for b in range(3):
        g2cat[:, b * CP : (b + 1) * CP] = gs[9 - b : 9 - b + N12, :].astype(BF)
    for part in range(5):
        at = part * 2 * ROW
        g = taps(g2cat, w2t, at, 2 * ROW, -1)
        zs[8 + at : 8 + at + 2 * ROW, :] = g * gp[at : at + 2 * ROW, :]
    for b in range(3):
        gzcat[:, b * CP : (b + 1) * CP] = zs[9 - b : 9 - b + N10, :].astype(BF)
    col = lax.broadcasted_iota(jnp.int32, (ROW, CP), 0)
    keep = jnp.where((col >= 2) & (col < 2 + TW), 1.0, 0.0)
    keep2 = jnp.concatenate([keep, keep], 0)
    for part in range(4):
        at = part * 2 * ROW
        g = gs[8 + 2 * ROW + at : 8 + 4 * ROW + at, :] + taps(gzcat, w1t, at, 2 * ROW, -1)
        own[at : at + 2 * ROW, :] = (g * keep2).astype(BF)
    g_in = dot(ft[2 * ROW : 10 * ROW, :], own[...], TN)
    g_fields = dot(win[...], own[...], NT)
    for r in range(8):
        gfields[pl.ds(r, 64, stride=8), :] = g_fields[:, r * ROW + 2 : r * ROW + 2 + TW]
    small = keep[:, 0:8]
    x_own = x[2 * ROW : 10 * ROW] * jnp.concatenate([small] * 8, 0)
    o_hi = x_own.astype(BF)
    o_lo = (x_own - o_hi.astype(F32)).astype(BF)
    g_out = dot(o_hi, h2b[...], TN) + dot(o_lo, h2b[...], TN)

    for part in range(4):
        at = part * 2 * ROW
        own[at : at + 2 * ROW, :] = (gs[8 + 2 * ROW + at : 8 + 4 * ROW + at, :] * keep2).astype(BF)
    second_t = own[...].T[0:192]
    for part in range(4):
        at = part * 2 * ROW
        own[at : at + 2 * ROW, :] = (zs[8 + ROW + at : 8 + 3 * ROW + at, :] * keep2).astype(BF)
    first_t = own[...].T[0:192]
    for a in range(3):
        y2 = dot(second_t, acat[a * ROW : a * ROW + N8, :])
        y1 = dot(first_t, xcat[(1 + a) * ROW : (1 + a) * ROW + N8, :])
        for b in range(3):
            at = (a * 3 + b) * 192
            pay[at : at + 192, :] = y2[:, b * CP : b * CP + 128].astype(BF)
            pay[1728 + at : 1728 + at + 192, :] = y1[:, b * CP : b * CP + 128].astype(BF)
            rest2 = y2[:, b * CP + 128 : b * CP + 256]
            rest1 = y1[:, b * CP + 128 : b * CP + 256]
            pay[3456 + at : 3456 + at + 192, :] = (rest2 + pltpu.roll(rest1, 64, 1)).astype(BF)
    pay[5184:5248, :] = g_in[:, 0:128].astype(BF)
    pay[5248:5312, :] = g_in[:, 128:256].astype(BF)
    pay[5312:5328, :] = jnp.concatenate([g_out[:, 0:128], g_out[:, 128:256]], 0).astype(BF)
    pay[5328:5344, :] = loss[...].astype(BF)
    pay[5344:, :] = jnp.zeros((128 * PIECE - 5344, 128), BF)


def neighbours(array, axis, dim, width):
    count, length = lax.axis_size(axis), array.shape[dim]
    up = [(i, i + 1) for i in range(count - 1)]
    down = [(j, i) for i, j in up]
    last = lax.slice_in_dim(array, length - width, length, axis=dim)
    first = lax.slice_in_dim(array, 0, width, axis=dim)
    before = lax.ppermute(last, axis, up)
    after = lax.ppermute(first, axis, down)
    return jnp.concatenate([before, array, after], axis=dim)


def exchange(rows):
    return lax.all_to_all(rows, AXES, split_axis=0, concat_axis=0, tiled=True)


def call(kernel, out_shapes, scratch, *operands, smem=0):
    specs = [pl.BlockSpec(memory_space=pltpu.SMEM)] * smem + [
        pl.BlockSpec(memory_space=pltpu.VMEM)
    ] * (len(operands) - smem)
    return pl.pallas_call(
        kernel,
        out_shape=[jax.ShapeDtypeStruct(s, d) for s, d in out_shapes],
        in_specs=specs,
        out_specs=[pl.BlockSpec(memory_space=pltpu.VMEM)] * len(out_shapes),
        scratch_shapes=[pltpu.VMEM(s, d) for s, d in scratch],
        compiler_params=PARAMS,
    )(*operands)


def stacked(kernel):
    padded = jnp.pad(kernel, ((0, 0), (0, 0), (0, CP - 192), (0, CP - 192)))
    return padded.reshape(3, 3 * CP, CP)


def on_device(
    fields,
    w_in,
    conv_first,
    conv_second,
    w_out,
    slot_cells,
    slot_weights,
    slot_count,
    recv_obs,
    targets,
):
    ns, ew = lax.axis_index("ns"), lax.axis_index("ew")
    flags = jnp.stack(
        [ns > 0, ns < lax.axis_size("ns") - 1, ew > 0, ew < lax.axis_size("ew") - 1]
    ).astype(F32)
    cells = slot_cells.reshape(4, 128, CAP)
    wts = slot_weights.reshape(4, 128, CAP)
    cnt = slot_count.reshape(128, 1)
    obs = recv_obs.reshape(128, CAP)
    win = jnp.pad(w_in, ((0, 0), (0, CP - 192)))
    wo = jnp.pad(w_out.T, ((0, 2), (0, CP - 192)))
    wo16 = jnp.pad(wo, ((0, 8), (0, 0)))

    grid = fields.transpose(1, 2, 0)
    grid = neighbours(grid, "ns", 0, 2)
    grid = neighbours(grid, "ew", 1, 2)
    ft = jnp.pad(grid, ((0, 0), (0, ROW - TW - 4), (0, 0))).reshape(N12, 64)
    sent, xcat, acat, gp, h2b = call(
        forward_kernel,
        [((1024, 128), BF), ((N12, 3 * CP), BF), ((N10, 3 * CP), BF), ((N10, CP), F32), ((N8, CP), BF)],
        [((N12 + 16, CP), F32), ((N10 + 16, CP), F32), ((64, 128), F32), ((1024, 128), F32)],
        flags, ft, win, stacked(conv_first), stacked(conv_second), wo16, cells, wts, cnt,
        smem=1,
    )
    received = exchange(sent)
    pred, loss, back = call(
        owner_kernel,
        [((6, 2048), F32), ((16, 128), F32), ((1024, 128), BF)],
        [((128, 16384), BF), ((128, 16384), BF), ((128, 128), F32), ((1024, 128), F32)],
        received, obs, targets,
    )
    grads = exchange(back)
    (g_field,) = call(
        spread_kernel,
        [((64, 128), F32)],
        [((64, 4096), BF), ((128, 4096), BF)],
        grads, cells, wts, cnt,
    )
    g_field = neighbours(g_field.reshape(8, 8, 128), "ns", 0, 2)
    g_field = neighbours(g_field, "ew", 2, 2).transpose(0, 2, 1)
    gfn = jnp.pad(g_field, ((0, 0), (0, ROW - TW - 4), (0, 0))).reshape(N12, 8)
    swap = (0, 1, 3, 2)
    pay, g_fields = call(
        backward_kernel,
        [((128 * PIECE, 128), BF), ((512, 128), F32)],
        [
            ((N12 + 16, CP), F32), ((N12, 3 * CP), BF), ((N10 + 16, CP), F32),
            ((N10, 3 * CP), BF), ((N8, CP), BF),
        ],
        gfn, ft, xcat, acat, gp, h2b,
        stacked(conv_second.transpose(swap)), stacked(conv_first.transpose(swap)), win, wo, loss,
    )
    share = jnp.sum(exchange(pay.reshape(128, PIECE, 128)).astype(F32), axis=0).astype(BF)
    whole = exchange(jnp.broadcast_to(share[None], (128, PIECE, 128)))
    whole = whole.reshape(128 * PIECE, 128).astype(F32)
    rest = whole[3456:5184].reshape(3, 3, 192, 128)
    second = whole[0:1728].reshape(3, 3, 192, 128)
    first = whole[1728:3456].reshape(3, 3, 192, 128)
    grad_second = jnp.concatenate([second, rest[..., :64]], -1).transpose(swap)
    grad_first = jnp.concatenate([first, rest[..., 64:]], -1).transpose(swap)
    grad_in = jnp.concatenate([whole[5184:5248], whole[5248:5312, :64]], 1)
    grad_out = jnp.concatenate([whole[5312:5318], whole[5320:5326, :64]], 1).T
    return (
        pred,
        whole[5328, 0],
        grad_first,
        grad_second,
        grad_in,
        grad_out,
        g_fields.reshape(64, TH, TW),
    )


def solution(mesh):
    in_specs = (
        P(None, "ns", "ew"),
        P(),
        P(),
        P(),
        P(),
        P(("ns", "ew"), None, None),
        P(("ns", "ew"), None, None),
        P(("ns", "ew"), None),
        P(("ns", "ew"), None),
        P(None, ("ns", "ew")),
    )
    out_specs = (P(None, ("ns", "ew")), P(), P(), P(), P(), P(), P(None, "ns", "ew"))
    return jax.shard_map(
        on_device, mesh=mesh, in_specs=in_specs, out_specs=out_specs, check_vma=False
    )
```

profile of v0, /device:TPU:1, one launch (start us, length us, event | category | flops | bytes accessed | tf_op | source)
XLA Modules:
  0.0 205.3 jit_solution(12412705478042056202)
XLA Ops:
  0.6 1.1 fusion.3
  1.7 3.3 %collective-permute-start.1 = (bf16[2,128,64]{1,0,2:T(2,128)(2,1)S(1)}, bf16[2,128,64]{1,0,2:T(2,128)(2,1)S(1)}, u32[]{:S(2)}, u32[]{:S(2)}) collective-permute-start(bf16[2,128,64]{1,0,2:T(2,128)(2,1)S(1)} %get-tuple-element.49), channel_id=1, source_target_pairs={{16,0},{32,16},{48,32},{64,48},{80,64},{96,80},{112,96},{17,1},{33... | collective-permute-start | bytes 98312 | tf_op jit(solution)/shard_map/ppermute | solution.py:267
  5.1 3.2 %collective-permute-start = (bf16[2,128,64]{1,0,2:T(2,128)(2,1)S(1)}, bf16[2,128,64]{1,0,2:T(2,128)(2,1)S(1)}, u32[]{:S(2)}, u32[]{:S(2)}) collective-permute-start(bf16[2,128,64]{1,0,2:T(2,128)(2,1)S(1)} %get-tuple-element.48), channel_id=1, source_target_pairs={{0,16},{16,32},{32,48},{48,64},{64,80},{80,96},{96,112},{1,17},{17... | collective-permute-start | bytes 98312 | tf_op jit(solution)/shard_map/ppermute | solution.py:266
  8.3 1.0 collective-permute-done
  9.3 1.0 pad_maximum_fusion.1
  10.5 1.3 collective-permute-start.3
  11.8 4.0 %collective-permute-start.2 = (bf16[12,2,64]{1,0,2:T(8,128)(2,1)S(1)}, bf16[12,2,64]{1,0,2:T(8,128)(2,1)S(1)}, u32[]{:S(2)}, u32[]{:S(2)}) collective-permute-start(bf16[12,2,64]{1,0,2:T(8,128)(2,1)S(1)} %get-tuple-element.46), channel_id=1, source_target_pairs={{0,1},{1,2},{2,3},{3,4},{4,5},{5,6},{6,7},{7,8},{8,9},{9,10},{10,1... | collective-permute-start | bytes 9224 | tf_op jit(solution)/shard_map/ppermute | solution.py:266
  16.3 1.4 pad.34.win
  17.7 1.2 pad.35
  18.9 1.2 pad.36
  24.0 0.9 pad.33.clone
  24.9 18.3 %shard_map.153 = (bf16[1024,128]{1,0:T(8,128)(2,1)}, bf16[1728,768]{1,0:T(8,128)(2,1)}, bf16[1440,768]{1,0:T(8,128)(2,1)}, f32[1440,256]{1,0:T(8,128)}, bf16[1152,256]{1,0:T(8,128)(2,1)}) custom-call(f32[4]{0:T(128)} %add_convert_fusion.flags, bf16[1728,64]{1,0:T(8,128)(2,1)} %bitcast.55, bf16[64,256]{1,0:T(8,128)(2,1)} %pad.34.win, ...), custom_call_target="tpu_custom_call" | custom-call | tf_op jit(solution)/shard_map/pallas_call | solution.py:279
  43.2 24.9 %all_to_all.32 = bf16[128,8,128]{2,1,0:T(8,128)(2,1)} all-to-all(bf16[128,8,128]{2,1,0:T(8,128)(2,1)} %bitcast.81), channel_id=1, replica_groups=mesh['ns'=8,'ew'=16] {'ns','ew'}, dimensions={0} | all-to-all | bytes 524288 | tf_op jit(solution)/shard_map/all_to_all | solution.py:272
  68.2 8.3 %shard_map.154 = (f32[6,2048]{1,0:T(8,128)}, f32[16,128]{1,0:T(8,128)}, bf16[1024,128]{1,0:T(8,128)(2,1)}) custom-call(bf16[1024,128]{1,0:T(8,128)(2,1)} %bitcast.73, s32[128,128]{1,0:T(8,128)} %bitcast.83, f32[6,2048]{1,0:T(8,128)} %target.1), custom_call_target="tpu_custom_call" | custom-call | tf_op jit(solution)/shard_map/pallas_call | solution.py:279
  76.5 16.7 %all_to_all.33 = bf16[128,8,128]{2,1,0:T(8,128)(2,1)} all-to-all(bf16[128,8,128]{2,1,0:T(8,128)(2,1)} %bitcast.82), channel_id=1, replica_groups=mesh['ns'=8,'ew'=16] {'ns','ew'}, dimensions={0} | all-to-all | bytes 524288 | tf_op jit(solution)/shard_map/all_to_all | solution.py:272
  93.2 12.2 %shard_map.155 = f32[64,128]{1,0:T(8,128)} custom-call(bf16[1024,128]{1,0:T(8,128)(2,1)} %bitcast.72, s32[4,128,128]{2,1,0:T(8,128)} %bitcast.68, f32[4,128,128]{2,1,0:T(8,128)} %bitcast.70, s32[128,1]{1,0:T(8,128)} %copy.36.cnt), custom_call_target="tpu_custom_call" | custom-call | tf_op jit(solution)/shard_map/pallas_call | solution.py:279
  106.1 2.4 %collective-permute-start.5 = (f32[2,8,128]{2,1,0:T(8,128)S(1)}, f32[2,8,128]{2,1,0:T(8,128)S(1)}, u32[]{:S(2)}, u32[]{:S(2)}) collective-permute-start(f32[2,8,128]{2,1,0:T(8,128)S(1)} %get-tuple-element.53), channel_id=1, source_target_pairs={{16,0},{32,16},{48,32},{64,48},{80,64},{96,80},{112,96},{17,1},{33... | collective-permute-start | bytes 24584 | tf_op jit(solution)/shard_map/ppermute | solution.py:267
  108.5 3.2 %collective-permute-start.4 = (f32[2,8,128]{2,1,0:T(8,128)S(1)}, f32[2,8,128]{2,1,0:T(8,128)S(1)}, u32[]{:S(2)}, u32[]{:S(2)}) collective-permute-start(f32[2,8,128]{2,1,0:T(8,128)S(1)} %get-tuple-element.52), channel_id=1, source_target_pairs={{0,16},{16,32},{32,48},{48,64},{64,80},{80,96},{96,112},{1,17},{17... | collective-permute-start | bytes 24584 | tf_op jit(solution)/shard_map/ppermute | solution.py:266
  111.7 0.8 collective-permute-done.4
  112.5 0.8 pad_maximum_fusion.3
  113.3 1.3 collective-permute-start.7
  114.6 4.2 %collective-permute-start.6 = (f32[12,8,2]{2,1,0:T(8,128)S(1)}, f32[12,8,2]{2,1,0:T(8,128)S(1)}, u32[]{:S(2)}, u32[]{:S(2)}) collective-permute-start(f32[12,8,2]{2,1,0:T(8,128)S(1)} %get-tuple-element.50), channel_id=1, source_target_pairs={{0,1},{1,2},{2,3},{3,4},{4,5},{5,6},{6,7},{7,8},{8,9},{9,10},{10,1... | collective-permute-start | bytes 2312 | tf_op jit(solution)/shard_map/ppermute | solution.py:266
  118.8 0.8 copy.45
  119.6 1.2 pad.40.clone
  120.8 0.7 copy.46
  121.5 1.2 pad.41.clone
  123.2 1.0 pad.39.clone
  124.2 12.3 %shard_map.156 = (bf16[6144,128]{1,0:T(8,128)(2,1)}, f32[512,128]{1,0:T(8,128)}) custom-call(f32[1728,8]{1,0:T(8,128)} %bitcast.59, bf16[1728,64]{1,0:T(8,128)(2,1)} %bitcast.56, bf16[1728,768]{1,0:T(8,128)(2,1)} %get-tuple-element.20.xcat, bf16[1440,768]{1,0:T(8,128)(2,1)} %get-tuple-element.21.acat, f32[1440,256]{1,0:T(8,128)} %get-tuple-element.22.gp, ...), custom_call_target="tpu_custom_call" | custom-call | tf_op jit(solution)/shard_map/pallas_call | solution.py:279
  136.4 32.2 %all_to_all.34 = bf16[128,48,128]{2,1,0:T(8,128)(2,1)S(1)} all-to-all(bf16[128,48,128]{2,1,0:T(8,128)(2,1)} %bitcast.71), channel_id=1, replica_groups=mesh['ns'=8,'ew'=16] {'ns','ew'}, dimensions={0} | all-to-all | bytes 3145728 | tf_op jit(solution)/shard_map/all_to_all | solution.py:272
  169.1 28.4 %all_to_all.35 = bf16[128,48,128]{2,1,0:T(8,128)(2,1)S(1)} all-to-all(bf16[128,48,128]{2,1,0:T(8,128)(2,1)S(1)} %broadcast_in_dim.2), channel_id=1, replica_groups=mesh['ns'=8,'ew'=16] {'ns','ew'}, dimensions={0} | all-to-all | bytes 3145728 | tf_op jit(solution)/shard_map/all_to_all | solution.py:272
  200.4 1.8 copy.41
  202.2 1.8 copy.42
  (54 shorter events, 10.3 us)
Async XLA Ops:
  0.6 17.1 %copy-start.1 = (bf16[3,3,192,192]{3,2,1,0:T(8,128)(2,1)S(1)}, bf16[3,3,192,192]{3,2,1,0:T(8,128)(2,1)}, u32[]{:S(2)}) copy-start(bf16[3,3,192,192]{3,2,1,0:T(8,128)(2,1)} %param.12) | copy-start | bytes 1990660
  1.7 6.6 %collective-permute-start.1 = (bf16[2,128,64]{1,0,2:T(2,128)(2,1)S(1)}, bf16[2,128,64]{1,0,2:T(2,128)(2,1)S(1)}, u32[]{:S(2)}, u32[]{:S(2)}) collective-permute-start(bf16[2,128,64]{1,0,2:T(2,128)(2,1)S(1)} %get-tuple-element.49), channel_id=1, source_target_pairs={{16,0},{32,16},{48,32},{64,48},{80,64},{96,80},{112,96},{17,1},{33... | collective-permute-start | bytes 98312 | tf_op jit(solution)/shard_map/ppermute | solution.py:267
  5.1 4.2 %collective-permute-start = (bf16[2,128,64]{1,0,2:T(2,128)(2,1)S(1)}, bf16[2,128,64]{1,0,2:T(2,128)(2,1)S(1)}, u32[]{:S(2)}, u32[]{:S(2)}) collective-permute-start(bf16[2,128,64]{1,0,2:T(2,128)(2,1)S(1)} %get-tuple-element.48), channel_id=1, source_target_pairs={{0,16},{16,32},{32,48},{48,64},{64,80},{80,96},{96,112},{1,17},{17... | collective-permute-start | bytes 98312 | tf_op jit(solution)/shard_map/ppermute | solution.py:266
  8.3 10.6 %copy-start = (bf16[3,3,192,192]{3,2,1,0:T(8,128)(2,1)S(1)}, bf16[3,3,192,192]{3,2,1,0:T(8,128)(2,1)}, u32[]{:S(2)}) copy-start(bf16[3,3,192,192]{3,2,1,0:T(8,128)(2,1)} %param.13) | copy-start | bytes 1990660
  10.5 12.5 %collective-permute-start.3 = (bf16[12,2,64]{1,0,2:T(8,128)(2,1)S(1)}, bf16[12,2,64]{1,0,2:T(8,128)(2,1)S(1)}, u32[]{:S(2)}, u32[]{:S(2)}) collective-permute-start(bf16[12,2,64]{1,0,2:T(8,128)(2,1)S(1)} %get-tuple-element.47), channel_id=1, source_target_pairs={{1,0},{2,1},{3,2},{4,3},{5,4},{6,5},{7,6},{8,7},{9,8},{10,9},{11,1... | collective-permute-start | bytes 9224 | tf_op jit(solution)/shard_map/ppermute | solution.py:267
  11.8 11.2 %collective-permute-start.2 = (bf16[12,2,64]{1,0,2:T(8,128)(2,1)S(1)}, bf16[12,2,64]{1,0,2:T(8,128)(2,1)S(1)}, u32[]{:S(2)}, u32[]{:S(2)}) collective-permute-start(bf16[12,2,64]{1,0,2:T(8,128)(2,1)S(1)} %get-tuple-element.46), channel_id=1, source_target_pairs={{0,1},{1,2},{2,3},{3,4},{4,5},{5,6},{6,7},{7,8},{8,9},{9,10},{10,1... | collective-permute-start | bytes 9224 | tf_op jit(solution)/shard_map/ppermute | solution.py:266
  17.7 2.4 %copy-start.9 = (bf16[192,6]{0,1:T(8,128)(2,1)S(1)}, bf16[192,6]{0,1:T(8,128)(2,1)}, u32[]{:S(2)}) copy-start(bf16[192,6]{0,1:T(8,128)(2,1)} %param.14) | copy-start | bytes 6916
  17.7 3.0 %copy-start.4 = (s32[1,4,16384]{2,1,0:T(4,128)S(1)}, s32[1,4,16384]{2,1,0:T(4,128)}, u32[]{:S(2)}) copy-start(s32[1,4,16384]{2,1,0:T(4,128)} %param.15) | copy-start | bytes 786436
  18.9 2.6 %copy-start.5 = (f32[1,4,16384]{2,1,0:T(4,128)S(1)}, f32[1,4,16384]{2,1,0:T(4,128)}, u32[]{:S(2)}) copy-start(f32[1,4,16384]{2,1,0:T(4,128)} %param.16) | copy-start | bytes 786436
  18.9 3.3 %copy-start.10 = (s32[1,128]{1,0:T(1,128)S(1)}, s32[1,128]{1,0:T(1,128)}, u32[]{:S(2)}) copy-start(s32[1,128]{1,0:T(1,128)} %param.17) | copy-start | bytes 1540
  18.9 4.0 %copy-start.2 = (bf16[64,8,128]{2,1,0:T(8,128)(2,1)S(1)}, bf16[64,8,128]{2,1,0:T(8,128)(2,1)}, u32[]{:S(2)}) copy-start(bf16[64,8,128]{2,1,0:T(8,128)(2,1)} %param.10) | copy-start | bytes 393220
  20.1 4.8 %copy-start.8 = (bf16[8,256]{1,0:T(8,128)(2,1)}, bf16[8,256]{1,0:T(8,128)(2,1)S(1)}, u32[]{:S(2)}) copy-start(bf16[8,256]{1,0:T(8,128)(2,1)S(1)} %pad.37.wo) | copy-start | bytes 12292
  106.1 5.6 %collective-permute-start.5 = (f32[2,8,128]{2,1,0:T(8,128)S(1)}, f32[2,8,128]{2,1,0:T(8,128)S(1)}, u32[]{:S(2)}, u32[]{:S(2)}) collective-permute-start(f32[2,8,128]{2,1,0:T(8,128)S(1)} %get-tuple-element.53), channel_id=1, source_target_pairs={{16,0},{32,16},{48,32},{64,48},{80,64},{96,80},{112,96},{17,1},{33... | collective-permute-start | bytes 24584 | tf_op jit(solution)/shard_map/ppermute | solution.py:267
  108.5 3.9 %collective-permute-start.4 = (f32[2,8,128]{2,1,0:T(8,128)S(1)}, f32[2,8,128]{2,1,0:T(8,128)S(1)}, u32[]{:S(2)}, u32[]{:S(2)}) collective-permute-start(f32[2,8,128]{2,1,0:T(8,128)S(1)} %get-tuple-element.52), channel_id=1, source_target_pairs={{0,16},{16,32},{32,48},{48,64},{64,80},{80,96},{96,112},{1,17},{17... | collective-permute-start | bytes 24584 | tf_op jit(solution)/shard_map/ppermute | solution.py:266
  113.3 9.4 %collective-permute-start.7 = (f32[12,8,2]{2,1,0:T(8,128)S(1)}, f32[12,8,2]{2,1,0:T(8,128)S(1)}, u32[]{:S(2)}, u32[]{:S(2)}) collective-permute-start(f32[12,8,2]{2,1,0:T(8,128)S(1)} %get-tuple-element.51), channel_id=1, source_target_pairs={{1,0},{2,1},{3,2},{4,3},{5,4},{6,5},{7,6},{8,7},{9,8},{10,9},{11,1... | collective-permute-start | bytes 2312 | tf_op jit(solution)/shard_map/ppermute | solution.py:267
  114.6 8.1 %collective-permute-start.6 = (f32[12,8,2]{2,1,0:T(8,128)S(1)}, f32[12,8,2]{2,1,0:T(8,128)S(1)}, u32[]{:S(2)}, u32[]{:S(2)}) collective-permute-start(f32[12,8,2]{2,1,0:T(8,128)S(1)} %get-tuple-element.50), channel_id=1, source_target_pairs={{0,1},{1,2},{2,3},{3,4},{4,5},{5,6},{6,7},{7,8},{8,9},{9,10},{10,1... | collective-permute-start | bytes 2312 | tf_op jit(solution)/shard_map/ppermute | solution.py:266
  120.8 2.0 copy-start.3
  202.2 1.8 copy-start.6
  202.2 1.8 copy-start.7
where the time goes:
time: 206 us; the launch traced here: 205 us
  blocking collectives  102 us (50%)
  Pallas kernels  51.1 us (25%)
  starting transfers between devices  22.8 us (11%)
  local copies, waits for them, and re-layouts  21.3 us (10%)
  other arithmetic  5.15 us (2%)
    all_to_all x4, blocking collectives, exchange(): return lax.all_to_all(rows, AXES, split_axis=0, concat_axis=0, tiled=True)  102 us
    pallas_call x4, Pallas kernels, call(): pl.pallas_call(kernel, out_shape=[jax.ShapeDtypeStruct(s, d) for s, d in...  51.1 us
    ppermute x4, starting transfers between devices, neighbours(): before = lax.ppermute(last, axis, up)  14.5 us
    ppermute x4, starting transfers between devices, neighbours(): after = lax.ppermute(first, axis, down)  8.29 us
    unnamed x30, local copies, waits for them, and re-layouts  7.39 us
    pad x4, local copies, waits for them, and re-layouts, stacked(): padded = jnp.pad(kernel, ((0, 0), (0, 0), (0, CP - 192), (0, CP - 192)))  4.82 us
  transfers between devices with their start and end apart: 8, of which 2 were waited for; matrix products, arithmetic and copies ran while one was open for 5% of the time, Pallas kernels for 0%

commit v1 on v0

v1 whole, which is shorter than its diff:
```python
import jax
import jax.numpy as jnp
from jax import lax
from jax.experimental import pallas as pl
from jax.experimental.pallas import tpu as pltpu
from jax.sharding import PartitionSpec as P

BF = jnp.bfloat16
F32 = jnp.float32
I32 = jnp.int32
CAP = 128
TH, TW = 8, 128
C = 192
ROW = 144
N12, N10, N8 = 12 * ROW, 10 * ROW, 8 * ROW
CP = 256
AXES = ("ns", "ew")
PIECE = 48
HALF = 64 * PIECE
REST = 1728
EXTRA = 2592
NT = (((1,), (1,)), ((), ()))
TN = (((0,), (0,)), ((), ()))


def dot(x, y, dims=(((1,), (0,)), ((), ()))):
    return lax.dot_general(x, y, dims, preferred_element_type=F32)


def taps(cat, weight, first, count, order):
    total = None
    for a in range(3):
        start = (a if order > 0 else 2 - a) * ROW + first
        rows = cat[start : start + count, :]
        term = dot(rows, weight[a]) if order > 0 else dot(rows, weight[a], NT)
        total = term if total is None else total + term
    return total


def stack_weights(out, kernel, order):
    out[...] = jnp.zeros_like(out)
    for a in range(3):
        for b in range(3):
            if order > 0:
                out[a, b * CP : b * CP + C, 0:C] = kernel[a, b]
            else:
                out[a, 0:C, b * CP : b * CP + C] = kernel[a, b]


def pick(table, row, index):
    return jnp.take_along_axis(
        jnp.broadcast_to(table[row : row + 1, :], (8, 128)),
        index,
        axis=1,
        mode="promise_in_bounds",
    )


def pack_pair(x, y):
    return x * 65536 + (y + 32768)


def unpack_pair(word):
    return (word >> 16).astype(F32), ((word & 65535) - 32768).astype(F32)


def forward_kernel(
    flags, ft, small, c1, c2, cells, wts, cnt, out, a1_out, gp, h2b, hs, xcat, as_, acat, w1, w2,
    fq, pf,
):
    zero8 = jnp.zeros((8, CP), F32)
    hs[0:8, :] = zero8
    hs[N12 + 8 : N12 + 16, :] = zero8
    as_[0:8, :] = zero8
    as_[N10 + 8 : N10 + 16, :] = zero8
    stack_weights(w1, c1, 1)
    stack_weights(w2, c2, 1)
    hs[8 : N12 + 8, :] = dot(ft[...], small[0:64, :])
    for b in range(3):
        xcat[:, b * CP : (b + 1) * CP] = hs[7 + b : 7 + b + N12, :].astype(BF)
    col = lax.broadcasted_iota(I32, (ROW, CP), 0)
    col_mask = jnp.where(col == 1, flags[2], jnp.where(col == 130, flags[3], 1.0))
    root = 0.7978845608028654
    for part in range(5):
        z2 = taps(xcat, w1, part * 2 * ROW, 2 * ROW, 1)
        for q in range(2):
            r = part * 2 + q
            z = z2[q * ROW : (q + 1) * ROW]
            mask = col_mask
            if r == 0:
                mask = col_mask * flags[0]
            if r == 9:
                mask = col_mask * flags[1]
            zz = z * z
            t = jnp.tanh(root * z * (1.0 + 0.044715 * zz))
            half = 0.5 * (1.0 + t)
            slope = half + 0.5 * z * (1.0 - t * t) * (root * (1.0 + 3 * 0.044715 * zz))
            a1 = z * half * mask
            as_[8 + r * ROW : 8 + (r + 1) * ROW, :] = a1
            a1_out[r * ROW : (r + 1) * ROW, :] = a1.astype(BF)
            gp[r * ROW : (r + 1) * ROW, :] = (slope * mask).astype(BF)
    for b in range(3):
        acat[:, b * CP : (b + 1) * CP] = as_[7 + b : 7 + b + N10, :].astype(BF)
    for part in range(4):
        at = part * 2 * ROW
        h2 = hs[8 + 2 * ROW + at : 8 + 4 * ROW + at, :] + taps(acat, w2, at, 2 * ROW, 1)
        h2b[at : at + 2 * ROW, :] = h2.astype(BF)
    field = dot(small[64:80, :], h2b[...], NT)
    tiles = [field[0:8, r * ROW + 2 : r * ROW + 2 + TW] for r in range(8)]
    top = tiles[0]
    for r in range(1, 8):
        top = jnp.maximum(jnp.abs(top), jnp.abs(tiles[r]))
    largest = jnp.maximum(jnp.max(jnp.abs(top)), 1e-30)
    up = 32000.0 / largest
    down = largest * (1.0 / 32000.0)
    for r in range(8):
        whole = jnp.round(tiles[r] * up).astype(I32)
        fq[r * 8 : r * 8 + 3, :] = pack_pair(whole[0:3], whole[3:6])
    pf[...] = jnp.zeros_like(pf)
    lane = lax.broadcasted_iota(I32, (8, 128), 1)

    def owners(ob, carry):
        rows = pl.ds(pl.multiple_of(ob * 8, 8), 8)
        live = lane < cnt[rows, 0:1]
        sums = [jnp.zeros((8, 128), F32)] * 6
        for k in range(4):
            index = cells[k, rows, :]
            low, high = index & 127, index >> 7
            weight = jnp.where(live, wts[k, rows, :] * down, 0.0)
            got = [jnp.zeros((8, 128), I32)] * 3
            for r in range(8):
                here = high == r
                got = [jnp.where(here, pick(fq, r * 8 + v, low), got[v]) for v in range(3)]
            for v in range(3):
                x, y = unpack_pair(got[v])
                sums[v] = sums[v] + weight * x
                sums[v + 3] = sums[v + 3] + weight * y
        for v in range(6):
            pf[pl.ds(ob * 64 + v, 8, stride=8), :] = sums[v]
        return carry

    lax.fori_loop(0, 16, owners, 0)
    out[...] = pf[...].astype(BF)


def turn_kernel(a1, ft, small, a1t, h0t, wide, thin, pa, pt):
    wide[...] = a1[...].astype(F32)
    thin[...] = ft[...].astype(F32)
    ones = lax.broadcasted_iota(I32, (CP, CP), 0) == lax.broadcasted_iota(I32, (CP, CP), 1)
    same = jnp.where(ones, 1.0, 0.0).astype(BF)
    win_t = dot(same[0:C, :], small[0:64, :], NT).astype(BF)
    for b in range(3):
        for r in range(10):
            at = slice(r * 128, r * 128 + 128)
            pa[at, :] = wide[r * ROW + 1 + b : r * ROW + 129 + b, :].astype(BF)
            pt[at, :] = thin[(r + 1) * ROW + 1 + b : (r + 1) * ROW + 129 + b, :].astype(BF)
        a1t[b * C : (b + 1) * C, :] = dot(same[0:C, :], pa[...], NT).astype(BF)
        h0t[b * C : (b + 1) * C, :] = dot(win_t, pt[...], NT).astype(BF)


def spread_row(row):
    return jnp.broadcast_to(row, (16, 128)).astype(BF)


def iotas(count):
    base = lax.broadcasted_iota(I32, (16, 128), 0)
    return [(base + 16 * m).astype(F32).astype(BF) for m in range(count)]


def owner_kernel(recv, obs, target, pred, loss, out, left, right, total, rq, gf):
    steps = iotas(8)
    none = jnp.zeros((16, 128), BF)
    one = jnp.ones((16, 128), BF)

    def collect(tb, carry):
        block = recv[pl.ds(pl.multiple_of(tb * 64, 64), 64), :].astype(F32)
        index = obs[pl.ds(pl.multiple_of(tb * 8, 8), 8), :]
        low = (index & 127).astype(F32)
        high = (index >> 7).astype(F32)
        for i in range(8):
            at = pl.ds(pl.multiple_of(tb * 1024 + i * 128, 128), 128)
            here = spread_row(high[i : i + 1]) == steps[0]
            for v in range(6):
                value = spread_row(block[i * 8 + v : i * 8 + v + 1])
                left[v * 16 : v * 16 + 16, at] = jnp.where(here, value, none)
            mine = spread_row(low[i : i + 1])
            for m in range(8):
                right[m * 16 : m * 16 + 16, at] = jnp.where(mine == steps[m], one, none)
        return carry

    lax.fori_loop(0, 16, collect, 0)
    total[...] = dot(left[...], right[...], NT)
    scale = 1.0 / (6 * 2048)
    squares = jnp.zeros((6, 128), F32)
    resids = []
    for h in range(16):
        at = slice(h * 128, h * 128 + 128)
        mine = total[pl.ds(h, 6, stride=16), :]
        pred[:, at] = mine
        resid = mine - target[:, at]
        squares = squares + resid * resid
        resids.append(resid * scale)
    loss[...] = jnp.full((16, 128), jnp.sum(squares) * (0.5 * scale), F32)
    top = jnp.abs(resids[0])
    for h in range(1, 16):
        top = jnp.maximum(top, jnp.abs(resids[h]))
    largest = jnp.maximum(jnp.max(top), 1e-30)
    up = 32000.0 / largest
    down = largest * (1.0 / 32000.0)
    for h in range(16):
        whole = jnp.round(resids[h] * up).astype(I32)
        rq[h * 8 : h * 8 + 3, :] = pack_pair(whole[0:3], whole[3:6])
    gf[...] = jnp.zeros_like(gf)

    def choose(tb, carry):
        index = obs[pl.ds(pl.multiple_of(tb * 8, 8), 8), :]
        low, high = index & 127, index >> 7
        got = [jnp.zeros((8, 128), I32)] * 3
        for h in range(16):
            here = high == h
            got = [jnp.where(here, pick(rq, h * 8 + v, low), got[v]) for v in range(3)]
        for v in range(3):
            x, y = unpack_pair(got[v])
            gf[pl.ds(tb * 64 + v, 8, stride=8), :] = x * down
            gf[pl.ds(tb * 64 + v + 3, 8, stride=8), :] = y * down
        return carry

    lax.fori_loop(0, 16, choose, 0)
    out[...] = gf[...].astype(BF)


def spread_kernel(grad, cells, wts, cnt, out, left, right, total):
    steps = iotas(4)
    none = jnp.zeros((16, 128), BF)
    total[...] = jnp.zeros_like(total)
    lane = lax.broadcasted_iota(I32, (8, 128), 1)

    def owners(ob, carry):
        rows = pl.ds(pl.multiple_of(ob * 8, 8), 8)
        live = lane < cnt[rows, 0:1]
        block = grad[pl.ds(pl.multiple_of(ob * 64, 64), 64), :].astype(F32)
        index = [cells[k, rows, :] for k in range(4)]
        low = [(i & 63).astype(F32) for i in index]
        high = [(i >> 6).astype(F32) for i in index]
        weight = [jnp.where(live, wts[k, rows, :], 0.0) for k in range(4)]
        for i in range(8):
            values = [spread_row(block[i * 8 + v : i * 8 + v + 1]) for v in range(6)]
            for k in range(4):
                at = slice((i * 4 + k) * 128, (i * 4 + k) * 128 + 128)
                here = spread_row(high[k][i : i + 1]) == steps[0]
                for v in range(6):
                    left[v * 16 : v * 16 + 16, at] = jnp.where(here, values[v], none)
                mine = spread_row(low[k][i : i + 1])
                amount = spread_row(weight[k][i : i + 1])
                for m in range(4):
                    right[m * 16 : m * 16 + 16, at] = jnp.where(mine == steps[m], amount, none)
        total[...] += dot(left[...], right[...], NT)
        return carry

    lax.fori_loop(0, 16, owners, 0)
    out[...] = jnp.zeros_like(out)
    for r in range(8):
        even = total[pl.ds(2 * r, 6, stride=16), :]
        odd = total[pl.ds(2 * r + 1, 6, stride=16), :]
        out[r * 8 : r * 8 + 6, :] = jnp.concatenate([even, odd], 1)


def backward_kernel(
    core, gfn, ft, a1t, h0t, gp, h2b, c2, c1, small, loss, pay, gfields, gs, g2cat, zs, gzcat, own,
    w2, w1, gc,
):
    zero8 = jnp.zeros((8, CP), F32)
    gs[0:8, :] = zero8
    gs[N12 + 8 : N12 + 16, :] = zero8
    zs[0:8, :] = zero8
    zs[N10 + 8 : N10 + 16, :] = zero8
    stack_weights(w2, c2, -1)
    stack_weights(w1, c1, -1)
    wo = small[64:72, :]
    base_s = pl.multiple_of(core[0] * HALF, 16)
    base_f = pl.multiple_of((1 - core[0]) * HALF, 16)

    def put(base, at, value):
        pay[pl.ds(pl.multiple_of(base + at, 16), value.shape[0]), :] = value.astype(BF)

    def put_taps(base, turned):
        for a in range(3):
            y = dot(turned[:, a * 128 : a * 128 + 1024], gc[...])
            for b in range(3):
                tap = a * 3 + b
                mine = y[b * C : (b + 1) * C]
                put(base, tap * C, mine[:, 0:128])
                rest = mine[:, 128:256]
                put(base, REST + tap * 96, rest[0:96] + pltpu.roll(rest[96:192], 64, 1))

    x = gfn[...]
    x_hi = x.astype(BF)
    x_lo = (x - x_hi.astype(F32)).astype(BF)
    gs[8 : N12 + 8, :] = dot(x_hi, wo) + dot(x_lo, wo)
    for b in range(3):
        g2cat[:, b * CP : (b + 1) * CP] = gs[9 - b : 9 - b + N12, :].astype(BF)
    for r in range(8):
        at = 8 + (r + 2) * ROW + 2
        gc[r * 128 : r * 128 + 128, :] = gs[at : at + 128, :].astype(BF)
    put_taps(base_s, a1t)
    for part in range(5):
        at = part * 2 * ROW
        g = taps(g2cat, w2, at, 2 * ROW, -1)
        zs[8 + at : 8 + at + 2 * ROW, :] = g * gp[at : at + 2 * ROW, :].astype(F32)
    for b in range(3):
        gzcat[:, b * CP : (b + 1) * CP] = zs[9 - b : 9 - b + N10, :].astype(BF)
    for r in range(8):
        at = 8 + (r + 1) * ROW + 2
        gc[r * 128 : r * 128 + 128, :] = zs[at : at + 128, :].astype(BF)
    put_taps(base_f, h0t)
    col = lax.broadcasted_iota(I32, (ROW, CP), 0)
    keep = jnp.where((col >= 2) & (col < 2 + TW), 1.0, 0.0)
    keep2 = jnp.concatenate([keep, keep], 0)
    for part in range(4):
        at = part * 2 * ROW
        g = gs[8 + 2 * ROW + at : 8 + 4 * ROW + at, :] + taps(gzcat, w1, at, 2 * ROW, -1)
        own[at : at + 2 * ROW, :] = (g * keep2).astype(BF)
    g_in = dot(ft[2 * ROW : 10 * ROW, :], own[...], TN)
    g_fields = dot(small[0:64, :], own[...], NT)
    for r in range(8):
        gfields[pl.ds(r, 64, stride=8), :] = g_fields[:, r * ROW + 2 : r * ROW + 2 + TW]
    x_own = x[2 * ROW : 10 * ROW] * jnp.concatenate([keep[:, 0:8]] * 8, 0)
    o_hi = x_own.astype(BF)
    o_lo = (x_own - o_hi.astype(F32)).astype(BF)
    g_out = dot(o_hi, h2b[...], TN) + dot(o_lo, h2b[...], TN)
    put(base_s, EXTRA, g_in[:, 0:128])
    rest = g_in[:, 128:256]
    put(base_s, EXTRA + 64, rest[0:32] + pltpu.roll(rest[32:64], 64, 1))
    put(base_s, EXTRA + 96, jnp.zeros((HALF - EXTRA - 96, 128), F32))
    put(base_f, EXTRA, jnp.concatenate([g_out[:, 0:128], g_out[:, 128:256]], 0))
    put(base_f, EXTRA + 16, loss[...])
    put(base_f, EXTRA + 32, jnp.zeros((HALF - EXTRA - 32, 128), F32))


def unpack_kernel(core, mine, other, second, first, g_in, g_out, loss):
    def unpack(source, kernel):
        for tap in range(9):
            a, b = tap // 3, tap % 3
            kernel[a, b, :, 0:128] = source[tap * C : (tap + 1) * C, :].astype(F32)
            rest = source[REST + tap * 96 : REST + tap * 96 + 96, :].astype(F32)
            kernel[a, b, 0:96, 128:C] = rest[:, 0:64]
            kernel[a, b, 96:C, 128:C] = pltpu.roll(rest, 64, 1)[:, 0:64]

    def both(s, f):
        unpack(s, second)
        unpack(f, first)
        g_in[:, 0:128] = s[EXTRA : EXTRA + 64, :].astype(F32)
        rest = s[EXTRA + 64 : EXTRA + 96, :].astype(F32)
        g_in[0:32, 128:C] = rest[:, 0:64]
        g_in[32:64, 128:C] = pltpu.roll(rest, 64, 1)[:, 0:64]
        extra = f[EXTRA : EXTRA + 32, :].astype(F32)
        g_out[:, 0:128] = extra[0:8]
        g_out[:, 128:256] = extra[8:16]
        loss[...] = extra[16:24]

    @pl.when(core[0] == 0)
    def _():
        both(mine, other)

    @pl.when(core[0] == 1)
    def _():
        both(other, mine)


def neighbours(array, axis, dim, width):
    count, length = lax.axis_size(axis), array.shape[dim]
    up = [(i, i + 1) for i in range(count - 1)]
    down = [(j, i) for i, j in up]
    last = lax.slice_in_dim(array, length - width, length, axis=dim)
    first = lax.slice_in_dim(array, 0, width, axis=dim)
    before = lax.ppermute(last, axis, up)
    after = lax.ppermute(first, axis, down)
    return jnp.concatenate([before, array, after], axis=dim)


def exchange(rows, groups=None):
    return lax.all_to_all(
        rows, AXES, split_axis=0, concat_axis=0, tiled=True, axis_index_groups=groups
    )


def call(kernel, out_shapes, scratch, *operands, smem=0, vmem=60, flops=0):
    specs = [pl.BlockSpec(memory_space=pltpu.SMEM)] * smem + [
        pl.BlockSpec(memory_space=pltpu.VMEM)
    ] * (len(operands) - smem)
    return pl.pallas_call(
        kernel,
        out_shape=[jax.ShapeDtypeStruct(s, d) for s, d in out_shapes],
        in_specs=specs,
        out_specs=[pl.BlockSpec(memory_space=pltpu.VMEM)] * len(out_shapes),
        scratch_shapes=[pltpu.VMEM(s, d) for s, d in scratch],
        compiler_params=pltpu.CompilerParams(vmem_limit_bytes=vmem * 1024 * 1024),
        cost_estimate=pl.CostEstimate(flops=flops, bytes_accessed=4_000_000, transcendentals=0),
    )(*operands)


def on_device(
    fields,
    w_in,
    conv_first,
    conv_second,
    w_out,
    slot_cells,
    slot_weights,
    slot_count,
    recv_obs,
    targets,
):
    ns, ew = lax.axis_index("ns"), lax.axis_index("ew")
    n_ns, n_ew = lax.axis_size("ns"), lax.axis_size("ew")
    flags = jnp.stack([ns > 0, ns < n_ns - 1, ew > 0, ew < n_ew - 1]).astype(F32)
    core = (ns % 2).astype(I32).reshape(1)
    cells = slot_cells.reshape(4, 128, CAP)
    wts = slot_weights.reshape(4, 128, CAP)
    cnt = slot_count.reshape(128, 1)
    obs = recv_obs.reshape(128, CAP)
    small = jnp.concatenate([w_in, jnp.pad(w_out.T, ((0, 10), (0, 0)))], 0)
    small = jnp.pad(small, ((0, 0), (0, CP - C)))

    grid = fields.transpose(1, 2, 0)
    grid = neighbours(grid, "ns", 0, 2)
    grid = neighbours(grid, "ew", 1, 2)
    ft = jnp.pad(grid, ((0, 0), (0, ROW - TW - 4), (0, 0))).reshape(N12, 64)
    sent, a1, gp, h2b = call(
        forward_kernel,
        [((1024, 128), BF), ((N10, CP), BF), ((N10, CP), BF), ((N8, CP), BF)],
        [
            ((N12 + 16, CP), F32), ((N12, 3 * CP), BF), ((N10 + 16, CP), F32),
            ((N10, 3 * CP), BF), ((3, 3 * CP, CP), BF), ((3, 3 * CP, CP), BF),
            ((64, 128), I32), ((1024, 128), F32),
        ],
        flags, ft, small, conv_first, conv_second, cells, wts, cnt,
        smem=1, vmem=40, flops=2 * 10**9,
    )
    received = exchange(sent)
    a1t, h0t = call(
        turn_kernel,
        [((3 * C, 1280), BF), ((3 * C, 1280), BF)],
        [((N10, CP), F32), ((N12, 64), F32), ((1280, CP), BF), ((1280, 64), BF)],
        a1, ft, small,
        vmem=32, flops=10**9,
    )
    pred, loss, back = call(
        owner_kernel,
        [((6, 2048), F32), ((16, 128), F32), ((1024, 128), BF)],
        [
            ((96, 16384), BF), ((128, 16384), BF), ((96, 128), F32), ((128, 128), I32),
            ((1024, 128), F32),
        ],
        received, obs, targets,
        vmem=32, flops=10**9,
    )
    grads = exchange(back)
    (g_field,) = call(
        spread_kernel,
        [((64, 128), F32)],
        [((96, 4096), BF), ((64, 4096), BF), ((96, 64), F32)],
        grads, cells, wts, cnt,
        vmem=32, flops=10**9,
    )
    g_field = neighbours(g_field.reshape(8, 8, 128), "ns", 0, 2)
    g_field = neighbours(g_field, "ew", 2, 2).transpose(0, 2, 1)
    gfn = jnp.pad(g_field, ((0, 0), (0, ROW - TW - 4), (0, 0))).reshape(N12, 8)
    pay, g_fields = call(
        backward_kernel,
        [((2 * HALF, 128), BF), ((512, 128), F32)],
        [
            ((N12 + 16, CP), F32), ((N12, 3 * CP), BF), ((N10 + 16, CP), F32),
            ((N10, 3 * CP), BF), ((N8, CP), BF), ((3, CP, 3 * CP), BF), ((3, CP, 3 * CP), BF),
            ((1024, CP), BF),
        ],
        core, gfn, ft, a1t, h0t, gp, h2b, conv_second, conv_first, small, loss,
        smem=1, vmem=40, flops=2 * 10**9,
    )
    pairs = [(n, n + 1 - 2 * (n % 2)) for n in range(n_ns)]
    groups = [[n * n_ew + e for n in range(c, n_ns, 2) for e in range(n_ew)] for c in range(2)]
    theirs = lax.ppermute(pay[HALF:], "ns", pairs)
    summed = (pay[:HALF].astype(F32) + theirs.astype(F32)).astype(BF).reshape(64, PIECE, 128)
    share = jnp.sum(exchange(summed, groups).astype(F32), axis=0).astype(BF)
    mine = exchange(jnp.broadcast_to(share[None], (64, PIECE, 128)), groups).reshape(HALF, 128)
    other = lax.ppermute(mine, "ns", pairs)
    grad_second, grad_first, grad_in, g_out, total = call(
        unpack_kernel,
        [((3, 3, C, C), F32), ((3, 3, C, C), F32), ((64, C), F32), ((8, CP), F32), ((8, 128), F32)],
        [],
        core, mine, other,
        smem=1, vmem=32,
    )
    return (
        pred,
        total[0, 0],
        grad_first,
        grad_second,
        grad_in,
        g_out[:6, :C].T,
        g_fields.reshape(64, TH, TW),
    )


def solution(mesh):
    in_specs = (
        P(None, "ns", "ew"),
        P(),
        P(),
        P(),
        P(),
        P(("ns", "ew"), None, None),
        P(("ns", "ew"), None, None),
        P(("ns", "ew"), None),
        P(("ns", "ew"), None),
        P(None, ("ns", "ew")),
    )
    out_specs = (P(None, ("ns", "ew")), P(), P(), P(), P(), P(), P(None, "ns", "ew"))
    return jax.shard_map(
        on_device, mesh=mesh, in_specs=in_specs, out_specs=out_specs, check_vma=False
    )
```

time: 206 us -> 175 us (0.85)
  blocking collectives: 102 us -> 83 us
  Pallas kernels: 51.1 us -> 33.8 us
  waiting for transfers between devices: 1.74 us -> 17.6 us
  local copies, waits for them, and re-layouts: 21.3 us -> 12.1 us
    all_to_all x4, blocking collectives: 102 us -> 83 us  [exchange(): lax.all_to_all(rows, AXES, split_axis=0, concat_axis=0, tiled=True, axis_...]
    pallas_call x4 -> x6, Pallas kernels: 51.1 us -> 33.8 us  [call(): pl.pallas_call(kernel, out_shape=[jax.ShapeDtypeStruct(s, d) for s, d in...]
    ppermute x4, waiting for transfers between devices: 0.01 us -> 10.6 us  [neighbours(): after = lax.ppermute(first, axis, down)]
    pad x7 -> x1, local copies, waits for them, and re-layouts: 6.8 us -> 0.01 us  [on_device(): small = jnp.pad(small, ((0, 0), (0, CP - C)))]
    ppermute x0 -> x2, waiting for transfers between devices: none -> 4.18 us  [the longest x1 2.27 us: on_device(): theirs = lax.ppermute(pay[HALF:], 'ns', pairs)]
    ppermute x0 -> x2, starting transfers between devices: none -> 2.95 us  [the longest x1 2.87 us: on_device(): other = lax.ppermute(mine, 'ns', pairs)]
    unnamed x30 -> x36, local copies, waits for them, and re-layouts: 7.39 us -> 7.02 us
  transfers between devices with their start and end apart: 8 -> 10, of which waited for: 2 -> 7; matrix products, arithmetic and copies ran while one was open for 5% -> 1% of each run, Pallas kernels for 0% -> 1%
where the time goes in v1:
time: 175 us; the launch traced here: 174 us
  blocking collectives  83 us (47%)
  Pallas kernels  33.8 us (19%)
  starting transfers between devices  22.1 us (13%)
  waiting for transfers between devices  17.6 us (10%)
  local copies, waits for them, and re-layouts  12.1 us (7%)
  other arithmetic  4.62 us (3%)
    all_to_all x4, blocking collectives, exchange(): lax.all_to_all(rows, AXES, split_axis=0, concat_axis=0, tiled=True, axis_...  83 us
    pallas_call x6, Pallas kernels, call(): pl.pallas_call(kernel, out_shape=[jax.ShapeDtypeStruct(s, d) for s, d in...  33.8 us
    ppermute x4, starting transfers between devices, neighbours(): before = lax.ppermute(last, axis, up)  12.6 us
    ppermute x4, waiting for transfers between devices, neighbours(): after = lax.ppermute(first, axis, down)  10.6 us
    unnamed x36, local copies, waits for them, and re-layouts  7.02 us
    ppermute x4, starting transfers between devices, neighbours(): after = lax.ppermute(first, axis, down)  6.61 us
  transfers between devices with their start and end apart: 10, of which 7 were waited for; matrix products, arithmetic and copies ran while one was open for 1% of the time, Pallas kernels for 1%

profile of v1, /device:TPU:1, one launch (start us, length us, event | category | flops | bytes accessed | tf_op | source)
XLA Modules:
  0.0 174.3 jit_solution(12434532585942068918)
XLA Ops:
  1.8 4.6 %collective-permute-start = (bf16[2,128,64]{1,0,2:T(2,128)(2,1)S(1)}, bf16[2,128,64]{1,0,2:T(2,128)(2,1)S(1)}, u32[]{:S(2)}, u32[]{:S(2)}) collective-permute-start(bf16[2,128,64]{1,0,2:T(2,128)(2,1)S(1)} %get-tuple-element.41), channel_id=1, source_target_pairs={{0,16},{16,32},{32,48},{48,64},{64,80},{80,96},{96,112},{1,17},{17... | collective-permute-start | bytes 98312 | tf_op jit(solution)/shard_map/ppermute | solution.py:376
  6.4 1.9 %collective-permute-start.1 = (bf16[2,128,64]{1,0,2:T(2,128)(2,1)S(1)}, bf16[2,128,64]{1,0,2:T(2,128)(2,1)S(1)}, u32[]{:S(2)}, u32[]{:S(2)}) collective-permute-start(bf16[2,128,64]{1,0,2:T(2,128)(2,1)S(1)} %get-tuple-element.42), channel_id=1, source_target_pairs={{16,0},{32,16},{48,32},{64,48},{80,64},{96,80},{112,96},{17,1},{33... | collective-permute-start | bytes 98312 | tf_op jit(solution)/shard_map/ppermute | solution.py:377
  9.1 2.5 %collective-permute-done.1 = bf16[2,128,64]{1,0,2:T(2,128)(2,1)S(1)} collective-permute-done((bf16[2,128,64]{1,0,2:T(2,128)(2,1)S(1)}, bf16[2,128,64]{1,0,2:T(2,128)(2,1)S(1)}, u32[]{:S(2)}, u32[]{:S(2)}) %collective-permute-start.1) | collective-permute-done | bytes 32800 | tf_op jit(solution)/shard_map/ppermute | solution.py:377
  12.8 3.1 %collective-permute-start.2 = (bf16[12,2,64]{1,0,2:T(8,128)(2,1)S(1)}, bf16[12,2,64]{1,0,2:T(8,128)(2,1)S(1)}, u32[]{:S(2)}, u32[]{:S(2)}) collective-permute-start(bf16[12,2,64]{1,0,2:T(8,128)(2,1)S(1)} %get-tuple-element.39), channel_id=1, source_target_pairs={{0,1},{1,2},{2,3},{3,4},{4,5},{5,6},{6,7},{7,8},{8,9},{9,10},{10,1... | collective-permute-start | bytes 9224 | tf_op jit(solution)/shard_map/ppermute | solution.py:376
  15.9 1.3 collective-permute-start.3
  17.5 2.8 %collective-permute-done.2 = bf16[12,2,64]{1,0,2:T(8,128)(2,1)S(1)} collective-permute-done((bf16[12,2,64]{1,0,2:T(8,128)(2,1)S(1)}, bf16[12,2,64]{1,0,2:T(8,128)(2,1)S(1)}, u32[]{:S(2)}, u32[]{:S(2)}) %collective-permute-start.2) | collective-permute-done | bytes 3104 | tf_op jit(solution)/shard_map/ppermute | solution.py:376
  20.4 4.2 %collective-permute-done.3 = bf16[12,2,64]{1,0,2:T(8,128)(2,1)} collective-permute-done((bf16[12,2,64]{1,0,2:T(8,128)(2,1)S(1)}, bf16[12,2,64]{1,0,2:T(8,128)(2,1)}, u32[]{:S(2)}, u32[]{:S(2)}) %collective-permute-start.3) | collective-permute-done | bytes 3104 | tf_op jit(solution)/shard_map/ppermute | solution.py:377
  24.6 1.6 pad_maximum_fusion
  26.2 1.2 copy.27
  27.4 1.1 pad.16.clone
  28.5 8.3 %shard_map.153 = (bf16[1024,128]{1,0:T(8,128)(2,1)S(1)}, bf16[1440,256]{1,0:T(8,128)(2,1)S(1)}, bf16[1440,256]{1,0:T(8,128)(2,1)S(1)}, bf16[1152,256]{1,0:T(8,128)(2,1)S(1)}) custom-call(f32[4]{0:T(128)S(1)} %add_convert_fusion.1.flags, bf16[1728,64]{1,0:T(8,128)(2,1)S(1)} %bitcast.41, bf16[80,256]{1,0:T(8,128)(2,1)S(1)} %pad.18.small, ...), custom_call_target="tpu_custom_call" | custom-call | flops 2000000000 | bytes 4000000 | tf_op jit(solution)/shard_map/pallas_call | solution.py:391
  36.9 24.5 %all_to_all.32 = bf16[128,8,128]{2,1,0:T(8,128)(2,1)S(1)} all-to-all(bf16[128,8,128]{2,1,0:T(8,128)(2,1)S(1)} %bitcast.48), channel_id=1, replica_groups=mesh['ns'=8,'ew'=16] {'ns','ew'}, dimensions={0} | all-to-all | bytes 524288 | tf_op jit(solution)/shard_map/all_to_all | solution.py:382
  61.3 6.2 %shard_map.154 = (f32[6,2048]{1,0:T(8,128)}, f32[16,128]{1,0:T(8,128)S(1)}, bf16[1024,128]{1,0:T(8,128)(2,1)S(1)}) custom-call(bf16[1024,128]{1,0:T(8,128)(2,1)S(1)} %bitcast.49, s32[128,128]{1,0:T(8,128)S(1)} %bitcast.54, f32[6,2048]{1,0:T(8,128)S(1)} %copy-done.9), custom_call_target="tpu_custom_call" | custom-call | flops 1000000000 | bytes 4000000 | tf_op jit(solution)/shard_map/pallas_call | solution.py:391
  67.6 15.3 %all_to_all.33 = bf16[128,8,128]{2,1,0:T(8,128)(2,1)S(1)} all-to-all(bf16[128,8,128]{2,1,0:T(8,128)(2,1)S(1)} %bitcast.50), channel_id=1, replica_groups=mesh['ns'=8,'ew'=16] {'ns','ew'}, dimensions={0} | all-to-all | bytes 524288 | tf_op jit(solution)/shard_map/all_to_all | solution.py:382
  82.9 8.3 %shard_map.155 = f32[64,128]{1,0:T(8,128)S(1)} custom-call(bf16[1024,128]{1,0:T(8,128)(2,1)S(1)} %bitcast.51, s32[4,128,128]{2,1,0:T(8,128)S(1)} %bitcast.45, f32[4,128,128]{2,1,0:T(8,128)S(1)} %bitcast.47, s32[128,1]{1,0:T(8,128)S(1)} %copy.24.cnt), custom_call_target="tpu_custom_call" | custom-call | flops 1000000000 | bytes 4000000 | tf_op jit(solution)/shard_map/pallas_call | solution.py:391
  91.2 2.6 %collective-permute-start.4 = (f32[2,8,128]{2,1,0:T(8,128)S(1)}, f32[2,8,128]{2,1,0:T(8,128)S(1)}, u32[]{:S(2)}, u32[]{:S(2)}) collective-permute-start(f32[2,8,128]{2,1,0:T(8,128)S(1)} %get-tuple-element.45), channel_id=1, source_target_pairs={{0,16},{16,32},{32,48},{48,64},{64,80},{80,96},{96,112},{1,17},{17... | collective-permute-start | bytes 24584 | tf_op jit(solution)/shard_map/ppermute | solution.py:376
  93.8 1.9 %collective-permute-start.5 = (f32[2,8,128]{2,1,0:T(8,128)S(1)}, f32[2,8,128]{2,1,0:T(8,128)S(1)}, u32[]{:S(2)}, u32[]{:S(2)}) collective-permute-start(f32[2,8,128]{2,1,0:T(8,128)S(1)} %get-tuple-element.46), channel_id=1, source_target_pairs={{16,0},{32,16},{48,32},{64,48},{80,64},{96,80},{112,96},{17,1},{33... | collective-permute-start | bytes 24584 | tf_op jit(solution)/shard_map/ppermute | solution.py:377
  95.7 3.0 %collective-permute-done.5 = f32[2,8,128]{2,1,0:T(8,128)S(1)} collective-permute-done((f32[2,8,128]{2,1,0:T(8,128)S(1)}, f32[2,8,128]{2,1,0:T(8,128)S(1)}, u32[]{:S(2)}, u32[]{:S(2)}) %collective-permute-start.5) | collective-permute-done | bytes 8224 | tf_op jit(solution)/shard_map/ppermute | solution.py:377
  98.9 2.2 %collective-permute-start.6 = (f32[12,8,2]{2,1,0:T(8,128)S(1)}, f32[12,8,2]{2,1,0:T(8,128)S(1)}, u32[]{:S(2)}, u32[]{:S(2)}) collective-permute-start(f32[12,8,2]{2,1,0:T(8,128)S(1)} %get-tuple-element.43), channel_id=1, source_target_pairs={{0,1},{1,2},{2,3},{3,4},{4,5},{5,6},{6,7},{7,8},{8,9},{9,10},{10,1... | collective-permute-start | bytes 2312 | tf_op jit(solution)/shard_map/ppermute | solution.py:376
  101.1 1.5 collective-permute-start.7
  102.6 1.1 copy-done.11
  103.7 1.4 shard_map.156
  106.7 2.1 %copy.28 = f32[12,132,8]{2,1,0:T(8,128)} copy(f32[12,132,8]{1,2,0:T(8,128)} %maximum_bitcast_fusion) | data formatting | bytes 101376
  108.8 1.3 pad.19.clone
  110.4 1.2 copy-done.3
  112.6 7.5 %shard_map.157 = (bf16[6144,128]{1,0:T(8,128)(2,1)S(1)}, f32[512,128]{1,0:T(8,128)}) custom-call(s32[1]{0:T(128)} %bitcast.11.core, f32[1728,8]{1,0:T(8,128)S(1)} %bitcast.38, bf16[1728,64]{1,0:T(8,128)(2,1)S(1)} %bitcast.43, bf16[576,1280]{1,0:T(8,128)(2,1)S(1)} %get-tuple-element.27.a1t, bf16[576,1280]{1,0:T(8,128)(2,1)S(1)} %get-tuple-element.28.h0t, ...), custom_call_target="tpu_custom_call" | custom-call | flops 2000000000 | bytes 4000000 | tf_op jit(solution)/shard_map/pallas_call | solution.py:391
  120.3 2.3 %collective-permute-done.8 = bf16[3072,128]{1,0:T(8,128)(2,1)S(1)} collective-permute-done((bf16[3072,128]{1,0:T(8,128)(2,1)S(1)}, bf16[3072,128]{1,0:T(8,128)(2,1)S(1)}, u32[]{:S(2)}, u32[]{:S(2)}) %collective-permute-start.8) | collective-permute-done | bytes 786464 | tf_op jit(solution)/shard_map/ppermute | solution.py:482
  122.7 24.7 %all_to_all.34 = bf16[64,48,128]{2,1,0:T(8,128)(2,1)S(1)} all-to-all(bf16[64,48,128]{2,1,0:T(8,128)(2,1)S(1)} %bitcast.55), channel_id=1, replica_groups={{0,1,2,3,4,5,6,7,8,9,10,11,12,13,14,15,32,33,34,35,36,37,38,39,40,41,42..., dimensions={0} | all-to-all | bytes 1572864 | tf_op jit(solution)/shard_map/all_to_all | solution.py:382
  147.7 18.6 %all_to_all.35 = bf16[64,48,128]{2,1,0:T(8,128)(2,1)S(1)} all-to-all(bf16[64,48,128]{2,1,0:T(8,128)(2,1)S(1)} %broadcast_in_dim.2), channel_id=1, replica_groups={{0,1,2,3,4,5,6,7,8,9,10,11,12,13,14,15,32,33,34,35,36,37,38,39,40,41,42..., dimensions={0} | all-to-all | bytes 1572864 | tf_op jit(solution)/shard_map/all_to_all | solution.py:382
  166.3 2.9 %collective-permute-start.9 = (bf16[3072,128]{1,0:T(8,128)(2,1)S(1)}, bf16[3072,128]{1,0:T(8,128)(2,1)S(1)}, u32[]{:S(2)}, u32[]{:S(2)}) collective-permute-start(bf16[3072,128]{1,0:T(8,128)(2,1)S(1)} %bitcast.39), channel_id=1, source_target_pairs={{0,16},{16,0},{32,48},{48,32},{64,80},{80,64},{96,112},{112,96},{1... | collective-permute-start | bytes 2359304 | tf_op jit(solution)/shard_map/ppermute | solution.py:486
  169.2 1.9 %collective-permute-done.9.other = bf16[3072,128]{1,0:T(8,128)(2,1)S(1)} collective-permute-done((bf16[3072,128]{1,0:T(8,128)(2,1)S(1)}, bf16[3072,128]{1,0:T(8,128)(2,1)S(1)}, u32[]{:S(2)}, u32[]{:S(2)}) %collective-permute-start.9) | collective-permute-done | bytes 786464 | tf_op jit(solution)/shard_map/ppermute | solution.py:486
  171.1 2.1 %shard_map.158 = (f32[3,3,192,192]{3,2,1,0:T(8,128)}, f32[3,3,192,192]{3,2,1,0:T(8,128)}, f32[64,192]{1,0:T(8,128)}, f32[8,256]{1,0:T(8,128)S(1)}, f32[8,128]{1,0:T(8,128)S(1)}) custom-call(s32[1]{0:T(128)} %bitcast.11.core, bf16[3072,128]{1,0:T(8,128)(2,1)S(1)} %bitcast.40, bf16[3072,128]{1,0:T(8,128)(2,1)S(1)} %collective-permute-done.9.other), custom_call_target="tpu_custom_call" | custom-call | bytes 4000000 | tf_op jit(solution)/shard_map/pallas_call | solution.py:391
  (54 shorter events, 8.1 us)
Async XLA Ops:
  0.6 24.0 %copy-start.12 = (bf16[64,8,128]{2,1,0:T(8,128)(2,1)S(1)}, bf16[64,8,128]{2,1,0:T(8,128)(2,1)}, u32[]{:S(2)}) copy-start(bf16[64,8,128]{2,1,0:T(8,128)(2,1)} %param.10) | copy-start | bytes 393220
  0.6 16.7 %copy-start.15 = (s32[1,128]{1,0:T(1,128)S(1)}, s32[1,128]{1,0:T(1,128)}, u32[]{:S(2)}) copy-start(s32[1,128]{1,0:T(1,128)} %param.17) | copy-start | bytes 1540
  0.7 16.8 %copy-start.13 = (s32[1,4,16384]{2,1,0:T(4,128)S(1)}, s32[1,4,16384]{2,1,0:T(4,128)}, u32[]{:S(2)}) copy-start(s32[1,4,16384]{2,1,0:T(4,128)} %param.15) | copy-start | bytes 786436
  0.7 16.8 %copy-start.14 = (f32[1,4,16384]{2,1,0:T(4,128)S(1)}, f32[1,4,16384]{2,1,0:T(4,128)}, u32[]{:S(2)}) copy-start(f32[1,4,16384]{2,1,0:T(4,128)} %param.16) | copy-start | bytes 786436
  1.8 7.3 %collective-permute-start = (bf16[2,128,64]{1,0,2:T(2,128)(2,1)S(1)}, bf16[2,128,64]{1,0,2:T(2,128)(2,1)S(1)}, u32[]{:S(2)}, u32[]{:S(2)}) collective-permute-start(bf16[2,128,64]{1,0,2:T(2,128)(2,1)S(1)} %get-tuple-element.41), channel_id=1, source_target_pairs={{0,16},{16,32},{32,48},{48,64},{64,80},{80,96},{96,112},{1,17},{17... | collective-permute-start | bytes 98312 | tf_op jit(solution)/shard_map/ppermute | solution.py:376
  6.4 5.2 %collective-permute-start.1 = (bf16[2,128,64]{1,0,2:T(2,128)(2,1)S(1)}, bf16[2,128,64]{1,0,2:T(2,128)(2,1)S(1)}, u32[]{:S(2)}, u32[]{:S(2)}) collective-permute-start(bf16[2,128,64]{1,0,2:T(2,128)(2,1)S(1)} %get-tuple-element.42), channel_id=1, source_target_pairs={{16,0},{32,16},{48,32},{64,48},{80,64},{96,80},{112,96},{17,1},{33... | collective-permute-start | bytes 98312 | tf_op jit(solution)/shard_map/ppermute | solution.py:377
  12.8 7.6 %collective-permute-start.2 = (bf16[12,2,64]{1,0,2:T(8,128)(2,1)S(1)}, bf16[12,2,64]{1,0,2:T(8,128)(2,1)S(1)}, u32[]{:S(2)}, u32[]{:S(2)}) collective-permute-start(bf16[12,2,64]{1,0,2:T(8,128)(2,1)S(1)} %get-tuple-element.39), channel_id=1, source_target_pairs={{0,1},{1,2},{2,3},{3,4},{4,5},{5,6},{6,7},{7,8},{8,9},{9,10},{10,1... | collective-permute-start | bytes 9224 | tf_op jit(solution)/shard_map/ppermute | solution.py:376
  15.9 8.7 %collective-permute-start.3 = (bf16[12,2,64]{1,0,2:T(8,128)(2,1)S(1)}, bf16[12,2,64]{1,0,2:T(8,128)(2,1)}, u32[]{:S(2)}, u32[]{:S(2)}) collective-permute-start(bf16[12,2,64]{1,0,2:T(8,128)(2,1)S(1)} %get-tuple-element.40), channel_id=1, source_target_pairs={{1,0},{2,1},{3,2},{4,3},{5,4},{6,5},{7,6},{8,7},{9,8},{10,9},{11,1... | collective-permute-start | bytes 9224 | tf_op jit(solution)/shard_map/ppermute | solution.py:377
  17.5 11.0 %copy-start = (bf16[3,3,192,192]{3,2,1,0:T(8,128)(2,1)S(1)}, bf16[3,3,192,192]{3,2,1,0:T(8,128)(2,1)}, u32[]{:S(2)}) copy-start(bf16[3,3,192,192]{3,2,1,0:T(8,128)(2,1)} %c1.3) | copy-start | bytes 1990660
  17.5 11.0 %copy-start.2 = (bf16[3,3,192,192]{3,2,1,0:T(8,128)(2,1)S(1)}, bf16[3,3,192,192]{3,2,1,0:T(8,128)(2,1)}, u32[]{:S(2)}) copy-start(bf16[3,3,192,192]{3,2,1,0:T(8,128)(2,1)} %c2.3) | copy-start | bytes 1990660
  28.5 32.8 %copy-start.8 = (s32[1,16384]{1,0:T(1,128)S(1)}, s32[1,16384]{1,0:T(1,128)}, u32[]{:S(2)}) copy-start(s32[1,16384]{1,0:T(1,128)} %param.18) | copy-start | bytes 196612
  28.5 32.8 %copy-start.9 = (f32[6,2048]{1,0:T(8,128)S(1)}, f32[6,2048]{1,0:T(8,128)}, u32[]{:S(2)}) copy-start(f32[6,2048]{1,0:T(8,128)} %target.1) | copy-start | bytes 147460
  36.8 30.8 %copy-start.4 = (bf16[1440,256]{1,0:T(8,128)(2,1)}, bf16[1440,256]{1,0:T(8,128)(2,1)S(1)}, u32[]{:S(2)}) copy-start(bf16[1440,256]{1,0:T(8,128)(2,1)S(1)} %get-tuple-element.29.gp) | copy-start | bytes 2211844
  36.8 30.7 %copy-start.6 = (bf16[1152,256]{1,0:T(8,128)(2,1)}, bf16[1152,256]{1,0:T(8,128)(2,1)S(1)}, u32[]{:S(2)}) copy-start(bf16[1152,256]{1,0:T(8,128)(2,1)S(1)} %get-tuple-element.30.h2b) | copy-start | bytes 1769476
  36.8 30.7 %copy-start.10 = (bf16[1440,256]{1,0:T(8,128)(2,1)}, bf16[1440,256]{1,0:T(8,128)(2,1)S(1)}, u32[]{:S(2)}) copy-start(bf16[1440,256]{1,0:T(8,128)(2,1)S(1)} %get-tuple-element.26.a1) | copy-start | bytes 2211844
  91.2 4.6 %collective-permute-start.4 = (f32[2,8,128]{2,1,0:T(8,128)S(1)}, f32[2,8,128]{2,1,0:T(8,128)S(1)}, u32[]{:S(2)}, u32[]{:S(2)}) collective-permute-start(f32[2,8,128]{2,1,0:T(8,128)S(1)} %get-tuple-element.45), channel_id=1, source_target_pairs={{0,16},{16,32},{32,48},{48,64},{64,80},{80,96},{96,112},{1,17},{17... | collective-permute-start | bytes 24584 | tf_op jit(solution)/shard_map/ppermute | solution.py:376
  93.8 5.0 %collective-permute-start.5 = (f32[2,8,128]{2,1,0:T(8,128)S(1)}, f32[2,8,128]{2,1,0:T(8,128)S(1)}, u32[]{:S(2)}, u32[]{:S(2)}) collective-permute-start(f32[2,8,128]{2,1,0:T(8,128)S(1)} %get-tuple-element.46), channel_id=1, source_target_pairs={{16,0},{32,16},{48,32},{64,48},{80,64},{96,80},{112,96},{17,1},{33... | collective-permute-start | bytes 24584 | tf_op jit(solution)/shard_map/ppermute | solution.py:377
  98.9 6.2 %collective-permute-start.6 = (f32[12,8,2]{2,1,0:T(8,128)S(1)}, f32[12,8,2]{2,1,0:T(8,128)S(1)}, u32[]{:S(2)}, u32[]{:S(2)}) collective-permute-start(f32[12,8,2]{2,1,0:T(8,128)S(1)} %get-tuple-element.43), channel_id=1, source_target_pairs={{0,1},{1,2},{2,3},{3,4},{4,5},{5,6},{6,7},{7,8},{8,9},{9,10},{10,1... | collective-permute-start | bytes 2312 | tf_op jit(solution)/shard_map/ppermute | solution.py:376
  101.1 4.8 %collective-permute-start.7 = (f32[12,8,2]{2,1,0:T(8,128)S(1)}, f32[12,8,2]{2,1,0:T(8,128)S(1)}, u32[]{:S(2)}, u32[]{:S(2)}) collective-permute-start(f32[12,8,2]{2,1,0:T(8,128)S(1)} %get-tuple-element.44), channel_id=1, source_target_pairs={{1,0},{2,1},{3,2},{4,3},{5,4},{6,5},{7,6},{8,7},{9,8},{10,9},{11,1... | collective-permute-start | bytes 2312 | tf_op jit(solution)/shard_map/ppermute | solution.py:377
  102.6 1.1 copy-start.11
  108.8 1.4 copy-start.1
  108.8 1.6 copy-start.5
  110.4 1.2 copy-start.3
  111.6 1.1 copy-start.7
  120.2 2.4 %collective-permute-start.8 = (bf16[3072,128]{1,0:T(8,128)(2,1)S(1)}, bf16[3072,128]{1,0:T(8,128)(2,1)S(1)}, u32[]{:S(2)}, u32[]{:S(2)}) collective-permute-start(bf16[3072,128]{1,0:T(8,128)(2,1)S(1)} %slice.53), channel_id=1, source_target_pairs={{0,16},{16,0},{32,48},{48,32},{64,80},{80,64},{96,112},{112,96},{1... | collective-permute-start | bytes 2359304 | tf_op jit(solution)/shard_map/ppermute | solution.py:482
  166.3 4.8 %collective-permute-start.9 = (bf16[3072,128]{1,0:T(8,128)(2,1)S(1)}, bf16[3072,128]{1,0:T(8,128)(2,1)S(1)}, u32[]{:S(2)}, u32[]{:S(2)}) collective-permute-start(bf16[3072,128]{1,0:T(8,128)(2,1)S(1)} %bitcast.39), channel_id=1, source_target_pairs={{0,16},{16,0},{32,48},{48,32},{64,80},{80,64},{96,112},{112,96},{1... | collective-permute-start | bytes 2359304 | tf_op jit(solution)/shard_map/ppermute | solution.py:486

commit v2 on v1

--- a/solution.py
+++ b/solution.py
@@ -64,9 +64,38 @@
     return (word >> 16).astype(F32), ((word & 65535) - 32768).astype(F32)
 
 
+def fields_kernel(f8, north, south, ftm, fm, wl, wr, s8, sn, ss, sw, se):
+    s8[...] = f8[...].astype(F32)
+    sn[...] = north[...].astype(F32)
+    ss[...] = south[...].astype(F32)
+    sw[...] = jnp.zeros_like(sw)
+    se[...] = jnp.zeros_like(se)
+    for r in range(12):
+        if r < 2:
+            block = sn[pl.ds(r, 64, stride=2), :]
+        elif r < 10:
+            block = s8[pl.ds(r - 2, 64, stride=8), :]
+            fm[:, (r - 2) * 128 : (r - 1) * 128] = block.astype(BF)
+        else:
+            block = ss[pl.ds(r - 10, 64, stride=2), :]
+        turned = block.T
+        ftm[r * 128 : r * 128 + 128, :] = turned.astype(BF)
+        sw[2 * r : 2 * r + 2, :] = turned[0:2]
+        se[2 * r : 2 * r + 2, :] = turned[126:128]
+    wl[...] = sw[...].astype(BF)
+    wr[...] = se[...].astype(BF)
+
+
+def turn_field_kernel(gf, north, south, et, wl, wr):
+    turned = jnp.concatenate([north[...], gf[...], south[...]], 0).T
+    et[...] = turned
+    wl[...] = turned[0:2]
+    wr[...] = turned[126:128]
+
+
 def forward_kernel(
-    flags, ft, small, c1, c2, cells, wts, cnt, out, a1_out, gp, h2b, hs, xcat, as_, acat, w1, w2,
-    fq, pf,
+    flags, ftm, wl, wr, small, c1, c2, cells, wts, cnt, out, a1_out, gp, h2c, hs, xcat, as_, acat,
+    w1, w2, fq, pf,
 ):
     zero8 = jnp.zeros((8, CP), F32)
     hs[0:8, :] = zero8
@@ -75,7 +104,14 @@
     as_[N10 + 8 : N10 + 16, :] = zero8
     stack_weights(w1, c1, 1)
     stack_weights(w2, c2, 1)
-    hs[8 : N12 + 8, :] = dot(ft[...], small[0:64, :])
+    main = dot(ftm[...], small[0:64, :])
+    west, east = dot(wl[...], small[0:64, :]), dot(wr[...], small[0:64, :])
+    for r in range(12):
+        at = 8 + r * ROW
+        hs[at + 128 : at + ROW, :] = jnp.zeros((ROW - 128, CP), F32)
+        hs[at : at + 2, :] = west[2 * r : 2 * r + 2]
+        hs[at + 2 : at + 130, :] = main[r * 128 : r * 128 + 128]
+        hs[at + 130 : at + 132, :] = east[2 * r : 2 * r + 2]
     for b in range(3):
         xcat[:, b * CP : (b + 1) * CP] = hs[7 + b : 7 + b + N12, :].astype(BF)
     col = lax.broadcasted_iota(I32, (ROW, CP), 0)
@@ -104,9 +140,11 @@
     for part in range(4):
         at = part * 2 * ROW
         h2 = hs[8 + 2 * ROW + at : 8 + 4 * ROW + at, :] + taps(acat, w2, at, 2 * ROW, 1)
-        h2b[at : at + 2 * ROW, :] = h2.astype(BF)
-    field = dot(small[64:80, :], h2b[...], NT)
-    tiles = [field[0:8, r * ROW + 2 : r * ROW + 2 + TW] for r in range(8)]
+        as_[at : at + 2 * ROW, :] = h2
+    for r in range(8):
+        h2c[r * 128 : r * 128 + 128, :] = as_[r * ROW + 2 : r * ROW + 130, :].astype(BF)
+    field = dot(small[64:80, :], h2c[...], NT)
+    tiles = [field[0:8, r * 128 : r * 128 + 128] for r in range(8)]
     top = tiles[0]
     for r in range(1, 8):
         top = jnp.maximum(jnp.abs(top), jnp.abs(tiles[r]))
@@ -143,9 +181,14 @@
     out[...] = pf[...].astype(BF)
 
 
-def turn_kernel(a1, ft, small, a1t, h0t, wide, thin, pa, pt):
+def turn_kernel(a1, ftm, wl, wr, small, a1t, h0t, wide, thin, pa, pt):
     wide[...] = a1[...].astype(F32)
-    thin[...] = ft[...].astype(F32)
+    west, east = wl[...].astype(F32), wr[...].astype(F32)
+    for r in range(12):
+        at = r * ROW
+        thin[at : at + 2, :] = west[2 * r : 2 * r + 2]
+        thin[at + 2 : at + 130, :] = ftm[r * 128 : r * 128 + 128, :].astype(F32)
+        thin[at + 130 : at + 132, :] = east[2 * r : 2 * r + 2]
     ones = lax.broadcasted_iota(I32, (CP, CP), 0) == lax.broadcasted_iota(I32, (CP, CP), 1)
     same = jnp.where(ones, 1.0, 0.0).astype(BF)
     win_t = dot(same[0:C, :], small[0:64, :], NT).astype(BF)
@@ -266,8 +309,8 @@
 
 
 def backward_kernel(
-    core, gfn, ft, a1t, h0t, gp, h2b, c2, c1, small, loss, pay, gfields, gs, g2cat, zs, gzcat, own,
-    w2, w1, gc,
+    core, gf, et, gl, gr, fm, a1t, h0t, gp, h2c, c2, c1, small, loss, pay, gfields, es, bw, gs,
+    g2cat, zs, gzcat, w2, w1, gc,
 ):
     zero8 = jnp.zeros((8, CP), F32)
     gs[0:8, :] = zero8
@@ -276,7 +319,6 @@
     zs[N10 + 8 : N10 + 16, :] = zero8
     stack_weights(w2, c2, -1)
     stack_weights(w1, c1, -1)
-    wo = small[64:72, :]
     base_s = pl.multiple_of(core[0] * HALF, 16)
     base_f = pl.multiple_of((1 - core[0]) * HALF, 16)
 
@@ -293,10 +335,21 @@
                 rest = mine[:, 128:256]
                 put(base, REST + tap * 96, rest[0:96] + pltpu.roll(rest[96:192], 64, 1))
 
-    x = gfn[...]
+    es[...] = jnp.zeros_like(es)
+    es[2:130, 0:96] = et[...]
+    es[0:2, 0:96] = gl[...]
+    es[130:132, 0:96] = gr[...]
+    bw[...] = jnp.zeros_like(bw)
+    for r in range(12):
+        at, block = (r // 2) * 16, small[64 + 16 * (r % 2) : 80 + 16 * (r % 2), :]
+        bw[at : at + 16, r * CP : (r + 1) * CP] = block
+        bw[128 + at : 144 + at, r * CP : (r + 1) * CP] = block
+    x = es[...]
     x_hi = x.astype(BF)
     x_lo = (x - x_hi.astype(F32)).astype(BF)
-    gs[8 : N12 + 8, :] = dot(x_hi, wo) + dot(x_lo, wo)
+    both = jnp.concatenate([x_hi, x_lo], 1)
+    for r in range(12):
+        gs[8 + r * ROW : 8 + (r + 1) * ROW, :] = dot(both, bw[:, r * CP : (r + 1) * CP])
     for b in range(3):
         g2cat[:, b * CP : (b + 1) * CP] = gs[9 - b : 9 - b + N12, :].astype(BF)
     for r in range(8):
@@ -313,21 +366,23 @@
         at = 8 + (r + 1) * ROW + 2
         gc[r * 128 : r * 128 + 128, :] = zs[at : at + 128, :].astype(BF)
     put_taps(base_f, h0t)
-    col = lax.broadcasted_iota(I32, (ROW, CP), 0)
-    keep = jnp.where((col >= 2) & (col < 2 + TW), 1.0, 0.0)
-    keep2 = jnp.concatenate([keep, keep], 0)
     for part in range(4):
-        at = part * 2 * ROW
-        g = gs[8 + 2 * ROW + at : 8 + 4 * ROW + at, :] + taps(gzcat, w1, at, 2 * ROW, -1)
-        own[at : at + 2 * ROW, :] = (g * keep2).astype(BF)
-    g_in = dot(ft[2 * ROW : 10 * ROW, :], own[...], TN)
-    g_fields = dot(small[0:64, :], own[...], NT)
-    for r in range(8):
-        gfields[pl.ds(r, 64, stride=8), :] = g_fields[:, r * ROW + 2 : r * ROW + 2 + TW]
-    x_own = x[2 * ROW : 10 * ROW] * jnp.concatenate([keep[:, 0:8]] * 8, 0)
-    o_hi = x_own.astype(BF)
-    o_lo = (x_own - o_hi.astype(F32)).astype(BF)
-    g_out = dot(o_hi, h2b[...], TN) + dot(o_lo, h2b[...], TN)
+        at = 8 + 2 * ROW + part * 2 * ROW
+        gs[at : at + 2 * ROW, :] = gs[at : at + 2 * ROW, :] + taps(
+            gzcat, w1, part * 2 * ROW, 2 * ROW, -1
+        )
+    for r in range(8):
+        at = 8 + (r + 2) * ROW + 2
+        gc[r * 128 : r * 128 + 128, :] = gs[at : at + 128, :].astype(BF)
+    g_in = dot(fm[...], gc[...])
+    g_fields = dot(small[0:64, :], gc[...], NT)
+    for r in range(8):
+        gfields[pl.ds(r, 64, stride=8), :] = g_fields[:, r * 128 : r * 128 + 128]
+    line = jnp.concatenate([gf[r * 8 : r * 8 + 8, :] for r in range(8)], 1)
+    line_hi = line.astype(BF).astype(F32)
+    line2 = jnp.concatenate([line_hi, line - line_hi], 0).astype(BF)
+    g_out = dot(line2, h2c[...])
+    g_out = g_out[0:8] + g_out[8:16]
     put(base_s, EXTRA, g_in[:, 0:128])
     rest = g_in[:, 128:256]
     put(base_s, EXTRA + 64, rest[0:32] + pltpu.roll(rest[32:64], 64, 1))
@@ -367,15 +422,11 @@
         both(other, mine)
 
 
-def neighbours(array, axis, dim, width):
-    count, length = lax.axis_size(axis), array.shape[dim]
+def shift_pair(last, first, axis):
+    count = lax.axis_size(axis)
     up = [(i, i + 1) for i in range(count - 1)]
     down = [(j, i) for i, j in up]
-    last = lax.slice_in_dim(array, length - width, length, axis=dim)
-    first = lax.slice_in_dim(array, 0, width, axis=dim)
-    before = lax.ppermute(last, axis, up)
-    after = lax.ppermute(first, axis, down)
-    return jnp.concatenate([before, array, after], axis=dim)
+    return lax.ppermute(last, axis, up), lax.ppermute(first, axis, down)
 
 
 def exchange(rows, groups=None):
@@ -419,31 +470,41 @@
     wts = slot_weights.reshape(4, 128, CAP)
     cnt = slot_count.reshape(128, 1)
     obs = recv_obs.reshape(128, CAP)
-    small = jnp.concatenate([w_in, jnp.pad(w_out.T, ((0, 10), (0, 0)))], 0)
+    turned = w_out.T
+    small = jnp.concatenate(
+        [w_in, jnp.pad(turned, ((0, 10), (0, 0))), jnp.pad(turned, ((8, 2), (0, 0)))], 0
+    )
     small = jnp.pad(small, ((0, 0), (0, CP - C)))
 
-    grid = fields.transpose(1, 2, 0)
-    grid = neighbours(grid, "ns", 0, 2)
-    grid = neighbours(grid, "ew", 1, 2)
-    ft = jnp.pad(grid, ((0, 0), (0, ROW - TW - 4), (0, 0))).reshape(N12, 64)
-    sent, a1, gp, h2b = call(
+    north, south = shift_pair(
+        fields[:, 6:8].reshape(128, 128), fields[:, 0:2].reshape(128, 128), "ns"
+    )
+    ftm, fm, first, last = call(
+        fields_kernel,
+        [((12 * 128, 64), BF), ((64, 1024), BF), ((32, 64), BF), ((32, 64), BF)],
+        [((512, 128), F32), ((128, 128), F32), ((128, 128), F32), ((32, 64), F32), ((32, 64), F32)],
+        fields.reshape(512, 128), north, south,
+        vmem=8,
+    )
+    west, east = shift_pair(last, first, "ew")
+    sent, a1, gp, h2c = call(
         forward_kernel,
-        [((1024, 128), BF), ((N10, CP), BF), ((N10, CP), BF), ((N8, CP), BF)],
+        [((1024, 128), BF), ((N10, CP), BF), ((N10, CP), BF), ((1024, CP), BF)],
         [
             ((N12 + 16, CP), F32), ((N12, 3 * CP), BF), ((N10 + 16, CP), F32),
             ((N10, 3 * CP), BF), ((3, 3 * CP, CP), BF), ((3, 3 * CP, CP), BF),
             ((64, 128), I32), ((1024, 128), F32),
         ],
-        flags, ft, small, conv_first, conv_second, cells, wts, cnt,
-        smem=1, vmem=40, flops=2 * 10**9,
+        flags, ftm, west, east, small, conv_first, conv_second, cells, wts, cnt,
+        smem=1, vmem=28, flops=2 * 10**9,
     )
     received = exchange(sent)
     a1t, h0t = call(
         turn_kernel,
         [((3 * C, 1280), BF), ((3 * C, 1280), BF)],
         [((N10, CP), F32), ((N12, 64), F32), ((1280, CP), BF), ((1280, 64), BF)],
-        a1, ft, small,
-        vmem=32, flops=10**9,
+        a1, ftm, west, east, small,
+        vmem=16, flops=10**9,
     )
     pred, loss, back = call(
         owner_kernel,
@@ -453,7 +514,7 @@
             ((1024, 128), F32),
         ],
         received, obs, targets,
-        vmem=32, flops=10**9,
+        vmem=16, flops=10**9,
     )
     grads = exchange(back)
     (g_field,) = call(
@@ -461,21 +522,28 @@
         [((64, 128), F32)],
         [((96, 4096), BF), ((64, 4096), BF), ((96, 64), F32)],
         grads, cells, wts, cnt,
-        vmem=32, flops=10**9,
-    )
-    g_field = neighbours(g_field.reshape(8, 8, 128), "ns", 0, 2)
-    g_field = neighbours(g_field, "ew", 2, 2).transpose(0, 2, 1)
-    gfn = jnp.pad(g_field, ((0, 0), (0, ROW - TW - 4), (0, 0))).reshape(N12, 8)
+        vmem=12, flops=10**9,
+    )
+    north, south = shift_pair(g_field[48:64], g_field[0:16], "ns")
+    et, first, last = call(
+        turn_field_kernel,
+        [((128, 96), F32), ((2, 96), F32), ((2, 96), F32)],
+        [],
+        g_field, north, south,
+        vmem=4,
+    )
+    g_west, g_east = shift_pair(last, first, "ew")
     pay, g_fields = call(
         backward_kernel,
         [((2 * HALF, 128), BF), ((512, 128), F32)],
         [
-            ((N12 + 16, CP), F32), ((N12, 3 * CP), BF), ((N10 + 16, CP), F32),
-            ((N10, 3 * CP), BF), ((N8, CP), BF), ((3, CP, 3 * CP), BF), ((3, CP, 3 * CP), BF),
-            ((1024, CP), BF),
+            ((ROW, 128), F32), ((CP, 12 * CP), BF), ((N12 + 16, CP), F32), ((N12, 3 * CP), BF),
+            ((N10 + 16, CP), F32), ((N10, 3 * CP), BF), ((3, CP, 3 * CP), BF),
+            ((3, CP, 3 * CP), BF), ((1024, CP), BF),
         ],
-        core, gfn, ft, a1t, h0t, gp, h2b, conv_second, conv_first, small, loss,
-        smem=1, vmem=40, flops=2 * 10**9,
+        core, g_field, et, g_west, g_east, fm, a1t, h0t, gp, h2c, conv_second, conv_first, small,
+        loss,
+        smem=1, vmem=28, flops=2 * 10**9,
     )
     pairs = [(n, n + 1 - 2 * (n % 2)) for n in range(n_ns)]
     groups = [[n * n_ew + e for n in range(c, n_ns, 2) for e in range(n_ew)] for c in range(2)]
@@ -489,7 +557,7 @@
         [((3, 3, C, C), F32), ((3, 3, C, C), F32), ((64, C), F32), ((8, CP), F32), ((8, 128), F32)],
         [],
         core, mine, other,
-        smem=1, vmem=32,
+        smem=1, vmem=16,
     )
     return (
         pred,

time: 175 us -> 160 us (0.914)
  waiting for transfers between devices: 17.6 us -> 8.56 us
  local copies, waits for them, and re-layouts: 12.1 us -> 8.28 us
  other arithmetic: 4.62 us -> 1.23 us
    ppermute x8, waiting for transfers between devices: 13.4 us -> 4.74 us  [shift_pair(): return (lax.ppermute(last, axis, up), lax.ppermute(first, axis, down))]
    concatenate x4 -> x1, other arithmetic: 3.44 us -> 0.8 us  [on_device(): jnp.concatenate([w_in, jnp.pad(turned, ((0, 10), (0, 0))), jnp.pad(turned...]
    pad x2 -> x0, local copies, waits for them, and re-layouts: 2.42 us -> none  [the longest x1 1.33 us: on_device(): gfn = jnp.pad(g_field, ((0, 0), (0, ROW - TW - 4), (0, 0))).reshape(N12, 8)]
    unnamed x36 -> x16, local copies, waits for them, and re-layouts: 7.02 us -> 5.2 us
    pallas_call x6 -> x8, Pallas kernels: 33.8 us -> 33.8 us  [call(): pl.pallas_call(kernel, out_shape=[jax.ShapeDtypeStruct(s, d) for s, d in...]
  transfers between devices with their start and end apart: 10 -> 10, of which waited for: 7 -> 6; matrix products, arithmetic and copies ran while one was open for 1% -> 2% of each run, Pallas kernels for 1% -> 1%
where the time goes in v2:
time: 160 us
  blocking collectives  83.2 us (52%)
  Pallas kernels  33.8 us (21%)
  starting transfers between devices  23.8 us (15%)
  waiting for transfers between devices  8.56 us (5%)
  local copies, waits for them, and re-layouts  8.28 us (5%)
    all_to_all x4, blocking collectives, exchange(): lax.all_to_all(rows, AXES, split_axis=0, concat_axis=0, tiled=True, axis_...  83.2 us
    pallas_call x8, Pallas kernels, call(): pl.pallas_call(kernel, out_shape=[jax.ShapeDtypeStruct(s, d) for s, d in...  33.8 us
    ppermute x8, starting transfers between devices, shift_pair(): return (lax.ppermute(last, axis, up), lax.ppermute(first, axis, down))  20.2 us
    unnamed x16, local copies, waits for them, and re-layouts  5.2 us
    ppermute x8, waiting for transfers between devices, shift_pair(): return (lax.ppermute(last, axis, up), lax.ppermute(first, axis, down))  4.74 us
  transfers between devices with their start and end apart: 10, of which 6 were waited for; matrix products, arithmetic and copies ran while one was open for 2% of the time, Pallas kernels for 1%

profile of v2, /device:TPU:1, one launch (start us, length us, event | category | flops | bytes accessed | tf_op | source)
XLA Modules:
  0.0 159.7 jit_solution(9936913924916651362)
XLA Ops:
  0.6 1.0 fusion.5
  1.7 4.6 %collective-permute-start = (bf16[128,128]{1,0:T(8,128)(2,1)S(1)}, bf16[128,128]{1,0:T(8,128)(2,1)S(1)}, u32[]{:S(2)}, u32[]{:S(2)}) collective-permute-start(bf16[128,128]{1,0:T(8,128)(2,1)S(1)} %bitcast.47), channel_id=1, source_target_pairs={{0,16},{16,32},{32,48},{48,64},{64,80},{80,96},{96,112},{1,17},{17... | collective-permute-start | bytes 98312 | tf_op jit(solution)/shard_map/ppermute | solution.py:429
  6.3 1.9 %collective-permute-start.1 = (bf16[128,128]{1,0:T(8,128)(2,1)S(1)}, bf16[128,128]{1,0:T(8,128)(2,1)S(1)}, u32[]{:S(2)}, u32[]{:S(2)}) collective-permute-start(bf16[128,128]{1,0:T(8,128)(2,1)S(1)} %bitcast.46), channel_id=1, source_target_pairs={{16,0},{32,16},{48,32},{64,48},{80,64},{96,80},{112,96},{17,1},{33... | collective-permute-start | bytes 98312 | tf_op jit(solution)/shard_map/ppermute | solution.py:429
  8.2 0.8 fusion.4
  9.0 2.5 %collective-permute-done.1.south = bf16[128,128]{1,0:T(8,128)(2,1)S(1)} collective-permute-done((bf16[128,128]{1,0:T(8,128)(2,1)S(1)}, bf16[128,128]{1,0:T(8,128)(2,1)S(1)}, u32[]{:S(2)}, u32[]{:S(2)}) %collective-permute-start.1) | collective-permute-done | bytes 32800 | tf_op jit(solution)/shard_map/ppermute | solution.py:429
  11.5 0.9 copy-done
  12.7 3.1 %collective-permute-start.2 = (bf16[32,64]{1,0:T(8,128)(2,1)S(1)}, bf16[32,64]{1,0:T(8,128)(2,1)S(1)}, u32[]{:S(2)}, u32[]{:S(2)}) collective-permute-start(bf16[32,64]{1,0:T(8,128)(2,1)S(1)} %get-tuple-element.31), channel_id=1, source_target_pairs={{0,1},{1,2},{2,3},{3,4},{4,5},{5,6},{6,7},{7,8},{8,9},{9,10},{10,1... | collective-permute-start | bytes 12296 | tf_op jit(solution)/shard_map/ppermute | solution.py:429
  15.8 1.3 collective-permute-start.3
  17.2 0.8 copy.17.cnt
  18.0 1.0 copy.24
  18.9 1.0 copy.23
  20.2 1.2 copy-done.1
  21.4 1.2 copy-done.3
  22.5 8.2 %shard_map.154 = (bf16[1024,128]{1,0:T(8,128)(2,1)S(1)}, bf16[1440,256]{1,0:T(8,128)(2,1)S(1)}, bf16[1440,256]{1,0:T(8,128)(2,1)S(1)}, bf16[1024,256]{1,0:T(8,128)(2,1)S(1)}) custom-call(f32[4]{0:T(128)S(1)} %add_convert_fusion.1.flags, bf16[1536,64]{1,0:T(8,128)(2,1)S(1)} %get-tuple-element.30.ftm, bf16[32,64]{1,0:T(8,128)(2,1)S(1)} %collective-permute-done.2.wl, ...), custom_call_target="tpu_custom_call" | custom-call | flops 2000000000 | bytes 4000000 | tf_op jit(solution)/shard_map/pallas_call | solution.py:442
  30.8 23.3 %all_to_all.32 = bf16[128,8,128]{2,1,0:T(8,128)(2,1)S(1)} all-to-all(bf16[128,8,128]{2,1,0:T(8,128)(2,1)S(1)} %bitcast.38), channel_id=1, replica_groups=mesh['ns'=8,'ew'=16] {'ns','ew'}, dimensions={0} | all-to-all | bytes 524288 | tf_op jit(solution)/shard_map/all_to_all | solution.py:433
  54.1 6.2 %shard_map.155 = (f32[6,2048]{1,0:T(8,128)}, f32[16,128]{1,0:T(8,128)S(1)}, bf16[1024,128]{1,0:T(8,128)(2,1)S(1)}) custom-call(bf16[1024,128]{1,0:T(8,128)(2,1)S(1)} %bitcast.39, s32[128,128]{1,0:T(8,128)S(1)} %bitcast.42, f32[6,2048]{1,0:T(8,128)S(1)} %copy-done.6), custom_call_target="tpu_custom_call" | custom-call | flops 1000000000 | bytes 4000000 | tf_op jit(solution)/shard_map/pallas_call | solution.py:442
  60.3 15.3 %all_to_all.33 = bf16[128,8,128]{2,1,0:T(8,128)(2,1)S(1)} all-to-all(bf16[128,8,128]{2,1,0:T(8,128)(2,1)S(1)} %bitcast.40), channel_id=1, replica_groups=mesh['ns'=8,'ew'=16] {'ns','ew'}, dimensions={0} | all-to-all | bytes 524288 | tf_op jit(solution)/shard_map/all_to_all | solution.py:433
  75.6 8.3 %shard_map.156.gf = f32[64,128]{1,0:T(8,128)S(1)} custom-call(bf16[1024,128]{1,0:T(8,128)(2,1)S(1)} %bitcast.41, s32[4,128,128]{2,1,0:T(8,128)S(1)} %bitcast.35, f32[4,128,128]{2,1,0:T(8,128)S(1)} %bitcast.37, s32[128,1]{1,0:T(8,128)S(1)} %copy.17.cnt), custom_call_target="tpu_custom_call" | custom-call | flops 1000000000 | bytes 4000000 | tf_op jit(solution)/shard_map/pallas_call | solution.py:442
  83.9 2.4 %collective-permute-start.5 = (f32[16,128]{1,0:T(8,128)S(1)}, f32[16,128]{1,0:T(8,128)S(1)}, u32[]{:S(2)}, u32[]{:S(2)}) collective-permute-start(f32[16,128]{1,0:T(8,128)S(1)} %get-tuple-element.55), channel_id=1, source_target_pairs={{16,0},{32,16},{48,32},{64,48},{80,64},{96,80},{112,96},{17,1},{33... | collective-permute-start | bytes 24584 | tf_op jit(solution)/shard_map/ppermute | solution.py:429
  86.3 3.2 %collective-permute-start.4 = (f32[16,128]{1,0:T(8,128)S(1)}, f32[16,128]{1,0:T(8,128)S(1)}, u32[]{:S(2)}, u32[]{:S(2)}) collective-permute-start(f32[16,128]{1,0:T(8,128)S(1)} %get-tuple-element.56), channel_id=1, source_target_pairs={{0,16},{16,32},{32,48},{48,64},{64,80},{80,96},{96,112},{1,17},{17... | collective-permute-start | bytes 24584 | tf_op jit(solution)/shard_map/ppermute | solution.py:429
  90.3 2.2 %collective-permute-start.6 = (f32[2,96]{1,0:T(2,128)S(1)}, f32[2,96]{1,0:T(2,128)S(1)}, u32[]{:S(2)}, u32[]{:S(2)}) collective-permute-start(f32[2,96]{1,0:T(2,128)S(1)} %get-tuple-element.37), channel_id=1, source_target_pairs={{0,1},{1,2},{2,3},{3,4},{4,5},{5,6},{6,7},{7,8},{8,9},{9,10},{10,1... | collective-permute-start | bytes 2312 | tf_op jit(solution)/shard_map/ppermute | solution.py:429
  92.5 1.5 collective-permute-start.7
  94.0 1.6 shard_map.158
  95.6 1.2 collective-permute-done.7.gr
  96.9 7.0 %shard_map.159 = (bf16[6144,128]{1,0:T(8,128)(2,1)S(1)}, f32[512,128]{1,0:T(8,128)}) custom-call(s32[1]{0:T(128)} %bitcast.12.core, f32[64,128]{1,0:T(8,128)S(1)} %shard_map.156.gf, f32[128,96]{1,0:T(8,128)S(1)} %get-tuple-element.36.et, f32[2,96]{1,0:T(2,128)S(1)} %collective-permute-done.6.gl, f32[2,96]{1,0:T(2,128)S(1)} %collective-permute-done.7.gr, ...), custom_call_target="tpu_custom_call" | custom-call | flops 2000000000 | bytes 4000000 | tf_op jit(solution)/shard_map/pallas_call | solution.py:442
  103.9 0.8 collective-permute-start.8
  104.7 1.9 %collective-permute-done.8 = bf16[3072,128]{1,0:T(8,128)(2,1)S(1)} collective-permute-done((bf16[3072,128]{1,0:T(8,128)(2,1)S(1)}, bf16[3072,128]{1,0:T(8,128)(2,1)S(1)}, u32[]{:S(2)}, u32[]{:S(2)}) %collective-permute-start.8) | collective-permute-done | bytes 786464 | tf_op jit(solution)/shard_map/ppermute | solution.py:550
  106.8 26.1 %all_to_all.34 = bf16[64,48,128]{2,1,0:T(8,128)(2,1)S(1)} all-to-all(bf16[64,48,128]{2,1,0:T(8,128)(2,1)S(1)} %bitcast.43), channel_id=1, replica_groups={{0,1,2,3,4,5,6,7,8,9,10,11,12,13,14,15,32,33,34,35,36,37,38,39,40,41,42..., dimensions={0} | all-to-all | bytes 1572864 | tf_op jit(solution)/shard_map/all_to_all | solution.py:433
  133.2 18.6 %all_to_all.35 = bf16[64,48,128]{2,1,0:T(8,128)(2,1)S(1)} all-to-all(bf16[64,48,128]{2,1,0:T(8,128)(2,1)S(1)} %broadcast_in_dim.2), channel_id=1, replica_groups={{0,1,2,3,4,5,6,7,8,9,10,11,12,13,14,15,32,33,34,35,36,37,38,39,40,41,42..., dimensions={0} | all-to-all | bytes 1572864 | tf_op jit(solution)/shard_map/all_to_all | solution.py:433
  151.8 2.9 %collective-permute-start.9 = (bf16[3072,128]{1,0:T(8,128)(2,1)S(1)}, bf16[3072,128]{1,0:T(8,128)(2,1)S(1)}, u32[]{:S(2)}, u32[]{:S(2)}) collective-permute-start(bf16[3072,128]{1,0:T(8,128)(2,1)S(1)} %bitcast.31), channel_id=1, source_target_pairs={{0,16},{16,0},{32,48},{48,32},{64,80},{80,64},{96,112},{112,96},{1... | collective-permute-start | bytes 2359304 | tf_op jit(solution)/shard_map/ppermute | solution.py:554
  154.6 1.9 %collective-permute-done.9.other = bf16[3072,128]{1,0:T(8,128)(2,1)S(1)} collective-permute-done((bf16[3072,128]{1,0:T(8,128)(2,1)S(1)}, bf16[3072,128]{1,0:T(8,128)(2,1)S(1)}, u32[]{:S(2)}, u32[]{:S(2)}) %collective-permute-start.9) | collective-permute-done | bytes 786464 | tf_op jit(solution)/shard_map/ppermute | solution.py:554
  156.6 2.1 %shard_map.160 = (f32[3,3,192,192]{3,2,1,0:T(8,128)}, f32[3,3,192,192]{3,2,1,0:T(8,128)}, f32[64,192]{1,0:T(8,128)}, f32[8,256]{1,0:T(8,128)S(1)}, f32[8,128]{1,0:T(8,128)S(1)}) custom-call(s32[1]{0:T(128)} %bitcast.12.core, bf16[3072,128]{1,0:T(8,128)(2,1)S(1)} %bitcast.32, bf16[3072,128]{1,0:T(8,128)(2,1)S(1)} %collective-permute-done.9.other), custom_call_target="tpu_custom_call" | custom-call | bytes 4000000 | tf_op jit(solution)/shard_map/pallas_call | solution.py:442
  (28 shorter events, 3.1 us)
Async XLA Ops:
  1.7 7.4 %collective-permute-start = (bf16[128,128]{1,0:T(8,128)(2,1)S(1)}, bf16[128,128]{1,0:T(8,128)(2,1)S(1)}, u32[]{:S(2)}, u32[]{:S(2)}) collective-permute-start(bf16[128,128]{1,0:T(8,128)(2,1)S(1)} %bitcast.47), channel_id=1, source_target_pairs={{0,16},{16,32},{32,48},{48,64},{64,80},{80,96},{96,112},{1,17},{17... | collective-permute-start | bytes 98312 | tf_op jit(solution)/shard_map/ppermute | solution.py:429
  6.3 5.2 %collective-permute-start.1 = (bf16[128,128]{1,0:T(8,128)(2,1)S(1)}, bf16[128,128]{1,0:T(8,128)(2,1)S(1)}, u32[]{:S(2)}, u32[]{:S(2)}) collective-permute-start(bf16[128,128]{1,0:T(8,128)(2,1)S(1)} %bitcast.46), channel_id=1, source_target_pairs={{16,0},{32,16},{48,32},{64,48},{80,64},{96,80},{112,96},{17,1},{33... | collective-permute-start | bytes 98312 | tf_op jit(solution)/shard_map/ppermute | solution.py:429
  11.5 0.9 copy-start
  12.7 7.2 %collective-permute-start.2 = (bf16[32,64]{1,0:T(8,128)(2,1)S(1)}, bf16[32,64]{1,0:T(8,128)(2,1)S(1)}, u32[]{:S(2)}, u32[]{:S(2)}) collective-permute-start(bf16[32,64]{1,0:T(8,128)(2,1)S(1)} %get-tuple-element.31), channel_id=1, source_target_pairs={{0,1},{1,2},{2,3},{3,4},{4,5},{5,6},{6,7},{7,8},{8,9},{9,10},{10,1... | collective-permute-start | bytes 12296 | tf_op jit(solution)/shard_map/ppermute | solution.py:429
  15.8 4.4 %collective-permute-start.3 = (bf16[32,64]{1,0:T(8,128)(2,1)S(1)}, bf16[32,64]{1,0:T(8,128)(2,1)S(1)}, u32[]{:S(2)}, u32[]{:S(2)}) collective-permute-start(bf16[32,64]{1,0:T(8,128)(2,1)S(1)} %get-tuple-element.32), channel_id=1, source_target_pairs={{1,0},{2,1},{3,2},{4,3},{5,4},{6,5},{7,6},{8,7},{9,8},{10,9},{11,1... | collective-permute-start | bytes 12296 | tf_op jit(solution)/shard_map/ppermute | solution.py:429
  20.2 1.2 copy-start.1
  21.4 1.2 copy-start.3
  22.5 31.5 %copy-start.5 = (s32[1,16384]{1,0:T(1,128)S(1)}, s32[1,16384]{1,0:T(1,128)}, u32[]{:S(2)}) copy-start(s32[1,16384]{1,0:T(1,128)} %param.18) | copy-start | bytes 196612
  22.5 31.5 %copy-start.6 = (f32[6,2048]{1,0:T(8,128)S(1)}, f32[6,2048]{1,0:T(8,128)}, u32[]{:S(2)}) copy-start(f32[6,2048]{1,0:T(8,128)} %target.1) | copy-start | bytes 147460
  83.9 5.6 %collective-permute-start.5 = (f32[16,128]{1,0:T(8,128)S(1)}, f32[16,128]{1,0:T(8,128)S(1)}, u32[]{:S(2)}, u32[]{:S(2)}) collective-permute-start(f32[16,128]{1,0:T(8,128)S(1)} %get-tuple-element.55), channel_id=1, source_target_pairs={{16,0},{32,16},{48,32},{64,48},{80,64},{96,80},{112,96},{17,1},{33... | collective-permute-start | bytes 24584 | tf_op jit(solution)/shard_map/ppermute | solution.py:429
  86.3 3.9 %collective-permute-start.4 = (f32[16,128]{1,0:T(8,128)S(1)}, f32[16,128]{1,0:T(8,128)S(1)}, u32[]{:S(2)}, u32[]{:S(2)}) collective-permute-start(f32[16,128]{1,0:T(8,128)S(1)} %get-tuple-element.56), channel_id=1, source_target_pairs={{0,16},{16,32},{32,48},{48,64},{64,80},{80,96},{96,112},{1,17},{17... | collective-permute-start | bytes 24584 | tf_op jit(solution)/shard_map/ppermute | solution.py:429
  90.3 5.3 %collective-permute-start.6 = (f32[2,96]{1,0:T(2,128)S(1)}, f32[2,96]{1,0:T(2,128)S(1)}, u32[]{:S(2)}, u32[]{:S(2)}) collective-permute-start(f32[2,96]{1,0:T(2,128)S(1)} %get-tuple-element.37), channel_id=1, source_target_pairs={{0,1},{1,2},{2,3},{3,4},{4,5},{5,6},{6,7},{7,8},{8,9},{9,10},{10,1... | collective-permute-start | bytes 2312 | tf_op jit(solution)/shard_map/ppermute | solution.py:429
  92.5 4.3 %collective-permute-start.7 = (f32[2,96]{1,0:T(2,128)S(1)}, f32[2,96]{1,0:T(2,128)S(1)}, u32[]{:S(2)}, u32[]{:S(2)}) collective-permute-start(f32[2,96]{1,0:T(2,128)S(1)} %get-tuple-element.38), channel_id=1, source_target_pairs={{1,0},{2,1},{3,2},{4,3},{5,4},{6,5},{7,6},{8,7},{9,8},{10,9},{11,1... | collective-permute-start | bytes 2312 | tf_op jit(solution)/shard_map/ppermute | solution.py:429
  94.0 2.8 %copy-start.2 = (bf16[3,3,192,192]{3,2,1,0:T(8,128)(2,1)S(1)}, bf16[3,3,192,192]{3,2,1,0:T(8,128)(2,1)}, u32[]{:S(2)}) copy-start(bf16[3,3,192,192]{3,2,1,0:T(8,128)(2,1)} %c1.3) | copy-start | bytes 1990660
  94.0 2.8 %copy-start.4 = (bf16[3,3,192,192]{3,2,1,0:T(8,128)(2,1)S(1)}, bf16[3,3,192,192]{3,2,1,0:T(8,128)(2,1)}, u32[]{:S(2)}) copy-start(bf16[3,3,192,192]{3,2,1,0:T(8,128)(2,1)} %c2.3) | copy-start | bytes 1990660
  103.9 2.7 %collective-permute-start.8 = (bf16[3072,128]{1,0:T(8,128)(2,1)S(1)}, bf16[3072,128]{1,0:T(8,128)(2,1)S(1)}, u32[]{:S(2)}, u32[]{:S(2)}) collective-permute-start(bf16[3072,128]{1,0:T(8,128)(2,1)S(1)} %slice.29), channel_id=1, source_target_pairs={{0,16},{16,0},{32,48},{48,32},{64,80},{80,64},{96,112},{112,96},{1... | collective-permute-start | bytes 2359304 | tf_op jit(solution)/shard_map/ppermute | solution.py:550
  151.8 4.8 %collective-permute-start.9 = (bf16[3072,128]{1,0:T(8,128)(2,1)S(1)}, bf16[3072,128]{1,0:T(8,128)(2,1)S(1)}, u32[]{:S(2)}, u32[]{:S(2)}) collective-permute-start(bf16[3072,128]{1,0:T(8,128)(2,1)S(1)} %bitcast.31), channel_id=1, source_target_pairs={{0,16},{16,0},{32,48},{48,32},{64,80},{80,64},{96,112},{112,96},{1... | collective-permute-start | bytes 2359304 | tf_op jit(solution)/shard_map/ppermute | solution.py:554

commit v3 on v2

--- a/solution.py
+++ b/solution.py
@@ -64,10 +64,13 @@
     return (word >> 16).astype(F32), ((word & 65535) - 32768).astype(F32)
 
 
-def fields_kernel(f8, north, south, ftm, fm, wl, wr, s8, sn, ss, sw, se):
+def ordered(odd, x, y):
+    return jnp.where(odd > 0, x, y), jnp.where(odd > 0, y, x)
+
+
+def fields_kernel(flags, f8, swap1, swap2, ftm, fm, out1, out2, s8, sn, ss, sw, se):
     s8[...] = f8[...].astype(F32)
-    sn[...] = north[...].astype(F32)
-    ss[...] = south[...].astype(F32)
+    sn[...], ss[...] = ordered(flags[4], swap1[...].astype(F32), swap2[...].astype(F32))
     sw[...] = jnp.zeros_like(sw)
     se[...] = jnp.zeros_like(se)
     for r in range(12):
@@ -82,19 +85,20 @@
         ftm[r * 128 : r * 128 + 128, :] = turned.astype(BF)
         sw[2 * r : 2 * r + 2, :] = turned[0:2]
         se[2 * r : 2 * r + 2, :] = turned[126:128]
-    wl[...] = sw[...].astype(BF)
-    wr[...] = se[...].astype(BF)
-
-
-def turn_field_kernel(gf, north, south, et, wl, wr):
-    turned = jnp.concatenate([north[...], gf[...], south[...]], 0).T
+    one, two = ordered(flags[5], sw[...], se[...])
+    out1[...] = one.astype(BF)
+    out2[...] = two.astype(BF)
+
+
+def turn_field_kernel(flags, gf, swap1, swap2, et, out1, out2):
+    north, south = ordered(flags[4], swap1[...], swap2[...])
+    turned = jnp.concatenate([north, gf[...], south], 0).T
     et[...] = turned
-    wl[...] = turned[0:2]
-    wr[...] = turned[126:128]
+    out1[...], out2[...] = ordered(flags[5], turned[0:2], turned[126:128])
 
 
 def forward_kernel(
-    flags, ftm, wl, wr, small, c1, c2, cells, wts, cnt, out, a1_out, gp, h2c, hs, xcat, as_, acat,
+    flags, ftm, swap1, swap2, small, c1, c2, cells, wts, cnt, out, a1_out, gp, h2c, hs, xcat, as_, acat,
     w1, w2, fq, pf,
 ):
     zero8 = jnp.zeros((8, CP), F32)
@@ -105,7 +109,9 @@
     stack_weights(w1, c1, 1)
     stack_weights(w2, c2, 1)
     main = dot(ftm[...], small[0:64, :])
-    west, east = dot(wl[...], small[0:64, :]), dot(wr[...], small[0:64, :])
+    west, east = ordered(
+        flags[5], dot(swap1[...], small[0:64, :]), dot(swap2[...], small[0:64, :])
+    )
     for r in range(12):
         at = 8 + r * ROW
         hs[at + 128 : at + ROW, :] = jnp.zeros((ROW - 128, CP), F32)
@@ -181,9 +187,9 @@
     out[...] = pf[...].astype(BF)
 
 
-def turn_kernel(a1, ftm, wl, wr, small, a1t, h0t, wide, thin, pa, pt):
+def turn_kernel(flags, a1, ftm, swap1, swap2, small, a1t, h0t, wide, thin, pa, pt):
     wide[...] = a1[...].astype(F32)
-    west, east = wl[...].astype(F32), wr[...].astype(F32)
+    west, east = ordered(flags[5], swap1[...].astype(F32), swap2[...].astype(F32))
     for r in range(12):
         at = r * ROW
         thin[at : at + 2, :] = west[2 * r : 2 * r + 2]
@@ -210,18 +216,33 @@
     return [(base + 16 * m).astype(F32).astype(BF) for m in range(count)]
 
 
-def owner_kernel(recv, obs, target, pred, loss, out, left, right, total, rq, gf):
+def overlapped(count, build, multiply):
+    build(0, 0)
+
+    def step(i, carry):
+        build(2 * i + 1, 1)
+        multiply(0)
+        build(jnp.minimum(2 * i + 2, count - 1), 0)
+        multiply(1)
+        return carry
+
+    lax.fori_loop(0, count // 2, step, 0)
+
+
+def owner_kernel(recv, obs, target, pred, loss, out, l0, l1, r0, r1, total, rq, gf):
     steps = iotas(8)
     none = jnp.zeros((16, 128), BF)
     one = jnp.ones((16, 128), BF)
-
-    def collect(tb, carry):
+    lefts, rights = (l0, l1), (r0, r1)
+
+    def collect(tb, slot):
+        left, right = lefts[slot], rights[slot]
         block = recv[pl.ds(pl.multiple_of(tb * 64, 64), 64), :].astype(F32)
         index = obs[pl.ds(pl.multiple_of(tb * 8, 8), 8), :]
         low = (index & 127).astype(F32)
         high = (index >> 7).astype(F32)
         for i in range(8):
-            at = pl.ds(pl.multiple_of(tb * 1024 + i * 128, 128), 128)
+            at = slice(i * 128, i * 128 + 128)
             here = spread_row(high[i : i + 1]) == steps[0]
             for v in range(6):
                 value = spread_row(block[i * 8 + v : i * 8 + v + 1])
@@ -229,10 +250,12 @@
             mine = spread_row(low[i : i + 1])
             for m in range(8):
                 right[m * 16 : m * 16 + 16, at] = jnp.where(mine == steps[m], one, none)
-        return carry
-
-    lax.fori_loop(0, 16, collect, 0)
-    total[...] = dot(left[...], right[...], NT)
+
+    def multiply(slot):
+        total[...] += dot(lefts[slot][...], rights[slot][...], NT)
+
+    total[...] = jnp.zeros_like(total)
+    overlapped(16, collect, multiply)
     scale = 1.0 / (6 * 2048)
     squares = jnp.zeros((6, 128), F32)
     resids = []
@@ -272,13 +295,17 @@
     out[...] = gf[...].astype(BF)
 
 
-def spread_kernel(grad, cells, wts, cnt, out, left, right, total):
+def spread_kernel(
+    flags, grad, cells, wts, cnt, out, out1, out2, l0, l1, r0, r1, total
+):
+    lefts, rights = (l0, l1), (r0, r1)
     steps = iotas(4)
     none = jnp.zeros((16, 128), BF)
     total[...] = jnp.zeros_like(total)
     lane = lax.broadcasted_iota(I32, (8, 128), 1)
 
-    def owners(ob, carry):
+    def owners(ob, slot):
+        left, right = lefts[slot], rights[slot]
         rows = pl.ds(pl.multiple_of(ob * 8, 8), 8)
         live = lane < cnt[rows, 0:1]
         block = grad[pl.ds(pl.multiple_of(ob * 64, 64), 64), :].astype(F32)
@@ -297,20 +324,22 @@
                 amount = spread_row(weight[k][i : i + 1])
                 for m in range(4):
                     right[m * 16 : m * 16 + 16, at] = jnp.where(mine == steps[m], amount, none)
-        total[...] += dot(left[...], right[...], NT)
-        return carry
-
-    lax.fori_loop(0, 16, owners, 0)
+
+    def multiply(slot):
+        total[...] += dot(lefts[slot][...], rights[slot][...], NT)
+
+    overlapped(16, owners, multiply)
     out[...] = jnp.zeros_like(out)
     for r in range(8):
         even = total[pl.ds(2 * r, 6, stride=16), :]
         odd = total[pl.ds(2 * r + 1, 6, stride=16), :]
         out[r * 8 : r * 8 + 6, :] = jnp.concatenate([even, odd], 1)
+    out1[...], out2[...] = ordered(flags[4], out[0:16, :], out[48:64, :])
 
 
 def backward_kernel(
-    core, gf, et, gl, gr, fm, a1t, h0t, gp, h2c, c2, c1, small, loss, pay, gfields, es, bw, gs,
-    g2cat, zs, gzcat, w2, w1, gc,
+    flags, gf, et, swap1, swap2, fm, a1t, h0t, gp, h2c, c2, c1, small, loss, pay, gfields, es, bw,
+    gs, g2cat, zs, gzcat, gc, w2, w1,
 ):
     zero8 = jnp.zeros((8, CP), F32)
     gs[0:8, :] = zero8
@@ -319,8 +348,9 @@
     zs[N10 + 8 : N10 + 16, :] = zero8
     stack_weights(w2, c2, -1)
     stack_weights(w1, c1, -1)
-    base_s = pl.multiple_of(core[0] * HALF, 16)
-    base_f = pl.multiple_of((1 - core[0]) * HALF, 16)
+    core = (flags[4] > 0).astype(I32)
+    base_s = pl.multiple_of(core * HALF, 16)
+    base_f = pl.multiple_of((1 - core) * HALF, 16)
 
     def put(base, at, value):
         pay[pl.ds(pl.multiple_of(base + at, 16), value.shape[0]), :] = value.astype(BF)
@@ -337,8 +367,7 @@
 
     es[...] = jnp.zeros_like(es)
     es[2:130, 0:96] = et[...]
-    es[0:2, 0:96] = gl[...]
-    es[130:132, 0:96] = gr[...]
+    es[0:2, 0:96], es[130:132, 0:96] = ordered(flags[5], swap1[...], swap2[...])
     bw[...] = jnp.zeros_like(bw)
     for r in range(12):
         at, block = (r // 2) * 16, small[64 + 16 * (r % 2) : 80 + 16 * (r % 2), :]
@@ -392,7 +421,7 @@
     put(base_f, EXTRA + 32, jnp.zeros((HALF - EXTRA - 32, 128), F32))
 
 
-def unpack_kernel(core, mine, other, second, first, g_in, g_out, loss):
+def unpack_kernel(flags, mine, other, second, first, g_in, g_out, loss):
     def unpack(source, kernel):
         for tap in range(9):
             a, b = tap // 3, tap % 3
@@ -413,20 +442,21 @@
         g_out[:, 128:256] = extra[8:16]
         loss[...] = extra[16:24]
 
-    @pl.when(core[0] == 0)
+    @pl.when(flags[4] == 0)
     def _():
         both(mine, other)
 
-    @pl.when(core[0] == 1)
+    @pl.when(flags[4] > 0)
     def _():
         both(other, mine)
 
 
-def shift_pair(last, first, axis):
+def swaps(one, two, axis):
     count = lax.axis_size(axis)
-    up = [(i, i + 1) for i in range(count - 1)]
-    down = [(j, i) for i, j in up]
-    return lax.ppermute(last, axis, up), lax.ppermute(first, axis, down)
+    pairs = [[(i, i + 1) for i in range(start, count - 1, 2)] for start in range(2)]
+    return tuple(
+        lax.ppermute(x, axis, p + [(j, i) for i, j in p]) for x, p in zip((one, two), pairs)
+    )
 
 
 def exchange(rows, groups=None):
@@ -464,8 +494,9 @@
 ):
     ns, ew = lax.axis_index("ns"), lax.axis_index("ew")
     n_ns, n_ew = lax.axis_size("ns"), lax.axis_size("ew")
-    flags = jnp.stack([ns > 0, ns < n_ns - 1, ew > 0, ew < n_ew - 1]).astype(F32)
-    core = (ns % 2).astype(I32).reshape(1)
+    flags = jnp.stack(
+        [ns > 0, ns < n_ns - 1, ew > 0, ew < n_ew - 1, (ns & 1) > 0, (ew & 1) > 0]
+    ).astype(F32)
     cells = slot_cells.reshape(4, 128, CAP)
     wts = slot_weights.reshape(4, 128, CAP)
     cnt = slot_count.reshape(128, 1)
@@ -476,17 +507,16 @@
     )
     small = jnp.pad(small, ((0, 0), (0, CP - C)))
 
-    north, south = shift_pair(
-        fields[:, 6:8].reshape(128, 128), fields[:, 0:2].reshape(128, 128), "ns"
-    )
-    ftm, fm, first, last = call(
+    last, first = fields[:, 6:8].reshape(128, 128), fields[:, 0:2].reshape(128, 128)
+    one, two = swaps(*ordered(ns & 1, first, last), "ns")
+    ftm, fm, one, two = call(
         fields_kernel,
         [((12 * 128, 64), BF), ((64, 1024), BF), ((32, 64), BF), ((32, 64), BF)],
         [((512, 128), F32), ((128, 128), F32), ((128, 128), F32), ((32, 64), F32), ((32, 64), F32)],
-        fields.reshape(512, 128), north, south,
-        vmem=8,
-    )
-    west, east = shift_pair(last, first, "ew")
+        flags, fields.reshape(512, 128), one, two,
+        smem=1, vmem=8,
+    )
+    west, east = swaps(one, two, "ew")
     sent, a1, gp, h2c = call(
         forward_kernel,
         [((1024, 128), BF), ((N10, CP), BF), ((N10, CP), BF), ((1024, CP), BF)],
@@ -503,49 +533,51 @@
         turn_kernel,
         [((3 * C, 1280), BF), ((3 * C, 1280), BF)],
         [((N10, CP), F32), ((N12, 64), F32), ((1280, CP), BF), ((1280, 64), BF)],
-        a1, ftm, west, east, small,
-        vmem=16, flops=10**9,
+        flags, a1, ftm, west, east, small,
+        smem=1, vmem=16, flops=10**9,
     )
     pred, loss, back = call(
         owner_kernel,
         [((6, 2048), F32), ((16, 128), F32), ((1024, 128), BF)],
         [
-            ((96, 16384), BF), ((128, 16384), BF), ((96, 128), F32), ((128, 128), I32),
-            ((1024, 128), F32),
+            ((96, 1024), BF), ((96, 1024), BF), ((128, 1024), BF), ((128, 1024), BF),
+            ((96, 128), F32), ((128, 128), I32), ((1024, 128), F32),
         ],
         received, obs, targets,
-        vmem=16, flops=10**9,
+        vmem=8, flops=10**9,
     )
     grads = exchange(back)
-    (g_field,) = call(
+    g_field, one, two = call(
         spread_kernel,
-        [((64, 128), F32)],
-        [((96, 4096), BF), ((64, 4096), BF), ((96, 64), F32)],
-        grads, cells, wts, cnt,
-        vmem=12, flops=10**9,
-    )
-    north, south = shift_pair(g_field[48:64], g_field[0:16], "ns")
-    et, first, last = call(
+        [((64, 128), F32), ((16, 128), F32), ((16, 128), F32)],
+        [
+            ((96, 4096), BF), ((96, 4096), BF), ((64, 4096), BF), ((64, 4096), BF),
+            ((96, 64), F32),
+        ],
+        flags, grads, cells, wts, cnt,
+        smem=1, vmem=12, flops=10**9,
+    )
+    one, two = swaps(one, two, "ns")
+    et, one, two = call(
         turn_field_kernel,
         [((128, 96), F32), ((2, 96), F32), ((2, 96), F32)],
         [],
-        g_field, north, south,
-        vmem=4,
-    )
-    g_west, g_east = shift_pair(last, first, "ew")
+        flags, g_field, one, two,
+        smem=1, vmem=4,
+    )
+    one, two = swaps(one, two, "ew")
     pay, g_fields = call(
         backward_kernel,
         [((2 * HALF, 128), BF), ((512, 128), F32)],
         [
             ((ROW, 128), F32), ((CP, 12 * CP), BF), ((N12 + 16, CP), F32), ((N12, 3 * CP), BF),
-            ((N10 + 16, CP), F32), ((N10, 3 * CP), BF), ((3, CP, 3 * CP), BF),
-            ((3, CP, 3 * CP), BF), ((1024, CP), BF),
+            ((N10 + 16, CP), F32), ((N10, 3 * CP), BF), ((1024, CP), BF),
+            ((3, CP, 3 * CP), BF), ((3, CP, 3 * CP), BF),
         ],
-        core, g_field, et, g_west, g_east, fm, a1t, h0t, gp, h2c, conv_second, conv_first, small,
-        loss,
+        flags, g_field, et, one, two, fm, a1t, h0t, gp, h2c, conv_second, conv_first, small, loss,
         smem=1, vmem=28, flops=2 * 10**9,
     )
-    pairs = [(n, n + 1 - 2 * (n % 2)) for n in range(n_ns)]
+    pairs = [(n, n ^ 1) for n in range(n_ns)]
     groups = [[n * n_ew + e for n in range(c, n_ns, 2) for e in range(n_ew)] for c in range(2)]
     theirs = lax.ppermute(pay[HALF:], "ns", pairs)
     summed = (pay[:HALF].astype(F32) + theirs.astype(F32)).astype(BF).reshape(64, PIECE, 128)
@@ -556,7 +588,7 @@
         unpack_kernel,
         [((3, 3, C, C), F32), ((3, 3, C, C), F32), ((64, C), F32), ((8, CP), F32), ((8, 128), F32)],
         [],
-        core, mine, other,
+        flags, mine, other,
         smem=1, vmem=16,
     )
     return (

time: 160 us -> 151 us (0.944)
  starting transfers between devices: 23.8 us -> 13.6 us
  Pallas kernels: 33.8 us -> 35.6 us
    ppermute x8, starting transfers between devices: 20.2 us -> 10.7 us  [swaps(): lax.ppermute(x, axis, p + [(j, i) for i, j in p])]
    pallas_call x8, Pallas kernels: 33.8 us -> 35.6 us  [call(): pl.pallas_call(kernel, out_shape=[jax.ShapeDtypeStruct(s, d) for s, d in...]
  transfers between devices with their start and end apart: 10 -> 10, of which waited for: 6 -> 4; matrix products, arithmetic and copies ran while one was open for 2% -> 2% of each run, Pallas kernels for 1% -> 1%
where the time goes in v3:
time: 151 us; the launch traced here: 150 us
  blocking collectives  81.8 us (54%)
  Pallas kernels  35.6 us (24%)
  starting transfers between devices  13.6 us (9%)
  waiting for transfers between devices  8.98 us (6%)
  local copies, waits for them, and re-layouts  7.34 us (5%)
  other arithmetic  2.22 us (1%)
    all_to_all x4, blocking collectives, exchange(): lax.all_to_all(rows, AXES, split_axis=0, concat_axis=0, tiled=True, axis_...  81.8 us
    pallas_call x8, Pallas kernels, call(): pl.pallas_call(kernel, out_shape=[jax.ShapeDtypeStruct(s, d) for s, d in...  35.6 us
    ppermute x8, starting transfers between devices, swaps(): lax.ppermute(x, axis, p + [(j, i) for i, j in p])  10.7 us
    unnamed x16, local copies, waits for them, and re-layouts  5.19 us
    ppermute x8, waiting for transfers between devices, swaps(): lax.ppermute(x, axis, p + [(j, i) for i, j in p])  4.8 us
  transfers between devices with their start and end apart: 10, of which 4 were waited for; matrix products, arithmetic and copies ran while one was open for 2% of the time, Pallas kernels for 1%

profile of v3, /device:TPU:1, one launch (start us, length us, event | category | flops | bytes accessed | tf_op | source)
XLA Modules:
  0.0 150.5 jit_solution(17324595967901991182)
XLA Ops:
  0.6 1.1 broadcast_select_fusion
  1.7 1.5 collective-permute-start
  3.2 3.2 %collective-permute-start.1 = (bf16[128,128]{1,0:T(8,128)(2,1)S(1)}, bf16[128,128]{1,0:T(8,128)(2,1)S(1)}, u32[]{:S(2)}, u32[]{:S(2)}) collective-permute-start(bf16[128,128]{1,0:T(8,128)(2,1)S(1)} %bitcast.47), channel_id=1, source_target_pairs={{16,32},{48,64},{80,96},{32,16},{64,48},{96,80},{17,33},{49,65},{8... | collective-permute-start | bytes 98312 | tf_op jit(solution)/shard_map/ppermute | solution.py:458
  6.5 1.9 %collective-permute-done.1.swap2 = bf16[128,128]{1,0:T(8,128)(2,1)S(1)} collective-permute-done((bf16[128,128]{1,0:T(8,128)(2,1)S(1)}, bf16[128,128]{1,0:T(8,128)(2,1)S(1)}, u32[]{:S(2)}, u32[]{:S(2)}) %collective-permute-start.1) | collective-permute-done | bytes 32800 | tf_op jit(solution)/shard_map/ppermute | solution.py:458
  8.4 0.9 copy-done
  9.3 0.8 shard_map.153
  10.1 1.4 collective-permute-start.2
  11.5 0.6 collective-permute-start.3
  12.2 0.8 fusion.4
  13.0 0.8 copy.17.cnt
  13.8 1.0 copy.24
  14.7 1.0 copy.23
  15.7 1.2 copy-done.1
  16.9 1.2 copy-done.3
  18.1 8.2 %shard_map.154 = (bf16[1024,128]{1,0:T(8,128)(2,1)S(1)}, bf16[1440,256]{1,0:T(8,128)(2,1)S(1)}, bf16[1440,256]{1,0:T(8,128)(2,1)S(1)}, bf16[1024,256]{1,0:T(8,128)(2,1)S(1)}) custom-call(f32[6]{0:T(128)S(1)} %convert_element_type.20.flags, bf16[1536,64]{1,0:T(8,128)(2,1)S(1)} %get-tuple-element.33.ftm, bf16[32,64]{1,0:T(8,128)(2,1)S(1)} %collective-permute-done.2.swap1, ...), custom_call_target="tpu_custom_call" | custom-call | flops 2000000000 | bytes 4000000 | tf_op jit(solution)/shard_map/pallas_call | solution.py:472
  26.3 23.9 %all_to_all.32 = bf16[128,8,128]{2,1,0:T(8,128)(2,1)S(1)} all-to-all(bf16[128,8,128]{2,1,0:T(8,128)(2,1)S(1)} %bitcast.40), channel_id=1, replica_groups=mesh['ns'=8,'ew'=16] {'ns','ew'}, dimensions={0} | all-to-all | bytes 524288 | tf_op jit(solution)/shard_map/all_to_all | solution.py:463
  50.3 5.9 %shard_map.155 = (f32[6,2048]{1,0:T(8,128)}, f32[16,128]{1,0:T(8,128)S(1)}, bf16[1024,128]{1,0:T(8,128)(2,1)S(1)}) custom-call(bf16[1024,128]{1,0:T(8,128)(2,1)S(1)} %bitcast.41, s32[128,128]{1,0:T(8,128)S(1)} %bitcast.43, f32[6,2048]{1,0:T(8,128)S(1)} %copy-done.6), custom_call_target="tpu_custom_call" | custom-call | flops 1000000000 | bytes 4000000 | tf_op jit(solution)/shard_map/pallas_call | solution.py:472
  56.2 15.3 %all_to_all.33 = bf16[128,8,128]{2,1,0:T(8,128)(2,1)S(1)} all-to-all(bf16[128,8,128]{2,1,0:T(8,128)(2,1)S(1)} %bitcast.42), channel_id=1, replica_groups=mesh['ns'=8,'ew'=16] {'ns','ew'}, dimensions={0} | all-to-all | bytes 524288 | tf_op jit(solution)/shard_map/all_to_all | solution.py:463
  71.4 7.8 %shard_map.156 = (f32[64,128]{1,0:T(8,128)S(1)}, f32[16,128]{1,0:T(8,128)S(1)}, f32[16,128]{1,0:T(8,128)S(1)}) custom-call(f32[6]{0:T(128)S(1)} %convert_element_type.20.flags, bf16[1024,128]{1,0:T(8,128)(2,1)S(1)} %bitcast.39, s32[4,128,128]{2,1,0:T(8,128)S(1)} %bitcast.36, f32[4,128,128]{2,1,0:T(8,128)S(1)} %bitcast.38, s32[128,1]{1,0:T(8,128)S(1)} %copy.17.cnt), custom_call_target="tpu_custom_call" | custom-call | flops 1000000000 | bytes 4000000 | tf_op jit(solution)/shard_map/pallas_call | solution.py:472
  79.8 2.2 %collective-permute-start.5 = (f32[16,128]{1,0:T(8,128)S(1)}, f32[16,128]{1,0:T(8,128)S(1)}, u32[]{:S(2)}, u32[]{:S(2)}) collective-permute-start(f32[16,128]{1,0:T(8,128)S(1)} %get-tuple-element.41), channel_id=1, source_target_pairs={{16,32},{48,64},{80,96},{32,16},{64,48},{96,80},{17,33},{49,65},{8... | collective-permute-start | bytes 24584 | tf_op jit(solution)/shard_map/ppermute | solution.py:458
  82.0 2.9 %collective-permute-done.5.swap2 = f32[16,128]{1,0:T(8,128)S(1)} collective-permute-done((f32[16,128]{1,0:T(8,128)S(1)}, f32[16,128]{1,0:T(8,128)S(1)}, u32[]{:S(2)}, u32[]{:S(2)}) %collective-permute-start.5) | collective-permute-done | bytes 8224 | tf_op jit(solution)/shard_map/ppermute | solution.py:458
  84.9 0.6 shard_map.157
  85.9 0.8 collective-permute-start.7
  86.8 2.1 %shard_map.158 = (bf16[576,1280]{1,0:T(8,128)(2,1)S(1)}, bf16[576,1280]{1,0:T(8,128)(2,1)S(1)}) custom-call(f32[6]{0:T(128)S(1)} %convert_element_type.20.flags, bf16[1440,256]{1,0:T(8,128)(2,1)S(1)} %get-tuple-element.46.a1, bf16[1536,64]{1,0:T(8,128)(2,1)S(1)} %get-tuple-element.33.ftm, bf16[32,64]{1,0:T(8,128)(2,1)S(1)} %collective-permute-done.2.swap1, ...), custom_call_target="tpu_custom_call" | custom-call | flops 1000000000 | bytes 4000000 | tf_op jit(solution)/shard_map/pallas_call | solution.py:472
  88.9 7.5 %shard_map.159 = (bf16[6144,128]{1,0:T(8,128)(2,1)S(1)}, f32[512,128]{1,0:T(8,128)}) custom-call(f32[6]{0:T(128)S(1)} %convert_element_type.20.flags, f32[64,128]{1,0:T(8,128)S(1)} %get-tuple-element.39.gf, f32[128,96]{1,0:T(8,128)S(1)} %get-tuple-element.42.et, f32[2,96]{1,0:T(2,128)S(1)} %collective-permute-done.6.swap1, ...), custom_call_target="tpu_custom_call" | custom-call | flops 2000000000 | bytes 4000000 | tf_op jit(solution)/shard_map/pallas_call | solution.py:472
  96.6 2.3 %collective-permute-done.8 = bf16[3072,128]{1,0:T(8,128)(2,1)S(1)} collective-permute-done((bf16[3072,128]{1,0:T(8,128)(2,1)S(1)}, bf16[3072,128]{1,0:T(8,128)(2,1)S(1)}, u32[]{:S(2)}, u32[]{:S(2)}) %collective-permute-start.8) | collective-permute-done | bytes 786464 | tf_op jit(solution)/shard_map/ppermute | solution.py:582
  99.1 24.0 %all_to_all.34 = bf16[64,48,128]{2,1,0:T(8,128)(2,1)S(1)} all-to-all(bf16[64,48,128]{2,1,0:T(8,128)(2,1)S(1)} %bitcast.44), channel_id=1, replica_groups={{0,1,2,3,4,5,6,7,8,9,10,11,12,13,14,15,32,33,34,35,36,37,38,39,40,41,42..., dimensions={0} | all-to-all | bytes 1572864 | tf_op jit(solution)/shard_map/all_to_all | solution.py:463
  123.4 18.6 %all_to_all.35 = bf16[64,48,128]{2,1,0:T(8,128)(2,1)S(1)} all-to-all(bf16[64,48,128]{2,1,0:T(8,128)(2,1)S(1)} %broadcast_in_dim.2), channel_id=1, replica_groups={{0,1,2,3,4,5,6,7,8,9,10,11,12,13,14,15,32,33,34,35,36,37,38,39,40,41,42..., dimensions={0} | all-to-all | bytes 1572864 | tf_op jit(solution)/shard_map/all_to_all | solution.py:463
  142.0 2.9 %collective-permute-start.9 = (bf16[3072,128]{1,0:T(8,128)(2,1)S(1)}, bf16[3072,128]{1,0:T(8,128)(2,1)S(1)}, u32[]{:S(2)}, u32[]{:S(2)}) collective-permute-start(bf16[3072,128]{1,0:T(8,128)(2,1)S(1)} %bitcast.32), channel_id=1, source_target_pairs={{0,16},{16,0},{32,48},{48,32},{64,80},{80,64},{96,112},{112,96},{1... | collective-permute-start | bytes 2359304 | tf_op jit(solution)/shard_map/ppermute | solution.py:586
  144.8 1.9 %collective-permute-done.9.other = bf16[3072,128]{1,0:T(8,128)(2,1)S(1)} collective-permute-done((bf16[3072,128]{1,0:T(8,128)(2,1)S(1)}, bf16[3072,128]{1,0:T(8,128)(2,1)S(1)}, u32[]{:S(2)}, u32[]{:S(2)}) %collective-permute-start.9) | collective-permute-done | bytes 786464 | tf_op jit(solution)/shard_map/ppermute | solution.py:586
  146.7 2.6 %shard_map.160 = (f32[3,3,192,192]{3,2,1,0:T(8,128)}, f32[3,3,192,192]{3,2,1,0:T(8,128)}, f32[64,192]{1,0:T(8,128)}, f32[8,256]{1,0:T(8,128)S(1)}, f32[8,128]{1,0:T(8,128)S(1)}) custom-call(f32[6]{0:T(128)S(1)} %convert_element_type.20.flags, bf16[3072,128]{1,0:T(8,128)(2,1)S(1)} %bitcast.33, bf16[3072,128]{1,0:T(8,128)(2,1)S(1)} %collective-permute-done.9.other), custom_call_target="tpu_custom_call" | custom-call | bytes 4000000 | tf_op jit(solution)/shard_map/pallas_call | solution.py:472
  149.9 0.6 slice_bitcast_fusion
  (28 shorter events, 2.2 us)
Async XLA Ops:
  1.7 4.8 %collective-permute-start = (bf16[128,128]{1,0:T(8,128)(2,1)S(1)}, bf16[128,128]{1,0:T(8,128)(2,1)S(1)}, u32[]{:S(2)}, u32[]{:S(2)}) collective-permute-start(bf16[128,128]{1,0:T(8,128)(2,1)S(1)} %bitcast.48), channel_id=1, source_target_pairs={{0,16},{32,48},{64,80},{96,112},{16,0},{48,32},{80,64},{112,96},{1... | collective-permute-start | bytes 98312 | tf_op jit(solution)/shard_map/ppermute | solution.py:458
  3.2 5.2 %collective-permute-start.1 = (bf16[128,128]{1,0:T(8,128)(2,1)S(1)}, bf16[128,128]{1,0:T(8,128)(2,1)S(1)}, u32[]{:S(2)}, u32[]{:S(2)}) collective-permute-start(bf16[128,128]{1,0:T(8,128)(2,1)S(1)} %bitcast.47), channel_id=1, source_target_pairs={{16,32},{48,64},{80,96},{32,16},{64,48},{96,80},{17,33},{49,65},{8... | collective-permute-start | bytes 98312 | tf_op jit(solution)/shard_map/ppermute | solution.py:458
  8.4 0.9 copy-start
  10.1 5.6 %collective-permute-start.2 = (bf16[32,64]{1,0:T(8,128)(2,1)S(1)}, bf16[32,64]{1,0:T(8,128)(2,1)S(1)}, u32[]{:S(2)}, u32[]{:S(2)}) collective-permute-start(bf16[32,64]{1,0:T(8,128)(2,1)S(1)} %get-tuple-element.34), channel_id=1, source_target_pairs={{0,1},{2,3},{4,5},{6,7},{8,9},{10,11},{12,13},{14,15},{1,0},{3,2},... | collective-permute-start | bytes 12296 | tf_op jit(solution)/shard_map/ppermute | solution.py:458
  11.5 4.2 %collective-permute-start.3 = (bf16[32,64]{1,0:T(8,128)(2,1)S(1)}, bf16[32,64]{1,0:T(8,128)(2,1)S(1)}, u32[]{:S(2)}, u32[]{:S(2)}) collective-permute-start(bf16[32,64]{1,0:T(8,128)(2,1)S(1)} %get-tuple-element.35), channel_id=1, source_target_pairs={{1,2},{3,4},{5,6},{7,8},{9,10},{11,12},{13,14},{2,1},{4,3},{6,5},{... | collective-permute-start | bytes 12296 | tf_op jit(solution)/shard_map/ppermute | solution.py:458
  15.7 1.2 copy-start.1
  16.9 1.2 copy-start.3
  18.1 32.2 %copy-start.5 = (s32[1,16384]{1,0:T(1,128)S(1)}, s32[1,16384]{1,0:T(1,128)}, u32[]{:S(2)}) copy-start(s32[1,16384]{1,0:T(1,128)} %param.18) | copy-start | bytes 196612
  18.1 32.2 %copy-start.6 = (f32[6,2048]{1,0:T(8,128)S(1)}, f32[6,2048]{1,0:T(8,128)}, u32[]{:S(2)}) copy-start(f32[6,2048]{1,0:T(8,128)} %target.1) | copy-start | bytes 147460
  79.2 2.7 %collective-permute-start.4 = (f32[16,128]{1,0:T(8,128)S(1)}, f32[16,128]{1,0:T(8,128)S(1)}, u32[]{:S(2)}, u32[]{:S(2)}) collective-permute-start(f32[16,128]{1,0:T(8,128)S(1)} %get-tuple-element.40), channel_id=1, source_target_pairs={{0,16},{32,48},{64,80},{96,112},{16,0},{48,32},{80,64},{112,96},{1... | collective-permute-start | bytes 24584 | tf_op jit(solution)/shard_map/ppermute | solution.py:458
  79.8 5.1 %collective-permute-start.5 = (f32[16,128]{1,0:T(8,128)S(1)}, f32[16,128]{1,0:T(8,128)S(1)}, u32[]{:S(2)}, u32[]{:S(2)}) collective-permute-start(f32[16,128]{1,0:T(8,128)S(1)} %get-tuple-element.41), channel_id=1, source_target_pairs={{16,32},{48,64},{80,96},{32,16},{64,48},{96,80},{17,33},{49,65},{8... | collective-permute-start | bytes 24584 | tf_op jit(solution)/shard_map/ppermute | solution.py:458
  85.5 3.4 %collective-permute-start.6 = (f32[2,96]{1,0:T(2,128)S(1)}, f32[2,96]{1,0:T(2,128)S(1)}, u32[]{:S(2)}, u32[]{:S(2)}) collective-permute-start(f32[2,96]{1,0:T(2,128)S(1)} %get-tuple-element.43), channel_id=1, source_target_pairs={{0,1},{2,3},{4,5},{6,7},{8,9},{10,11},{12,13},{14,15},{1,0},{3,2},... | collective-permute-start | bytes 2312 | tf_op jit(solution)/shard_map/ppermute | solution.py:458
  85.9 3.0 %collective-permute-start.7 = (f32[2,96]{1,0:T(2,128)S(1)}, f32[2,96]{1,0:T(2,128)S(1)}, u32[]{:S(2)}, u32[]{:S(2)}) collective-permute-start(f32[2,96]{1,0:T(2,128)S(1)} %get-tuple-element.44), channel_id=1, source_target_pairs={{1,2},{3,4},{5,6},{7,8},{9,10},{11,12},{13,14},{2,1},{4,3},{6,5},{... | collective-permute-start | bytes 2312 | tf_op jit(solution)/shard_map/ppermute | solution.py:458
  86.8 2.1 %copy-start.2 = (bf16[3,3,192,192]{3,2,1,0:T(8,128)(2,1)S(1)}, bf16[3,3,192,192]{3,2,1,0:T(8,128)(2,1)}, u32[]{:S(2)}) copy-start(bf16[3,3,192,192]{3,2,1,0:T(8,128)(2,1)} %c1.3) | copy-start | bytes 1990660
  86.8 2.1 %copy-start.4 = (bf16[3,3,192,192]{3,2,1,0:T(8,128)(2,1)S(1)}, bf16[3,3,192,192]{3,2,1,0:T(8,128)(2,1)}, u32[]{:S(2)}) copy-start(bf16[3,3,192,192]{3,2,1,0:T(8,128)(2,1)} %c2.3) | copy-start | bytes 1990660
  96.5 2.4 %collective-permute-start.8 = (bf16[3072,128]{1,0:T(8,128)(2,1)S(1)}, bf16[3072,128]{1,0:T(8,128)(2,1)S(1)}, u32[]{:S(2)}, u32[]{:S(2)}) collective-permute-start(bf16[3072,128]{1,0:T(8,128)(2,1)S(1)} %slice.21), channel_id=1, source_target_pairs={{0,16},{16,0},{32,48},{48,32},{64,80},{80,64},{96,112},{112,96},{1... | collective-permute-start | bytes 2359304 | tf_op jit(solution)/shard_map/ppermute | solution.py:582
  142.0 4.8 %collective-permute-start.9 = (bf16[3072,128]{1,0:T(8,128)(2,1)S(1)}, bf16[3072,128]{1,0:T(8,128)(2,1)S(1)}, u32[]{:S(2)}, u32[]{:S(2)}) collective-permute-start(bf16[3072,128]{1,0:T(8,128)(2,1)S(1)} %bitcast.32), channel_id=1, source_target_pairs={{0,16},{16,0},{32,48},{48,32},{64,80},{80,64},{96,112},{112,96},{1... | collective-permute-start | bytes 2359304 | tf_op jit(solution)/shard_map/ppermute | solution.py:586

commit v4 on v3

--- a/solution.py
+++ b/solution.py
@@ -19,6 +19,7 @@
 HALF = 64 * PIECE
 REST = 1728
 EXTRA = 2592
+LONG = 2 * 10**10
 NT = (((1,), (1,)), ((), ()))
 TN = (((0,), (0,)), ((), ()))
 
@@ -68,21 +69,28 @@
     return jnp.where(odd > 0, x, y), jnp.where(odd > 0, y, x)
 
 
-def fields_kernel(flags, f8, swap1, swap2, ftm, fm, out1, out2, s8, sn, ss, sw, se):
+def own_kernel(f8, fto, fm, wo, eo, s8):
     s8[...] = f8[...].astype(F32)
+    for r in range(8):
+        block = s8[pl.ds(r, 64, stride=8), :]
+        fm[:, r * 128 : r * 128 + 128] = block.astype(BF)
+        turned = block.T
+        fto[r * 128 : r * 128 + 128, :] = turned.astype(BF)
+        wo[2 * r : 2 * r + 2, :] = turned[0:2]
+        eo[2 * r : 2 * r + 2, :] = turned[126:128]
+
+
+def rim_kernel(flags, swap1, swap2, wo, eo, ftr, out1, out2, sn, ss, sw, se):
     sn[...], ss[...] = ordered(flags[4], swap1[...].astype(F32), swap2[...].astype(F32))
     sw[...] = jnp.zeros_like(sw)
     se[...] = jnp.zeros_like(se)
-    for r in range(12):
-        if r < 2:
-            block = sn[pl.ds(r, 64, stride=2), :]
-        elif r < 10:
-            block = s8[pl.ds(r - 2, 64, stride=8), :]
-            fm[:, (r - 2) * 128 : (r - 1) * 128] = block.astype(BF)
-        else:
-            block = ss[pl.ds(r - 10, 64, stride=2), :]
+    sw[4:20, :] = wo[...]
+    se[4:20, :] = eo[...]
+    for i in range(4):
+        block = (sn if i < 2 else ss)[pl.ds(i % 2, 64, stride=2), :]
+        r = i if i < 2 else i + 8
         turned = block.T
-        ftm[r * 128 : r * 128 + 128, :] = turned.astype(BF)
+        ftr[i * 128 : i * 128 + 128, :] = turned.astype(BF)
         sw[2 * r : 2 * r + 2, :] = turned[0:2]
         se[2 * r : 2 * r + 2, :] = turned[126:128]
     one, two = ordered(flags[5], sw[...], se[...])
@@ -90,6 +98,13 @@
     out2[...] = two.astype(BF)
 
 
+def row_of(own, rim, r):
+    if 2 <= r < 10:
+        return own[(r - 2) * 128 : (r - 1) * 128]
+    i = r if r < 2 else r - 8
+    return rim[i * 128 : i * 128 + 128]
+
+
 def turn_field_kernel(flags, gf, swap1, swap2, et, out1, out2):
     north, south = ordered(flags[4], swap1[...], swap2[...])
     turned = jnp.concatenate([north, gf[...], south], 0).T
@@ -98,8 +113,8 @@
 
 
 def forward_kernel(
-    flags, ftm, swap1, swap2, small, c1, c2, cells, wts, cnt, out, a1_out, gp, h2c, hs, xcat, as_, acat,
-    w1, w2, fq, pf,
+    flags, fto, ftr, swap1, swap2, small, c1, c2, cells, wts, cnt, out, a1_out, gp, h2c, hs, xcat,
+    as_, acat, w1, w2, fq, pf,
 ):
     zero8 = jnp.zeros((8, CP), F32)
     hs[0:8, :] = zero8
@@ -108,7 +123,7 @@
     as_[N10 + 8 : N10 + 16, :] = zero8
     stack_weights(w1, c1, 1)
     stack_weights(w2, c2, 1)
-    main = dot(ftm[...], small[0:64, :])
+    own, rim = dot(fto[...], small[0:64, :]), dot(ftr[...], small[0:64, :])
     west, east = ordered(
         flags[5], dot(swap1[...], small[0:64, :]), dot(swap2[...], small[0:64, :])
     )
@@ -116,7 +131,7 @@
         at = 8 + r * ROW
         hs[at + 128 : at + ROW, :] = jnp.zeros((ROW - 128, CP), F32)
         hs[at : at + 2, :] = west[2 * r : 2 * r + 2]
-        hs[at + 2 : at + 130, :] = main[r * 128 : r * 128 + 128]
+        hs[at + 2 : at + 130, :] = row_of(own, rim, r)
         hs[at + 130 : at + 132, :] = east[2 * r : 2 * r + 2]
     for b in range(3):
         xcat[:, b * CP : (b + 1) * CP] = hs[7 + b : 7 + b + N12, :].astype(BF)
@@ -187,13 +202,13 @@
     out[...] = pf[...].astype(BF)
 
 
-def turn_kernel(flags, a1, ftm, swap1, swap2, small, a1t, h0t, wide, thin, pa, pt):
+def turn_kernel(flags, a1, fto, ftr, swap1, swap2, small, a1t, h0t, wide, thin, pa, pt):
     wide[...] = a1[...].astype(F32)
     west, east = ordered(flags[5], swap1[...].astype(F32), swap2[...].astype(F32))
     for r in range(12):
         at = r * ROW
         thin[at : at + 2, :] = west[2 * r : 2 * r + 2]
-        thin[at + 2 : at + 130, :] = ftm[r * 128 : r * 128 + 128, :].astype(F32)
+        thin[at + 2 : at + 130, :] = row_of(fto, ftr, r).astype(F32)
         thin[at + 130 : at + 132, :] = east[2 * r : 2 * r + 2]
     ones = lax.broadcasted_iota(I32, (CP, CP), 0) == lax.broadcasted_iota(I32, (CP, CP), 1)
     same = jnp.where(ones, 1.0, 0.0).astype(BF)
@@ -438,9 +453,9 @@
         g_in[0:32, 128:C] = rest[:, 0:64]
         g_in[32:64, 128:C] = pltpu.roll(rest, 64, 1)[:, 0:64]
         extra = f[EXTRA : EXTRA + 32, :].astype(F32)
-        g_out[:, 0:128] = extra[0:8]
-        g_out[:, 128:256] = extra[8:16]
-        loss[...] = extra[16:24]
+        g_out[:, 0:128] = extra[0:6]
+        g_out[:, 128:C] = extra[8:14, 0:64]
+        loss[0, 0] = jnp.max(extra[16:24])
 
     @pl.when(flags[4] == 0)
     def _():
@@ -465,15 +480,13 @@
     )
 
 
-def call(kernel, out_shapes, scratch, *operands, smem=0, vmem=60, flops=0):
-    specs = [pl.BlockSpec(memory_space=pltpu.SMEM)] * smem + [
-        pl.BlockSpec(memory_space=pltpu.VMEM)
-    ] * (len(operands) - smem)
+def call(kernel, out_shapes, scratch, *operands, smem=0, smem_out=0, vmem=60, flops=0):
+    vm, sm = pl.BlockSpec(memory_space=pltpu.VMEM), pl.BlockSpec(memory_space=pltpu.SMEM)
     return pl.pallas_call(
         kernel,
         out_shape=[jax.ShapeDtypeStruct(s, d) for s, d in out_shapes],
-        in_specs=specs,
-        out_specs=[pl.BlockSpec(memory_space=pltpu.VMEM)] * len(out_shapes),
+        in_specs=[sm] * smem + [vm] * (len(operands) - smem),
+        out_specs=[vm] * (len(out_shapes) - smem_out) + [sm] * smem_out,
         scratch_shapes=[pltpu.VMEM(s, d) for s, d in scratch],
         compiler_params=pltpu.CompilerParams(vmem_limit_bytes=vmem * 1024 * 1024),
         cost_estimate=pl.CostEstimate(flops=flops, bytes_accessed=4_000_000, transcendentals=0),
@@ -509,12 +522,19 @@
 
     last, first = fields[:, 6:8].reshape(128, 128), fields[:, 0:2].reshape(128, 128)
     one, two = swaps(*ordered(ns & 1, first, last), "ns")
-    ftm, fm, one, two = call(
-        fields_kernel,
-        [((12 * 128, 64), BF), ((64, 1024), BF), ((32, 64), BF), ((32, 64), BF)],
-        [((512, 128), F32), ((128, 128), F32), ((128, 128), F32), ((32, 64), F32), ((32, 64), F32)],
-        flags, fields.reshape(512, 128), one, two,
-        smem=1, vmem=8,
+    fto, fm, own_west, own_east = call(
+        own_kernel,
+        [((1024, 64), BF), ((64, 1024), BF), ((16, 64), F32), ((16, 64), F32)],
+        [((512, 128), F32)],
+        fields.reshape(512, 128),
+        vmem=8, flops=LONG,
+    )
+    ftr, one, two = call(
+        rim_kernel,
+        [((512, 64), BF), ((32, 64), BF), ((32, 64), BF)],
+        [((128, 128), F32), ((128, 128), F32), ((32, 64), F32), ((32, 64), F32)],
+        flags, one, two, own_west, own_east,
+        smem=1, vmem=8, flops=LONG,
     )
     west, east = swaps(one, two, "ew")
     sent, a1, gp, h2c = call(
@@ -525,7 +545,7 @@
             ((N10, 3 * CP), BF), ((3, 3 * CP, CP), BF), ((3, 3 * CP, CP), BF),
             ((64, 128), I32), ((1024, 128), F32),
         ],
-        flags, ftm, west, east, small, conv_first, conv_second, cells, wts, cnt,
+        flags, fto, ftr, west, east, small, conv_first, conv_second, cells, wts, cnt,
         smem=1, vmem=28, flops=2 * 10**9,
     )
     received = exchange(sent)
@@ -533,7 +553,7 @@
         turn_kernel,
         [((3 * C, 1280), BF), ((3 * C, 1280), BF)],
         [((N10, CP), F32), ((N12, 64), F32), ((1280, CP), BF), ((1280, 64), BF)],
-        flags, a1, ftm, west, east, small,
+        flags, a1, fto, ftr, west, east, small,
         smem=1, vmem=16, flops=10**9,
     )
     pred, loss, back = call(
@@ -563,7 +583,7 @@
         [((128, 96), F32), ((2, 96), F32), ((2, 96), F32)],
         [],
         flags, g_field, one, two,
-        smem=1, vmem=4,
+        smem=1, vmem=4, flops=LONG,
     )
     one, two = swaps(one, two, "ew")
     pay, g_fields = call(
@@ -586,10 +606,10 @@
     other = lax.ppermute(mine, "ns", pairs)
     grad_second, grad_first, grad_in, g_out, total = call(
         unpack_kernel,
-        [((3, 3, C, C), F32), ((3, 3, C, C), F32), ((64, C), F32), ((8, CP), F32), ((8, 128), F32)],
+        [((3, 3, C, C), F32), ((3, 3, C, C), F32), ((64, C), F32), ((6, C), F32), ((1, 1), F32)],
         [],
         flags, mine, other,
-        smem=1, vmem=16,
+        smem=1, smem_out=1, vmem=16,
     )
     return (
         pred,
@@ -597,7 +617,7 @@
         grad_first,
         grad_second,
         grad_in,
-        g_out[:6, :C].T,
+        g_out.T,
         g_fields.reshape(64, TH, TW),
     )
 

time: 151 us -> 147 us (0.974)
  local copies, waits for them, and re-layouts: 7.34 us -> 1.37 us
  blocking collectives: 81.8 us -> 84.8 us
    unnamed x16 -> x22, local copies, waits for them, and re-layouts: 5.19 us -> 0.98 us
    all_to_all x4, blocking collectives: 81.8 us -> 84.8 us  [exchange(): lax.all_to_all(rows, AXES, split_axis=0, concat_axis=0, tiled=True, axis_...]
    pallas_call x8 -> x9, Pallas kernels: 35.6 us -> 35.9 us  [call(): pl.pallas_call(kernel, out_shape=[jax.ShapeDtypeStruct(s, d) for s, d in...]
  transfers between devices with their start and end apart: 10 -> 10, of which waited for: 4 -> 5; matrix products, arithmetic and copies ran while one was open for 2% -> 0% of each run, Pallas kernels for 1% -> 2%
where the time goes in v4:
time: 147 us; the launch traced here: 146 us
  blocking collectives  84.8 us (58%)
  Pallas kernels  35.9 us (24%)
  starting transfers between devices  13.6 us (9%)
  waiting for transfers between devices  8.15 us (6%)
    all_to_all x4, blocking collectives, exchange(): lax.all_to_all(rows, AXES, split_axis=0, concat_axis=0, tiled=True, axis_...  84.8 us
    pallas_call x9, Pallas kernels, call(): pl.pallas_call(kernel, out_shape=[jax.ShapeDtypeStruct(s, d) for s, d in...  35.9 us
    ppermute x8, starting transfers between devices, swaps(): lax.ppermute(x, axis, p + [(j, i) for i, j in p])  10.7 us
    ppermute x8, waiting for transfers between devices, swaps(): lax.ppermute(x, axis, p + [(j, i) for i, j in p])  3.97 us
  transfers between devices with their start and end apart: 10, of which 5 were waited for; matrix products, arithmetic and copies ran while one was open for 0% of the time, Pallas kernels for 2%

profile of v4, /device:TPU:1, one launch (start us, length us, event | category | flops | bytes accessed | tf_op | source)
XLA Modules:
  0.0 146.3 jit_solution(3528297637985152002)
XLA Ops:
  0.6 1.1 broadcast_select_fusion
  1.7 1.5 %collective-permute-start = (bf16[128,128]{1,0:T(8,128)(2,1)S(1)}, bf16[128,128]{1,0:T(8,128)(2,1)S(1)}, u32[]{:S(2)}, u32[]{:S(2)}) collective-permute-start(bf16[128,128]{1,0:T(8,128)(2,1)S(1)} %bitcast.47), channel_id=1, source_target_pairs={{0,16},{32,48},{64,80},{96,112},{16,0},{48,32},{80,64},{112,96},{1... | collective-permute-start | bytes 98312 | tf_op jit(solution)/shard_map/ppermute | solution.py:473
  3.2 3.2 %collective-permute-start.1 = (bf16[128,128]{1,0:T(8,128)(2,1)S(1)}, bf16[128,128]{1,0:T(8,128)(2,1)S(1)}, u32[]{:S(2)}, u32[]{:S(2)}) collective-permute-start(bf16[128,128]{1,0:T(8,128)(2,1)S(1)} %bitcast.46), channel_id=1, source_target_pairs={{16,32},{48,64},{80,96},{32,16},{64,48},{96,80},{17,33},{49,65},{8... | collective-permute-start | bytes 98312 | tf_op jit(solution)/shard_map/ppermute | solution.py:473
  6.4 0.9 copy-done
  7.3 0.2 shard_map.153
  7.7 0.8 collective-permute-done.1.swap2
  8.5 0.7 shard_map.154
  9.1 1.4 collective-permute-start.2
  10.5 0.6 collective-permute-start.3
  11.2 0.1 copy.17.cnt
  11.4 0.3 collective-permute-done.2.swap1
  11.8 8.4 %shard_map.155 = (bf16[1024,128]{1,0:T(8,128)(2,1)S(1)}, bf16[1440,256]{1,0:T(8,128)(2,1)S(1)}, bf16[1440,256]{1,0:T(8,128)(2,1)S(1)}, bf16[1024,256]{1,0:T(8,128)(2,1)S(1)}) custom-call(f32[6]{0:T(128)S(1)} %convert_element_type.20.flags, bf16[1024,64]{1,0:T(8,128)(2,1)S(1)} %get-tuple-element.36.fto, bf16[512,64]{1,0:T(8,128)(2,1)S(1)} %get-tuple-element.39.ftr, ...), custom_call_target="tpu_custom_call" | custom-call | flops 2000000000 | bytes 4000000 | tf_op jit(solution)/shard_map/pallas_call | solution.py:485
  20.1 26.9 %all_to_all.32 = bf16[128,8,128]{2,1,0:T(8,128)(2,1)S(1)} all-to-all(bf16[128,8,128]{2,1,0:T(8,128)(2,1)S(1)} %bitcast.38), channel_id=1, replica_groups=mesh['ns'=8,'ew'=16] {'ns','ew'}, dimensions={0} | all-to-all | bytes 524288 | tf_op jit(solution)/shard_map/all_to_all | solution.py:478
  47.0 5.9 %shard_map.156 = (f32[6,2048]{1,0:T(8,128)}, f32[16,128]{1,0:T(8,128)S(1)}, bf16[1024,128]{1,0:T(8,128)(2,1)S(1)}) custom-call(bf16[1024,128]{1,0:T(8,128)(2,1)S(1)} %bitcast.39, s32[128,128]{1,0:T(8,128)S(1)} %bitcast.42, f32[6,2048]{1,0:T(8,128)S(1)} %copy-done.4), custom_call_target="tpu_custom_call" | custom-call | flops 1000000000 | bytes 4000000 | tf_op jit(solution)/shard_map/pallas_call | solution.py:485
  52.9 15.3 %all_to_all.33 = bf16[128,8,128]{2,1,0:T(8,128)(2,1)S(1)} all-to-all(bf16[128,8,128]{2,1,0:T(8,128)(2,1)S(1)} %bitcast.40), channel_id=1, replica_groups=mesh['ns'=8,'ew'=16] {'ns','ew'}, dimensions={0} | all-to-all | bytes 524288 | tf_op jit(solution)/shard_map/all_to_all | solution.py:478
  68.2 7.8 %shard_map.157 = (f32[64,128]{1,0:T(8,128)S(1)}, f32[16,128]{1,0:T(8,128)S(1)}, f32[16,128]{1,0:T(8,128)S(1)}) custom-call(f32[6]{0:T(128)S(1)} %convert_element_type.20.flags, bf16[1024,128]{1,0:T(8,128)(2,1)S(1)} %bitcast.37, s32[4,128,128]{2,1,0:T(8,128)S(1)} %bitcast.34, f32[4,128,128]{2,1,0:T(8,128)S(1)} %bitcast.36, s32[128,1]{1,0:T(8,128)S(1)} %copy.17.cnt), custom_call_target="tpu_custom_call" | custom-call | flops 1000000000 | bytes 4000000 | tf_op jit(solution)/shard_map/pallas_call | solution.py:485
  76.0 0.6 collective-permute-start.4
  76.6 2.2 %collective-permute-start.5 = (f32[16,128]{1,0:T(8,128)S(1)}, f32[16,128]{1,0:T(8,128)S(1)}, u32[]{:S(2)}, u32[]{:S(2)}) collective-permute-start(f32[16,128]{1,0:T(8,128)S(1)} %get-tuple-element.47), channel_id=1, source_target_pairs={{16,32},{48,64},{80,96},{32,16},{64,48},{96,80},{17,33},{49,65},{8... | collective-permute-start | bytes 24584 | tf_op jit(solution)/shard_map/ppermute | solution.py:473
  78.8 2.9 %collective-permute-done.5.swap2 = f32[16,128]{1,0:T(8,128)S(1)} collective-permute-done((f32[16,128]{1,0:T(8,128)S(1)}, f32[16,128]{1,0:T(8,128)S(1)}, u32[]{:S(2)}, u32[]{:S(2)}) %collective-permute-start.5) | collective-permute-done | bytes 8224 | tf_op jit(solution)/shard_map/ppermute | solution.py:473
  81.6 0.6 shard_map.158
  82.3 0.4 collective-permute-start.6
  82.7 0.8 collective-permute-start.7
  83.5 2.1 %shard_map.159 = (bf16[576,1280]{1,0:T(8,128)(2,1)S(1)}, bf16[576,1280]{1,0:T(8,128)(2,1)S(1)}) custom-call(f32[6]{0:T(128)S(1)} %convert_element_type.20.flags, bf16[1440,256]{1,0:T(8,128)(2,1)S(1)} %get-tuple-element.52.a1, bf16[1024,64]{1,0:T(8,128)(2,1)S(1)} %get-tuple-element.36.fto, bf16[512,64]{1,0:T(8,128)(2,1)S(1)} %get-tuple-element.39.ftr, ...), custom_call_target="tpu_custom_call" | custom-call | flops 1000000000 | bytes 4000000 | tf_op jit(solution)/shard_map/pallas_call | solution.py:485
  85.6 7.5 %shard_map.160 = (bf16[6144,128]{1,0:T(8,128)(2,1)S(1)}, f32[512,128]{1,0:T(8,128)}) custom-call(f32[6]{0:T(128)S(1)} %convert_element_type.20.flags, f32[64,128]{1,0:T(8,128)S(1)} %get-tuple-element.45.gf, f32[128,96]{1,0:T(8,128)S(1)} %get-tuple-element.48.et, f32[2,96]{1,0:T(2,128)S(1)} %collective-permute-done.6.swap1, ...), custom_call_target="tpu_custom_call" | custom-call | flops 2000000000 | bytes 4000000 | tf_op jit(solution)/shard_map/pallas_call | solution.py:485
  93.3 2.3 %collective-permute-done.8 = bf16[3072,128]{1,0:T(8,128)(2,1)S(1)} collective-permute-done((bf16[3072,128]{1,0:T(8,128)(2,1)S(1)}, bf16[3072,128]{1,0:T(8,128)(2,1)S(1)}, u32[]{:S(2)}, u32[]{:S(2)}) %collective-permute-start.8) | collective-permute-done | bytes 786464 | tf_op jit(solution)/shard_map/ppermute | solution.py:602
  95.6 0.2 add_convert_fusion
  95.8 24.1 %all_to_all.34 = bf16[64,48,128]{2,1,0:T(8,128)(2,1)S(1)} all-to-all(bf16[64,48,128]{2,1,0:T(8,128)(2,1)S(1)} %bitcast.43), channel_id=1, replica_groups={{0,1,2,3,4,5,6,7,8,9,10,11,12,13,14,15,32,33,34,35,36,37,38,39,40,41,42..., dimensions={0} | all-to-all | bytes 1572864 | tf_op jit(solution)/shard_map/all_to_all | solution.py:478
  119.9 0.1 reduce_sum.12
  120.1 18.6 %all_to_all.35 = bf16[64,48,128]{2,1,0:T(8,128)(2,1)S(1)} all-to-all(bf16[64,48,128]{2,1,0:T(8,128)(2,1)S(1)} %broadcast_in_dim.2), channel_id=1, replica_groups={{0,1,2,3,4,5,6,7,8,9,10,11,12,13,14,15,32,33,34,35,36,37,38,39,40,41,42..., dimensions={0} | all-to-all | bytes 1572864 | tf_op jit(solution)/shard_map/all_to_all | solution.py:478
  138.7 2.9 %collective-permute-start.9 = (bf16[3072,128]{1,0:T(8,128)(2,1)S(1)}, bf16[3072,128]{1,0:T(8,128)(2,1)S(1)}, u32[]{:S(2)}, u32[]{:S(2)}) collective-permute-start(bf16[3072,128]{1,0:T(8,128)(2,1)S(1)} %bitcast.31), channel_id=1, source_target_pairs={{0,16},{16,0},{32,48},{48,32},{64,80},{80,64},{96,112},{112,96},{1... | collective-permute-start | bytes 2359304 | tf_op jit(solution)/shard_map/ppermute | solution.py:606
  141.6 1.9 %collective-permute-done.9.other = bf16[3072,128]{1,0:T(8,128)(2,1)S(1)} collective-permute-done((bf16[3072,128]{1,0:T(8,128)(2,1)S(1)}, bf16[3072,128]{1,0:T(8,128)(2,1)S(1)}, u32[]{:S(2)}, u32[]{:S(2)}) %collective-permute-start.9) | collective-permute-done | bytes 786464 | tf_op jit(solution)/shard_map/ppermute | solution.py:606
  143.5 2.7 %shard_map.161 = (f32[3,3,192,192]{3,2,1,0:T(8,128)}, f32[3,3,192,192]{3,2,1,0:T(8,128)}, f32[64,192]{1,0:T(8,128)}, f32[6,192]{1,0:T(8,128)}, f32[1,1]{1,0:T(1,128)}) custom-call(f32[6]{0:T(128)S(1)} %convert_element_type.20.flags, bf16[3072,128]{1,0:T(8,128)(2,1)S(1)} %bitcast.32, bf16[3072,128]{1,0:T(8,128)(2,1)S(1)} %collective-permute-done.9.other), custom_call_target="tpu_custom_call" | custom-call | bytes 4000000 | tf_op jit(solution)/shard_map/pallas_call | solution.py:485
  (33 shorter events, 0.5 us)
Async XLA Ops:
  1.7 6.0 %collective-permute-start = (bf16[128,128]{1,0:T(8,128)(2,1)S(1)}, bf16[128,128]{1,0:T(8,128)(2,1)S(1)}, u32[]{:S(2)}, u32[]{:S(2)}) collective-permute-start(bf16[128,128]{1,0:T(8,128)(2,1)S(1)} %bitcast.47), channel_id=1, source_target_pairs={{0,16},{32,48},{64,80},{96,112},{16,0},{48,32},{80,64},{112,96},{1... | collective-permute-start | bytes 98312 | tf_op jit(solution)/shard_map/ppermute | solution.py:473
  3.2 5.2 %collective-permute-start.1 = (bf16[128,128]{1,0:T(8,128)(2,1)S(1)}, bf16[128,128]{1,0:T(8,128)(2,1)S(1)}, u32[]{:S(2)}, u32[]{:S(2)}) collective-permute-start(bf16[128,128]{1,0:T(8,128)(2,1)S(1)} %bitcast.46), channel_id=1, source_target_pairs={{16,32},{48,64},{80,96},{32,16},{64,48},{96,80},{17,33},{49,65},{8... | collective-permute-start | bytes 98312 | tf_op jit(solution)/shard_map/ppermute | solution.py:473
  6.4 0.9 copy-start
  8.4 2.8 %copy-start.7 = (bf16[64,192]{1,0:T(8,128)(2,1)S(1)}, bf16[64,192]{1,0:T(8,128)(2,1)}, u32[]{:S(2)}) copy-start(bf16[64,192]{1,0:T(8,128)(2,1)} %param.11) | copy-start | bytes 73732
  8.4 2.8 %copy-start.8 = (bf16[192,6]{0,1:T(8,128)(2,1)S(1)}, bf16[192,6]{0,1:T(8,128)(2,1)}, u32[]{:S(2)}) copy-start(bf16[192,6]{0,1:T(8,128)(2,1)} %param.14) | copy-start | bytes 6916
  8.4 2.8 %copy-start.9 = (s32[1,128]{1,0:T(1,128)S(1)}, s32[1,128]{1,0:T(1,128)}, u32[]{:S(2)}) copy-start(s32[1,128]{1,0:T(1,128)} %param.17) | copy-start | bytes 1540
  8.4 2.9 %copy-start.5 = (s32[1,4,16384]{2,1,0:T(4,128)S(1)}, s32[1,4,16384]{2,1,0:T(4,128)}, u32[]{:S(2)}) copy-start(s32[1,4,16384]{2,1,0:T(4,128)} %param.15) | copy-start | bytes 786436
  8.4 2.9 %copy-start.6 = (f32[1,4,16384]{2,1,0:T(4,128)S(1)}, f32[1,4,16384]{2,1,0:T(4,128)}, u32[]{:S(2)}) copy-start(f32[1,4,16384]{2,1,0:T(4,128)} %param.16) | copy-start | bytes 786436
  8.4 3.3 %copy-start.1 = (bf16[3,3,192,192]{3,2,1,0:T(8,128)(2,1)S(1)}, bf16[3,3,192,192]{3,2,1,0:T(8,128)(2,1)}, u32[]{:S(2)}) copy-start(bf16[3,3,192,192]{3,2,1,0:T(8,128)(2,1)} %c1.3) | copy-start | bytes 1990660
  8.5 3.3 %copy-start.2 = (bf16[3,3,192,192]{3,2,1,0:T(8,128)(2,1)S(1)}, bf16[3,3,192,192]{3,2,1,0:T(8,128)(2,1)}, u32[]{:S(2)}) copy-start(bf16[3,3,192,192]{3,2,1,0:T(8,128)(2,1)} %c2.3) | copy-start | bytes 1990660
  9.1 2.6 %collective-permute-start.2 = (bf16[32,64]{1,0:T(8,128)(2,1)S(1)}, bf16[32,64]{1,0:T(8,128)(2,1)S(1)}, u32[]{:S(2)}, u32[]{:S(2)}) collective-permute-start(bf16[32,64]{1,0:T(8,128)(2,1)S(1)} %get-tuple-element.40), channel_id=1, source_target_pairs={{0,1},{2,3},{4,5},{6,7},{8,9},{10,11},{12,13},{14,15},{1,0},{3,2},... | collective-permute-start | bytes 12296 | tf_op jit(solution)/shard_map/ppermute | solution.py:473
  10.5 1.2 collective-permute-start.3
  11.7 35.3 %copy-start.3 = (s32[1,16384]{1,0:T(1,128)S(1)}, s32[1,16384]{1,0:T(1,128)}, u32[]{:S(2)}) copy-start(s32[1,16384]{1,0:T(1,128)} %param.18) | copy-start | bytes 196612
  11.7 35.3 %copy-start.4 = (f32[6,2048]{1,0:T(8,128)S(1)}, f32[6,2048]{1,0:T(8,128)}, u32[]{:S(2)}) copy-start(f32[6,2048]{1,0:T(8,128)} %target.1) | copy-start | bytes 147460
  76.0 2.7 %collective-permute-start.4 = (f32[16,128]{1,0:T(8,128)S(1)}, f32[16,128]{1,0:T(8,128)S(1)}, u32[]{:S(2)}, u32[]{:S(2)}) collective-permute-start(f32[16,128]{1,0:T(8,128)S(1)} %get-tuple-element.46), channel_id=1, source_target_pairs={{0,16},{32,48},{64,80},{96,112},{16,0},{48,32},{80,64},{112,96},{1... | collective-permute-start | bytes 24584 | tf_op jit(solution)/shard_map/ppermute | solution.py:473
  76.6 5.1 %collective-permute-start.5 = (f32[16,128]{1,0:T(8,128)S(1)}, f32[16,128]{1,0:T(8,128)S(1)}, u32[]{:S(2)}, u32[]{:S(2)}) collective-permute-start(f32[16,128]{1,0:T(8,128)S(1)} %get-tuple-element.47), channel_id=1, source_target_pairs={{16,32},{48,64},{80,96},{32,16},{64,48},{96,80},{17,33},{49,65},{8... | collective-permute-start | bytes 24584 | tf_op jit(solution)/shard_map/ppermute | solution.py:473
  82.3 3.3 %collective-permute-start.6 = (f32[2,96]{1,0:T(2,128)S(1)}, f32[2,96]{1,0:T(2,128)S(1)}, u32[]{:S(2)}, u32[]{:S(2)}) collective-permute-start(f32[2,96]{1,0:T(2,128)S(1)} %get-tuple-element.49), channel_id=1, source_target_pairs={{0,1},{2,3},{4,5},{6,7},{8,9},{10,11},{12,13},{14,15},{1,0},{3,2},... | collective-permute-start | bytes 2312 | tf_op jit(solution)/shard_map/ppermute | solution.py:473
  82.7 2.9 %collective-permute-start.7 = (f32[2,96]{1,0:T(2,128)S(1)}, f32[2,96]{1,0:T(2,128)S(1)}, u32[]{:S(2)}, u32[]{:S(2)}) collective-permute-start(f32[2,96]{1,0:T(2,128)S(1)} %get-tuple-element.50), channel_id=1, source_target_pairs={{1,2},{3,4},{5,6},{7,8},{9,10},{11,12},{13,14},{2,1},{4,3},{6,5},{... | collective-permute-start | bytes 2312 | tf_op jit(solution)/shard_map/ppermute | solution.py:473
  93.3 2.4 %collective-permute-start.8 = (bf16[3072,128]{1,0:T(8,128)(2,1)S(1)}, bf16[3072,128]{1,0:T(8,128)(2,1)S(1)}, u32[]{:S(2)}, u32[]{:S(2)}) collective-permute-start(bf16[3072,128]{1,0:T(8,128)(2,1)S(1)} %slice.15), channel_id=1, source_target_pairs={{0,16},{16,0},{32,48},{48,32},{64,80},{80,64},{96,112},{112,96},{1... | collective-permute-start | bytes 2359304 | tf_op jit(solution)/shard_map/ppermute | solution.py:602
  138.7 4.8 %collective-permute-start.9 = (bf16[3072,128]{1,0:T(8,128)(2,1)S(1)}, bf16[3072,128]{1,0:T(8,128)(2,1)S(1)}, u32[]{:S(2)}, u32[]{:S(2)}) collective-permute-start(bf16[3072,128]{1,0:T(8,128)(2,1)S(1)} %bitcast.31), channel_id=1, source_target_pairs={{0,16},{16,0},{32,48},{48,32},{64,80},{80,64},{96,112},{112,96},{1... | collective-permute-start | bytes 2359304 | tf_op jit(solution)/shard_map/ppermute | solution.py:606

commit v5 on v4

--- a/solution.py
+++ b/solution.py
@@ -198,7 +198,7 @@
             pf[pl.ds(ob * 64 + v, 8, stride=8), :] = sums[v]
         return carry
 
-    lax.fori_loop(0, 16, owners, 0)
+    lax.fori_loop(0, 16, owners, 0, unroll=4)
     out[...] = pf[...].astype(BF)
 
 
@@ -241,7 +241,7 @@
         multiply(1)
         return carry
 
-    lax.fori_loop(0, count // 2, step, 0)
+    lax.fori_loop(0, count // 2, step, 0, unroll=2)
 
 
 def owner_kernel(recv, obs, target, pred, loss, out, l0, l1, r0, r1, total, rq, gf):
@@ -306,7 +306,7 @@
             gf[pl.ds(tb * 64 + v + 3, 8, stride=8), :] = y * down
         return carry
 
-    lax.fori_loop(0, 16, choose, 0)
+    lax.fori_loop(0, 16, choose, 0, unroll=4)
     out[...] = gf[...].astype(BF)
 
 
@@ -436,18 +436,22 @@
     put(base_f, EXTRA + 32, jnp.zeros((HALF - EXTRA - 32, 128), F32))
 
 
-def unpack_kernel(flags, mine, other, second, first, g_in, g_out, loss):
-    def unpack(source, kernel):
+def unpack_kernel(flags, mine, other, second, first, g_in, g_out, loss, sv, fv, sems):
+    def unpack(source, kernel, out, at):
+        copies = []
         for tap in range(9):
             a, b = tap // 3, tap % 3
             kernel[a, b, :, 0:128] = source[tap * C : (tap + 1) * C, :].astype(F32)
             rest = source[REST + tap * 96 : REST + tap * 96 + 96, :].astype(F32)
             kernel[a, b, 0:96, 128:C] = rest[:, 0:64]
             kernel[a, b, 96:C, 128:C] = pltpu.roll(rest, 64, 1)[:, 0:64]
+            if b == 2:
+                copies.append(pltpu.make_async_copy(kernel.at[a], out.at[a], sems.at[at + a]))
+                copies[-1].start()
+        return copies
 
     def both(s, f):
-        unpack(s, second)
-        unpack(f, first)
+        copies = unpack(s, sv, second, 0) + unpack(f, fv, first, 3)
         g_in[:, 0:128] = s[EXTRA : EXTRA + 64, :].astype(F32)
         rest = s[EXTRA + 64 : EXTRA + 96, :].astype(F32)
         g_in[0:32, 128:C] = rest[:, 0:64]
@@ -456,6 +460,8 @@
         g_out[:, 0:128] = extra[0:6]
         g_out[:, 128:C] = extra[8:14, 0:64]
         loss[0, 0] = jnp.max(extra[16:24])
+        for copy in copies:
+            copy.wait()
 
     @pl.when(flags[4] == 0)
     def _():
@@ -480,14 +486,16 @@
     )
 
 
-def call(kernel, out_shapes, scratch, *operands, smem=0, smem_out=0, vmem=60, flops=0):
+def call(kernel, out_shapes, scratch, *operands, smem=0, any_out=0, smem_out=0, vmem=60, flops=0):
     vm, sm = pl.BlockSpec(memory_space=pltpu.VMEM), pl.BlockSpec(memory_space=pltpu.SMEM)
     return pl.pallas_call(
         kernel,
         out_shape=[jax.ShapeDtypeStruct(s, d) for s, d in out_shapes],
         in_specs=[sm] * smem + [vm] * (len(operands) - smem),
-        out_specs=[vm] * (len(out_shapes) - smem_out) + [sm] * smem_out,
-        scratch_shapes=[pltpu.VMEM(s, d) for s, d in scratch],
+        out_specs=[pl.BlockSpec(memory_space=pl.ANY)] * any_out
+        + [vm] * (len(out_shapes) - any_out - smem_out)
+        + [sm] * smem_out,
+        scratch_shapes=[pltpu.VMEM(*s) if isinstance(s, tuple) else s for s in scratch],
         compiler_params=pltpu.CompilerParams(vmem_limit_bytes=vmem * 1024 * 1024),
         cost_estimate=pl.CostEstimate(flops=flops, bytes_accessed=4_000_000, transcendentals=0),
     )(*operands)
@@ -607,9 +615,9 @@
     grad_second, grad_first, grad_in, g_out, total = call(
         unpack_kernel,
         [((3, 3, C, C), F32), ((3, 3, C, C), F32), ((64, C), F32), ((6, C), F32), ((1, 1), F32)],
-        [],
+        [((3, 3, C, C), F32), ((3, 3, C, C), F32), pltpu.SemaphoreType.DMA((6,))],
         flags, mine, other,
-        smem=1, smem_out=1, vmem=16,
+        smem=1, any_out=2, smem_out=1, vmem=16,
     )
     return (
         pred,

time: 147 us -> 145 us (0.986)
  Pallas kernels: 35.9 us -> 34 us
    pallas_call x9, Pallas kernels: 35.9 us -> 34 us  [call(): pl.pallas_call(kernel, out_shape=[jax.ShapeDtypeStruct(s, d) for s, d in...]
where the time goes in v5:
time: 145 us; the launch traced here: 144 us
  blocking collectives  84.8 us (58%)
  Pallas kernels  34 us (23%)
  starting transfers between devices  13.6 us (9%)
  waiting for transfers between devices  8.15 us (6%)
    all_to_all x4, blocking collectives, exchange(): lax.all_to_all(rows, AXES, split_axis=0, concat_axis=0, tiled=True, axis_...  84.8 us
    pallas_call x9, Pallas kernels, call(): pl.pallas_call(kernel, out_shape=[jax.ShapeDtypeStruct(s, d) for s, d in...  34 us
    ppermute x8, starting transfers between devices, swaps(): lax.ppermute(x, axis, p + [(j, i) for i, j in p])  10.7 us
    ppermute x8, waiting for transfers between devices, swaps(): lax.ppermute(x, axis, p + [(j, i) for i, j in p])  3.97 us
  transfers between devices with their start and end apart: 10, of which 5 were waited for; matrix products, arithmetic and copies ran while one was open for 0% of the time, Pallas kernels for 2%

profile of v5, /device:TPU:1, one launch (start us, length us, event | category | flops | bytes accessed | tf_op | source)
XLA Modules:
  0.0 144.5 jit_solution(4490618772193960971)
XLA Ops:
  0.6 1.1 broadcast_select_fusion
  1.7 1.5 %collective-permute-start = (bf16[128,128]{1,0:T(8,128)(2,1)S(1)}, bf16[128,128]{1,0:T(8,128)(2,1)S(1)}, u32[]{:S(2)}, u32[]{:S(2)}) collective-permute-start(bf16[128,128]{1,0:T(8,128)(2,1)S(1)} %bitcast.47), channel_id=1, source_target_pairs={{0,16},{32,48},{64,80},{96,112},{16,0},{48,32},{80,64},{112,96},{1... | collective-permute-start | bytes 98312 | tf_op jit(solution)/shard_map/ppermute | solution.py:479
  3.2 3.2 %collective-permute-start.1 = (bf16[128,128]{1,0:T(8,128)(2,1)S(1)}, bf16[128,128]{1,0:T(8,128)(2,1)S(1)}, u32[]{:S(2)}, u32[]{:S(2)}) collective-permute-start(bf16[128,128]{1,0:T(8,128)(2,1)S(1)} %bitcast.46), channel_id=1, source_target_pairs={{16,32},{48,64},{80,96},{32,16},{64,48},{96,80},{17,33},{49,65},{8... | collective-permute-start | bytes 98312 | tf_op jit(solution)/shard_map/ppermute | solution.py:479
  6.4 0.9 copy-done
  7.3 0.2 shard_map.153
  7.7 0.8 collective-permute-done.1.swap2
  8.5 0.7 shard_map.154
  9.1 1.4 collective-permute-start.2
  10.5 0.6 collective-permute-start.3
  11.2 0.1 copy.17.cnt
  11.4 0.3 collective-permute-done.2.swap1
  11.8 7.5 %shard_map.155 = (bf16[1024,128]{1,0:T(8,128)(2,1)S(1)}, bf16[1440,256]{1,0:T(8,128)(2,1)S(1)}, bf16[1440,256]{1,0:T(8,128)(2,1)S(1)}, bf16[1024,256]{1,0:T(8,128)(2,1)S(1)}) custom-call(f32[6]{0:T(128)S(1)} %convert_element_type.20.flags, bf16[1024,64]{1,0:T(8,128)(2,1)S(1)} %get-tuple-element.36.fto, bf16[512,64]{1,0:T(8,128)(2,1)S(1)} %get-tuple-element.39.ftr, ...), custom_call_target="tpu_custom_call" | custom-call | flops 2000000000 | bytes 4000000 | tf_op jit(solution)/shard_map/pallas_call | solution.py:491
  19.3 26.9 %all_to_all.32 = bf16[128,8,128]{2,1,0:T(8,128)(2,1)S(1)} all-to-all(bf16[128,8,128]{2,1,0:T(8,128)(2,1)S(1)} %bitcast.38), channel_id=1, replica_groups=mesh['ns'=8,'ew'=16] {'ns','ew'}, dimensions={0} | all-to-all | bytes 524288 | tf_op jit(solution)/shard_map/all_to_all | solution.py:484
  46.2 4.4 %shard_map.156 = (f32[6,2048]{1,0:T(8,128)}, f32[16,128]{1,0:T(8,128)S(1)}, bf16[1024,128]{1,0:T(8,128)(2,1)S(1)}) custom-call(bf16[1024,128]{1,0:T(8,128)(2,1)S(1)} %bitcast.39, s32[128,128]{1,0:T(8,128)S(1)} %bitcast.42, f32[6,2048]{1,0:T(8,128)S(1)} %copy-done.4), custom_call_target="tpu_custom_call" | custom-call | flops 1000000000 | bytes 4000000 | tf_op jit(solution)/shard_map/pallas_call | solution.py:491
  50.6 15.3 %all_to_all.33 = bf16[128,8,128]{2,1,0:T(8,128)(2,1)S(1)} all-to-all(bf16[128,8,128]{2,1,0:T(8,128)(2,1)S(1)} %bitcast.40), channel_id=1, replica_groups=mesh['ns'=8,'ew'=16] {'ns','ew'}, dimensions={0} | all-to-all | bytes 524288 | tf_op jit(solution)/shard_map/all_to_all | solution.py:484
  65.9 7.8 %shard_map.157 = (f32[64,128]{1,0:T(8,128)S(1)}, f32[16,128]{1,0:T(8,128)S(1)}, f32[16,128]{1,0:T(8,128)S(1)}) custom-call(f32[6]{0:T(128)S(1)} %convert_element_type.20.flags, bf16[1024,128]{1,0:T(8,128)(2,1)S(1)} %bitcast.37, s32[4,128,128]{2,1,0:T(8,128)S(1)} %bitcast.34, f32[4,128,128]{2,1,0:T(8,128)S(1)} %bitcast.36, s32[128,1]{1,0:T(8,128)S(1)} %copy.17.cnt), custom_call_target="tpu_custom_call" | custom-call | flops 1000000000 | bytes 4000000 | tf_op jit(solution)/shard_map/pallas_call | solution.py:491
  73.7 0.6 collective-permute-start.4
  74.3 2.2 %collective-permute-start.5 = (f32[16,128]{1,0:T(8,128)S(1)}, f32[16,128]{1,0:T(8,128)S(1)}, u32[]{:S(2)}, u32[]{:S(2)}) collective-permute-start(f32[16,128]{1,0:T(8,128)S(1)} %get-tuple-element.47), channel_id=1, source_target_pairs={{16,32},{48,64},{80,96},{32,16},{64,48},{96,80},{17,33},{49,65},{8... | collective-permute-start | bytes 24584 | tf_op jit(solution)/shard_map/ppermute | solution.py:479
  76.4 2.9 %collective-permute-done.5.swap2 = f32[16,128]{1,0:T(8,128)S(1)} collective-permute-done((f32[16,128]{1,0:T(8,128)S(1)}, f32[16,128]{1,0:T(8,128)S(1)}, u32[]{:S(2)}, u32[]{:S(2)}) %collective-permute-start.5) | collective-permute-done | bytes 8224 | tf_op jit(solution)/shard_map/ppermute | solution.py:479
  79.3 0.6 shard_map.158
  80.0 0.4 collective-permute-start.6
  80.4 0.8 collective-permute-start.7
  81.2 2.1 %shard_map.159 = (bf16[576,1280]{1,0:T(8,128)(2,1)S(1)}, bf16[576,1280]{1,0:T(8,128)(2,1)S(1)}) custom-call(f32[6]{0:T(128)S(1)} %convert_element_type.20.flags, bf16[1440,256]{1,0:T(8,128)(2,1)S(1)} %get-tuple-element.52.a1, bf16[1024,64]{1,0:T(8,128)(2,1)S(1)} %get-tuple-element.36.fto, bf16[512,64]{1,0:T(8,128)(2,1)S(1)} %get-tuple-element.39.ftr, ...), custom_call_target="tpu_custom_call" | custom-call | flops 1000000000 | bytes 4000000 | tf_op jit(solution)/shard_map/pallas_call | solution.py:491
  83.3 7.5 %shard_map.160 = (bf16[6144,128]{1,0:T(8,128)(2,1)S(1)}, f32[512,128]{1,0:T(8,128)}) custom-call(f32[6]{0:T(128)S(1)} %convert_element_type.20.flags, f32[64,128]{1,0:T(8,128)S(1)} %get-tuple-element.45.gf, f32[128,96]{1,0:T(8,128)S(1)} %get-tuple-element.48.et, f32[2,96]{1,0:T(2,128)S(1)} %collective-permute-done.6.swap1, ...), custom_call_target="tpu_custom_call" | custom-call | flops 2000000000 | bytes 4000000 | tf_op jit(solution)/shard_map/pallas_call | solution.py:491
  91.0 2.3 %collective-permute-done.8 = bf16[3072,128]{1,0:T(8,128)(2,1)S(1)} collective-permute-done((bf16[3072,128]{1,0:T(8,128)(2,1)S(1)}, bf16[3072,128]{1,0:T(8,128)(2,1)S(1)}, u32[]{:S(2)}, u32[]{:S(2)}) %collective-permute-start.8) | collective-permute-done | bytes 786464 | tf_op jit(solution)/shard_map/ppermute | solution.py:610
  93.3 0.2 add_convert_fusion
  93.5 24.1 %all_to_all.34 = bf16[64,48,128]{2,1,0:T(8,128)(2,1)S(1)} all-to-all(bf16[64,48,128]{2,1,0:T(8,128)(2,1)S(1)} %bitcast.43), channel_id=1, replica_groups={{0,1,2,3,4,5,6,7,8,9,10,11,12,13,14,15,32,33,34,35,36,37,38,39,40,41,42..., dimensions={0} | all-to-all | bytes 1572864 | tf_op jit(solution)/shard_map/all_to_all | solution.py:484
  117.6 0.1 reduce_sum.12
  117.8 18.6 %all_to_all.35 = bf16[64,48,128]{2,1,0:T(8,128)(2,1)S(1)} all-to-all(bf16[64,48,128]{2,1,0:T(8,128)(2,1)S(1)} %broadcast_in_dim.2), channel_id=1, replica_groups={{0,1,2,3,4,5,6,7,8,9,10,11,12,13,14,15,32,33,34,35,36,37,38,39,40,41,42..., dimensions={0} | all-to-all | bytes 1572864 | tf_op jit(solution)/shard_map/all_to_all | solution.py:484
  136.4 2.9 %collective-permute-start.9 = (bf16[3072,128]{1,0:T(8,128)(2,1)S(1)}, bf16[3072,128]{1,0:T(8,128)(2,1)S(1)}, u32[]{:S(2)}, u32[]{:S(2)}) collective-permute-start(bf16[3072,128]{1,0:T(8,128)(2,1)S(1)} %bitcast.31), channel_id=1, source_target_pairs={{0,16},{16,0},{32,48},{48,32},{64,80},{80,64},{96,112},{112,96},{1... | collective-permute-start | bytes 2359304 | tf_op jit(solution)/shard_map/ppermute | solution.py:614
  139.3 1.9 %collective-permute-done.9.other = bf16[3072,128]{1,0:T(8,128)(2,1)S(1)} collective-permute-done((bf16[3072,128]{1,0:T(8,128)(2,1)S(1)}, bf16[3072,128]{1,0:T(8,128)(2,1)S(1)}, u32[]{:S(2)}, u32[]{:S(2)}) %collective-permute-start.9) | collective-permute-done | bytes 786464 | tf_op jit(solution)/shard_map/ppermute | solution.py:614
  141.2 3.1 %shard_map.161 = (f32[3,3,192,192]{3,2,1,0:T(8,128)}, f32[3,3,192,192]{3,2,1,0:T(8,128)}, f32[64,192]{1,0:T(8,128)}, f32[6,192]{1,0:T(8,128)}, f32[1,1]{1,0:T(1,128)}) custom-call(f32[6]{0:T(128)S(1)} %convert_element_type.20.flags, bf16[3072,128]{1,0:T(8,128)(2,1)S(1)} %bitcast.32, bf16[3072,128]{1,0:T(8,128)(2,1)S(1)} %collective-permute-done.9.other), custom_call_target="tpu_custom_call" | custom-call | bytes 4000000 | tf_op jit(solution)/shard_map/pallas_call | solution.py:491
  (33 shorter events, 0.5 us)
Async XLA Ops:
  1.7 6.0 %collective-permute-start = (bf16[128,128]{1,0:T(8,128)(2,1)S(1)}, bf16[128,128]{1,0:T(8,128)(2,1)S(1)}, u32[]{:S(2)}, u32[]{:S(2)}) collective-permute-start(bf16[128,128]{1,0:T(8,128)(2,1)S(1)} %bitcast.47), channel_id=1, source_target_pairs={{0,16},{32,48},{64,80},{96,112},{16,0},{48,32},{80,64},{112,96},{1... | collective-permute-start | bytes 98312 | tf_op jit(solution)/shard_map/ppermute | solution.py:479
  3.2 5.2 %collective-permute-start.1 = (bf16[128,128]{1,0:T(8,128)(2,1)S(1)}, bf16[128,128]{1,0:T(8,128)(2,1)S(1)}, u32[]{:S(2)}, u32[]{:S(2)}) collective-permute-start(bf16[128,128]{1,0:T(8,128)(2,1)S(1)} %bitcast.46), channel_id=1, source_target_pairs={{16,32},{48,64},{80,96},{32,16},{64,48},{96,80},{17,33},{49,65},{8... | collective-permute-start | bytes 98312 | tf_op jit(solution)/shard_map/ppermute | solution.py:479
  6.4 0.9 copy-start
  8.4 2.8 %copy-start.7 = (bf16[64,192]{1,0:T(8,128)(2,1)S(1)}, bf16[64,192]{1,0:T(8,128)(2,1)}, u32[]{:S(2)}) copy-start(bf16[64,192]{1,0:T(8,128)(2,1)} %param.11) | copy-start | bytes 73732
  8.4 2.8 %copy-start.8 = (bf16[192,6]{0,1:T(8,128)(2,1)S(1)}, bf16[192,6]{0,1:T(8,128)(2,1)}, u32[]{:S(2)}) copy-start(bf16[192,6]{0,1:T(8,128)(2,1)} %param.14) | copy-start | bytes 6916
  8.4 2.8 %copy-start.9 = (s32[1,128]{1,0:T(1,128)S(1)}, s32[1,128]{1,0:T(1,128)}, u32[]{:S(2)}) copy-start(s32[1,128]{1,0:T(1,128)} %param.17) | copy-start | bytes 1540
  8.4 2.9 %copy-start.5 = (s32[1,4,16384]{2,1,0:T(4,128)S(1)}, s32[1,4,16384]{2,1,0:T(4,128)}, u32[]{:S(2)}) copy-start(s32[1,4,16384]{2,1,0:T(4,128)} %param.15) | copy-start | bytes 786436
  8.4 2.9 %copy-start.6 = (f32[1,4,16384]{2,1,0:T(4,128)S(1)}, f32[1,4,16384]{2,1,0:T(4,128)}, u32[]{:S(2)}) copy-start(f32[1,4,16384]{2,1,0:T(4,128)} %param.16) | copy-start | bytes 786436
  8.4 3.3 %copy-start.1 = (bf16[3,3,192,192]{3,2,1,0:T(8,128)(2,1)S(1)}, bf16[3,3,192,192]{3,2,1,0:T(8,128)(2,1)}, u32[]{:S(2)}) copy-start(bf16[3,3,192,192]{3,2,1,0:T(8,128)(2,1)} %c1.3) | copy-start | bytes 1990660
  8.5 3.3 %copy-start.2 = (bf16[3,3,192,192]{3,2,1,0:T(8,128)(2,1)S(1)}, bf16[3,3,192,192]{3,2,1,0:T(8,128)(2,1)}, u32[]{:S(2)}) copy-start(bf16[3,3,192,192]{3,2,1,0:T(8,128)(2,1)} %c2.3) | copy-start | bytes 1990660
  9.1 2.6 %collective-permute-start.2 = (bf16[32,64]{1,0:T(8,128)(2,1)S(1)}, bf16[32,64]{1,0:T(8,128)(2,1)S(1)}, u32[]{:S(2)}, u32[]{:S(2)}) collective-permute-start(bf16[32,64]{1,0:T(8,128)(2,1)S(1)} %get-tuple-element.40), channel_id=1, source_target_pairs={{0,1},{2,3},{4,5},{6,7},{8,9},{10,11},{12,13},{14,15},{1,0},{3,2},... | collective-permute-start | bytes 12296 | tf_op jit(solution)/shard_map/ppermute | solution.py:479
  10.5 1.2 collective-permute-start.3
  11.7 34.4 %copy-start.3 = (s32[1,16384]{1,0:T(1,128)S(1)}, s32[1,16384]{1,0:T(1,128)}, u32[]{:S(2)}) copy-start(s32[1,16384]{1,0:T(1,128)} %param.18) | copy-start | bytes 196612
  11.7 34.4 %copy-start.4 = (f32[6,2048]{1,0:T(8,128)S(1)}, f32[6,2048]{1,0:T(8,128)}, u32[]{:S(2)}) copy-start(f32[6,2048]{1,0:T(8,128)} %target.1) | copy-start | bytes 147460
  73.7 2.7 %collective-permute-start.4 = (f32[16,128]{1,0:T(8,128)S(1)}, f32[16,128]{1,0:T(8,128)S(1)}, u32[]{:S(2)}, u32[]{:S(2)}) collective-permute-start(f32[16,128]{1,0:T(8,128)S(1)} %get-tuple-element.46), channel_id=1, source_target_pairs={{0,16},{32,48},{64,80},{96,112},{16,0},{48,32},{80,64},{112,96},{1... | collective-permute-start | bytes 24584 | tf_op jit(solution)/shard_map/ppermute | solution.py:479
  74.3 5.1 %collective-permute-start.5 = (f32[16,128]{1,0:T(8,128)S(1)}, f32[16,128]{1,0:T(8,128)S(1)}, u32[]{:S(2)}, u32[]{:S(2)}) collective-permute-start(f32[16,128]{1,0:T(8,128)S(1)} %get-tuple-element.47), channel_id=1, source_target_pairs={{16,32},{48,64},{80,96},{32,16},{64,48},{96,80},{17,33},{49,65},{8... | collective-permute-start | bytes 24584 | tf_op jit(solution)/shard_map/ppermute | solution.py:479
  80.0 3.3 %collective-permute-start.6 = (f32[2,96]{1,0:T(2,128)S(1)}, f32[2,96]{1,0:T(2,128)S(1)}, u32[]{:S(2)}, u32[]{:S(2)}) collective-permute-start(f32[2,96]{1,0:T(2,128)S(1)} %get-tuple-element.49), channel_id=1, source_target_pairs={{0,1},{2,3},{4,5},{6,7},{8,9},{10,11},{12,13},{14,15},{1,0},{3,2},... | collective-permute-start | bytes 2312 | tf_op jit(solution)/shard_map/ppermute | solution.py:479
  80.4 2.9 %collective-permute-start.7 = (f32[2,96]{1,0:T(2,128)S(1)}, f32[2,96]{1,0:T(2,128)S(1)}, u32[]{:S(2)}, u32[]{:S(2)}) collective-permute-start(f32[2,96]{1,0:T(2,128)S(1)} %get-tuple-element.50), channel_id=1, source_target_pairs={{1,2},{3,4},{5,6},{7,8},{9,10},{11,12},{13,14},{2,1},{4,3},{6,5},{... | collective-permute-start | bytes 2312 | tf_op jit(solution)/shard_map/ppermute | solution.py:479
  90.9 2.4 %collective-permute-start.8 = (bf16[3072,128]{1,0:T(8,128)(2,1)S(1)}, bf16[3072,128]{1,0:T(8,128)(2,1)S(1)}, u32[]{:S(2)}, u32[]{:S(2)}) collective-permute-start(bf16[3072,128]{1,0:T(8,128)(2,1)S(1)} %slice.15), channel_id=1, source_target_pairs={{0,16},{16,0},{32,48},{48,32},{64,80},{80,64},{96,112},{112,96},{1... | collective-permute-start | bytes 2359304 | tf_op jit(solution)/shard_map/ppermute | solution.py:610
  136.4 4.8 %collective-permute-start.9 = (bf16[3072,128]{1,0:T(8,128)(2,1)S(1)}, bf16[3072,128]{1,0:T(8,128)(2,1)S(1)}, u32[]{:S(2)}, u32[]{:S(2)}) collective-permute-start(bf16[3072,128]{1,0:T(8,128)(2,1)S(1)} %bitcast.31), channel_id=1, source_target_pairs={{0,16},{16,0},{32,48},{48,32},{64,80},{80,64},{96,112},{112,96},{1... | collective-permute-start | bytes 2359304 | tf_op jit(solution)/shard_map/ppermute | solution.py:614

commit v6 on v4

--- a/solution.py
+++ b/solution.py
@@ -198,7 +198,7 @@
             pf[pl.ds(ob * 64 + v, 8, stride=8), :] = sums[v]
         return carry
 
-    lax.fori_loop(0, 16, owners, 0)
+    lax.fori_loop(0, 16, owners, 0, unroll=8)
     out[...] = pf[...].astype(BF)
 
 
@@ -250,14 +250,17 @@
     one = jnp.ones((16, 128), BF)
     lefts, rights = (l0, l1), (r0, r1)
 
-    def collect(tb, slot):
-        left, right = lefts[slot], rights[slot]
+    def collect(group, slot):
+        for q in range(4):
+            collect_eight(group * 4 + q, q * 1024, lefts[slot], rights[slot])
+
+    def collect_eight(tb, start, left, right):
         block = recv[pl.ds(pl.multiple_of(tb * 64, 64), 64), :].astype(F32)
         index = obs[pl.ds(pl.multiple_of(tb * 8, 8), 8), :]
         low = (index & 127).astype(F32)
         high = (index >> 7).astype(F32)
         for i in range(8):
-            at = slice(i * 128, i * 128 + 128)
+            at = slice(start + i * 128, start + i * 128 + 128)
             here = spread_row(high[i : i + 1]) == steps[0]
             for v in range(6):
                 value = spread_row(block[i * 8 + v : i * 8 + v + 1])
@@ -270,7 +273,7 @@
         total[...] += dot(lefts[slot][...], rights[slot][...], NT)
 
     total[...] = jnp.zeros_like(total)
-    overlapped(16, collect, multiply)
+    overlapped(4, collect, multiply)
     scale = 1.0 / (6 * 2048)
     squares = jnp.zeros((6, 128), F32)
     resids = []
@@ -306,7 +309,7 @@
             gf[pl.ds(tb * 64 + v + 3, 8, stride=8), :] = y * down
         return carry
 
-    lax.fori_loop(0, 16, choose, 0)
+    lax.fori_loop(0, 16, choose, 0, unroll=8)
     out[...] = gf[...].astype(BF)
 
 
@@ -319,8 +322,11 @@
     total[...] = jnp.zeros_like(total)
     lane = lax.broadcasted_iota(I32, (8, 128), 1)
 
-    def owners(ob, slot):
-        left, right = lefts[slot], rights[slot]
+    def owners(group, slot):
+        for q in range(2):
+            owners_eight(group * 2 + q, q * 4096, lefts[slot], rights[slot])
+
+    def owners_eight(ob, start, left, right):
         rows = pl.ds(pl.multiple_of(ob * 8, 8), 8)
         live = lane < cnt[rows, 0:1]
         block = grad[pl.ds(pl.multiple_of(ob * 64, 64), 64), :].astype(F32)
@@ -331,7 +337,7 @@
         for i in range(8):
             values = [spread_row(block[i * 8 + v : i * 8 + v + 1]) for v in range(6)]
             for k in range(4):
-                at = slice((i * 4 + k) * 128, (i * 4 + k) * 128 + 128)
+                at = slice(start + (i * 4 + k) * 128, start + (i * 4 + k) * 128 + 128)
                 here = spread_row(high[k][i : i + 1]) == steps[0]
                 for v in range(6):
                     left[v * 16 : v * 16 + 16, at] = jnp.where(here, values[v], none)
@@ -343,7 +349,7 @@
     def multiply(slot):
         total[...] += dot(lefts[slot][...], rights[slot][...], NT)
 
-    overlapped(16, owners, multiply)
+    overlapped(8, owners, multiply)
     out[...] = jnp.zeros_like(out)
     for r in range(8):
         even = total[pl.ds(2 * r, 6, stride=16), :]
@@ -560,22 +566,22 @@
         owner_kernel,
         [((6, 2048), F32), ((16, 128), F32), ((1024, 128), BF)],
         [
-            ((96, 1024), BF), ((96, 1024), BF), ((128, 1024), BF), ((128, 1024), BF),
+            ((96, 4096), BF), ((96, 4096), BF), ((128, 4096), BF), ((128, 4096), BF),
             ((96, 128), F32), ((128, 128), I32), ((1024, 128), F32),
         ],
         received, obs, targets,
-        vmem=8, flops=10**9,
+        vmem=12, flops=10**9,
     )
     grads = exchange(back)
     g_field, one, two = call(
         spread_kernel,
         [((64, 128), F32), ((16, 128), F32), ((16, 128), F32)],
         [
-            ((96, 4096), BF), ((96, 4096), BF), ((64, 4096), BF), ((64, 4096), BF),
+            ((96, 8192), BF), ((96, 8192), BF), ((64, 8192), BF), ((64, 8192), BF),
             ((96, 64), F32),
         ],
         flags, grads, cells, wts, cnt,
-        smem=1, vmem=12, flops=10**9,
+        smem=1, vmem=16, flops=10**9,
     )
     one, two = swaps(one, two, "ns")
     et, one, two = call(

time: 147 us -> 143 us (0.973)
  Pallas kernels: 35.9 us -> 32.6 us
    pallas_call x9, Pallas kernels: 35.9 us -> 32.6 us  [call(): pl.pallas_call(kernel, out_shape=[jax.ShapeDtypeStruct(s, d) for s, d in...]
where the time goes in v6:
time: 143 us
  blocking collectives  84.8 us (59%)
  Pallas kernels  32.6 us (23%)
  starting transfers between devices  13.6 us (10%)
  waiting for transfers between devices  8.16 us (6%)
    all_to_all x4, blocking collectives, exchange(): lax.all_to_all(rows, AXES, split_axis=0, concat_axis=0, tiled=True, axis_...  84.8 us
    pallas_call x9, Pallas kernels, call(): pl.pallas_call(kernel, out_shape=[jax.ShapeDtypeStruct(s, d) for s, d in...  32.6 us
    ppermute x8, starting transfers between devices, swaps(): lax.ppermute(x, axis, p + [(j, i) for i, j in p])  10.7 us
    ppermute x8, waiting for transfers between devices, swaps(): lax.ppermute(x, axis, p + [(j, i) for i, j in p])  3.97 us
    ppermute x1, starting transfers between devices, on_device(): other = lax.ppermute(mine, 'ns', pairs)  2.87 us
  transfers between devices with their start and end apart: 10, of which 5 were waited for; matrix products, arithmetic and copies ran while one was open for 0% of the time, Pallas kernels for 2%

profile of v6, /device:TPU:1, one launch (start us, length us, event | category | flops | bytes accessed | tf_op | source)
XLA Modules:
  0.0 143.1 jit_solution(3391687006467258829)
XLA Ops:
  0.6 1.1 broadcast_select_fusion
  1.7 1.5 %collective-permute-start = (bf16[128,128]{1,0:T(8,128)(2,1)S(1)}, bf16[128,128]{1,0:T(8,128)(2,1)S(1)}, u32[]{:S(2)}, u32[]{:S(2)}) collective-permute-start(bf16[128,128]{1,0:T(8,128)(2,1)S(1)} %bitcast.47), channel_id=1, source_target_pairs={{0,16},{32,48},{64,80},{96,112},{16,0},{48,32},{80,64},{112,96},{1... | collective-permute-start | bytes 98312 | tf_op jit(solution)/shard_map/ppermute | solution.py:479
  3.2 3.2 %collective-permute-start.1 = (bf16[128,128]{1,0:T(8,128)(2,1)S(1)}, bf16[128,128]{1,0:T(8,128)(2,1)S(1)}, u32[]{:S(2)}, u32[]{:S(2)}) collective-permute-start(bf16[128,128]{1,0:T(8,128)(2,1)S(1)} %bitcast.46), channel_id=1, source_target_pairs={{16,32},{48,64},{80,96},{32,16},{64,48},{96,80},{17,33},{49,65},{8... | collective-permute-start | bytes 98312 | tf_op jit(solution)/shard_map/ppermute | solution.py:479
  6.4 0.9 copy-done
  7.3 0.2 shard_map.153
  7.7 0.8 collective-permute-done.1.swap2
  8.5 0.7 shard_map.154
  9.1 1.4 collective-permute-start.2
  10.5 0.6 collective-permute-start.3
  11.2 0.1 copy.17.cnt
  11.4 0.3 collective-permute-done.2.swap1
  11.8 7.4 %shard_map.155 = (bf16[1024,128]{1,0:T(8,128)(2,1)S(1)}, bf16[1440,256]{1,0:T(8,128)(2,1)S(1)}, bf16[1440,256]{1,0:T(8,128)(2,1)S(1)}, bf16[1024,256]{1,0:T(8,128)(2,1)S(1)}) custom-call(f32[6]{0:T(128)S(1)} %convert_element_type.20.flags, bf16[1024,64]{1,0:T(8,128)(2,1)S(1)} %get-tuple-element.36.fto, bf16[512,64]{1,0:T(8,128)(2,1)S(1)} %get-tuple-element.39.ftr, ...), custom_call_target="tpu_custom_call" | custom-call | flops 2000000000 | bytes 4000000 | tf_op jit(solution)/shard_map/pallas_call | solution.py:491
  19.1 26.9 %all_to_all.32 = bf16[128,8,128]{2,1,0:T(8,128)(2,1)S(1)} all-to-all(bf16[128,8,128]{2,1,0:T(8,128)(2,1)S(1)} %bitcast.38), channel_id=1, replica_groups=mesh['ns'=8,'ew'=16] {'ns','ew'}, dimensions={0} | all-to-all | bytes 524288 | tf_op jit(solution)/shard_map/all_to_all | solution.py:484
  46.0 4.0 %shard_map.156 = (f32[6,2048]{1,0:T(8,128)}, f32[16,128]{1,0:T(8,128)S(1)}, bf16[1024,128]{1,0:T(8,128)(2,1)S(1)}) custom-call(bf16[1024,128]{1,0:T(8,128)(2,1)S(1)} %bitcast.39, s32[128,128]{1,0:T(8,128)S(1)} %bitcast.42, f32[6,2048]{1,0:T(8,128)S(1)} %copy-done.4), custom_call_target="tpu_custom_call" | custom-call | flops 1000000000 | bytes 4000000 | tf_op jit(solution)/shard_map/pallas_call | solution.py:491
  50.1 15.3 %all_to_all.33 = bf16[128,8,128]{2,1,0:T(8,128)(2,1)S(1)} all-to-all(bf16[128,8,128]{2,1,0:T(8,128)(2,1)S(1)} %bitcast.40), channel_id=1, replica_groups=mesh['ns'=8,'ew'=16] {'ns','ew'}, dimensions={0} | all-to-all | bytes 524288 | tf_op jit(solution)/shard_map/all_to_all | solution.py:484
  65.3 7.4 %shard_map.157 = (f32[64,128]{1,0:T(8,128)S(1)}, f32[16,128]{1,0:T(8,128)S(1)}, f32[16,128]{1,0:T(8,128)S(1)}) custom-call(f32[6]{0:T(128)S(1)} %convert_element_type.20.flags, bf16[1024,128]{1,0:T(8,128)(2,1)S(1)} %bitcast.37, s32[4,128,128]{2,1,0:T(8,128)S(1)} %bitcast.34, f32[4,128,128]{2,1,0:T(8,128)S(1)} %bitcast.36, s32[128,1]{1,0:T(8,128)S(1)} %copy.17.cnt), custom_call_target="tpu_custom_call" | custom-call | flops 1000000000 | bytes 4000000 | tf_op jit(solution)/shard_map/pallas_call | solution.py:491
  72.7 0.6 collective-permute-start.4
  73.3 2.2 %collective-permute-start.5 = (f32[16,128]{1,0:T(8,128)S(1)}, f32[16,128]{1,0:T(8,128)S(1)}, u32[]{:S(2)}, u32[]{:S(2)}) collective-permute-start(f32[16,128]{1,0:T(8,128)S(1)} %get-tuple-element.47), channel_id=1, source_target_pairs={{16,32},{48,64},{80,96},{32,16},{64,48},{96,80},{17,33},{49,65},{8... | collective-permute-start | bytes 24584 | tf_op jit(solution)/shard_map/ppermute | solution.py:479
  75.5 2.9 %collective-permute-done.5.swap2 = f32[16,128]{1,0:T(8,128)S(1)} collective-permute-done((f32[16,128]{1,0:T(8,128)S(1)}, f32[16,128]{1,0:T(8,128)S(1)}, u32[]{:S(2)}, u32[]{:S(2)}) %collective-permute-start.5) | collective-permute-done | bytes 8224 | tf_op jit(solution)/shard_map/ppermute | solution.py:479
  78.4 0.6 shard_map.158
  79.0 0.4 collective-permute-start.6
  79.4 0.8 collective-permute-start.7
  80.3 2.1 %shard_map.159 = (bf16[576,1280]{1,0:T(8,128)(2,1)S(1)}, bf16[576,1280]{1,0:T(8,128)(2,1)S(1)}) custom-call(f32[6]{0:T(128)S(1)} %convert_element_type.20.flags, bf16[1440,256]{1,0:T(8,128)(2,1)S(1)} %get-tuple-element.52.a1, bf16[1024,64]{1,0:T(8,128)(2,1)S(1)} %get-tuple-element.36.fto, bf16[512,64]{1,0:T(8,128)(2,1)S(1)} %get-tuple-element.39.ftr, ...), custom_call_target="tpu_custom_call" | custom-call | flops 1000000000 | bytes 4000000 | tf_op jit(solution)/shard_map/pallas_call | solution.py:491
  82.4 7.5 %shard_map.160 = (bf16[6144,128]{1,0:T(8,128)(2,1)S(1)}, f32[512,128]{1,0:T(8,128)}) custom-call(f32[6]{0:T(128)S(1)} %convert_element_type.20.flags, f32[64,128]{1,0:T(8,128)S(1)} %get-tuple-element.45.gf, f32[128,96]{1,0:T(8,128)S(1)} %get-tuple-element.48.et, f32[2,96]{1,0:T(2,128)S(1)} %collective-permute-done.6.swap1, ...), custom_call_target="tpu_custom_call" | custom-call | flops 2000000000 | bytes 4000000 | tf_op jit(solution)/shard_map/pallas_call | solution.py:491
  90.1 2.3 %collective-permute-done.8 = bf16[3072,128]{1,0:T(8,128)(2,1)S(1)} collective-permute-done((bf16[3072,128]{1,0:T(8,128)(2,1)S(1)}, bf16[3072,128]{1,0:T(8,128)(2,1)S(1)}, u32[]{:S(2)}, u32[]{:S(2)}) %collective-permute-start.8) | collective-permute-done | bytes 786464 | tf_op jit(solution)/shard_map/ppermute | solution.py:608
  92.3 0.2 add_convert_fusion
  92.6 24.1 %all_to_all.34 = bf16[64,48,128]{2,1,0:T(8,128)(2,1)S(1)} all-to-all(bf16[64,48,128]{2,1,0:T(8,128)(2,1)S(1)} %bitcast.43), channel_id=1, replica_groups={{0,1,2,3,4,5,6,7,8,9,10,11,12,13,14,15,32,33,34,35,36,37,38,39,40,41,42..., dimensions={0} | all-to-all | bytes 1572864 | tf_op jit(solution)/shard_map/all_to_all | solution.py:484
  116.6 0.1 reduce_sum.12
  116.9 18.6 %all_to_all.35 = bf16[64,48,128]{2,1,0:T(8,128)(2,1)S(1)} all-to-all(bf16[64,48,128]{2,1,0:T(8,128)(2,1)S(1)} %broadcast_in_dim.2), channel_id=1, replica_groups={{0,1,2,3,4,5,6,7,8,9,10,11,12,13,14,15,32,33,34,35,36,37,38,39,40,41,42..., dimensions={0} | all-to-all | bytes 1572864 | tf_op jit(solution)/shard_map/all_to_all | solution.py:484
  135.5 2.9 %collective-permute-start.9 = (bf16[3072,128]{1,0:T(8,128)(2,1)S(1)}, bf16[3072,128]{1,0:T(8,128)(2,1)S(1)}, u32[]{:S(2)}, u32[]{:S(2)}) collective-permute-start(bf16[3072,128]{1,0:T(8,128)(2,1)S(1)} %bitcast.31), channel_id=1, source_target_pairs={{0,16},{16,0},{32,48},{48,32},{64,80},{80,64},{96,112},{112,96},{1... | collective-permute-start | bytes 2359304 | tf_op jit(solution)/shard_map/ppermute | solution.py:612
  138.3 1.9 %collective-permute-done.9.other = bf16[3072,128]{1,0:T(8,128)(2,1)S(1)} collective-permute-done((bf16[3072,128]{1,0:T(8,128)(2,1)S(1)}, bf16[3072,128]{1,0:T(8,128)(2,1)S(1)}, u32[]{:S(2)}, u32[]{:S(2)}) %collective-permute-start.9) | collective-permute-done | bytes 786464 | tf_op jit(solution)/shard_map/ppermute | solution.py:612
  140.2 2.7 %shard_map.161 = (f32[3,3,192,192]{3,2,1,0:T(8,128)}, f32[3,3,192,192]{3,2,1,0:T(8,128)}, f32[64,192]{1,0:T(8,128)}, f32[6,192]{1,0:T(8,128)}, f32[1,1]{1,0:T(1,128)}) custom-call(f32[6]{0:T(128)S(1)} %convert_element_type.20.flags, bf16[3072,128]{1,0:T(8,128)(2,1)S(1)} %bitcast.32, bf16[3072,128]{1,0:T(8,128)(2,1)S(1)} %collective-permute-done.9.other), custom_call_target="tpu_custom_call" | custom-call | bytes 4000000 | tf_op jit(solution)/shard_map/pallas_call | solution.py:491
  (33 shorter events, 0.5 us)
Async XLA Ops:
  1.7 6.0 %collective-permute-start = (bf16[128,128]{1,0:T(8,128)(2,1)S(1)}, bf16[128,128]{1,0:T(8,128)(2,1)S(1)}, u32[]{:S(2)}, u32[]{:S(2)}) collective-permute-start(bf16[128,128]{1,0:T(8,128)(2,1)S(1)} %bitcast.47), channel_id=1, source_target_pairs={{0,16},{32,48},{64,80},{96,112},{16,0},{48,32},{80,64},{112,96},{1... | collective-permute-start | bytes 98312 | tf_op jit(solution)/shard_map/ppermute | solution.py:479
  3.2 5.2 %collective-permute-start.1 = (bf16[128,128]{1,0:T(8,128)(2,1)S(1)}, bf16[128,128]{1,0:T(8,128)(2,1)S(1)}, u32[]{:S(2)}, u32[]{:S(2)}) collective-permute-start(bf16[128,128]{1,0:T(8,128)(2,1)S(1)} %bitcast.46), channel_id=1, source_target_pairs={{16,32},{48,64},{80,96},{32,16},{64,48},{96,80},{17,33},{49,65},{8... | collective-permute-start | bytes 98312 | tf_op jit(solution)/shard_map/ppermute | solution.py:479
  6.4 0.9 copy-start
  8.4 2.8 %copy-start.7 = (bf16[64,192]{1,0:T(8,128)(2,1)S(1)}, bf16[64,192]{1,0:T(8,128)(2,1)}, u32[]{:S(2)}) copy-start(bf16[64,192]{1,0:T(8,128)(2,1)} %param.11) | copy-start | bytes 73732
  8.4 2.8 %copy-start.8 = (bf16[192,6]{0,1:T(8,128)(2,1)S(1)}, bf16[192,6]{0,1:T(8,128)(2,1)}, u32[]{:S(2)}) copy-start(bf16[192,6]{0,1:T(8,128)(2,1)} %param.14) | copy-start | bytes 6916
  8.4 2.8 %copy-start.9 = (s32[1,128]{1,0:T(1,128)S(1)}, s32[1,128]{1,0:T(1,128)}, u32[]{:S(2)}) copy-start(s32[1,128]{1,0:T(1,128)} %param.17) | copy-start | bytes 1540
  8.4 2.9 %copy-start.5 = (s32[1,4,16384]{2,1,0:T(4,128)S(1)}, s32[1,4,16384]{2,1,0:T(4,128)}, u32[]{:S(2)}) copy-start(s32[1,4,16384]{2,1,0:T(4,128)} %param.15) | copy-start | bytes 786436
  8.4 2.9 %copy-start.6 = (f32[1,4,16384]{2,1,0:T(4,128)S(1)}, f32[1,4,16384]{2,1,0:T(4,128)}, u32[]{:S(2)}) copy-start(f32[1,4,16384]{2,1,0:T(4,128)} %param.16) | copy-start | bytes 786436
  8.4 3.3 %copy-start.1 = (bf16[3,3,192,192]{3,2,1,0:T(8,128)(2,1)S(1)}, bf16[3,3,192,192]{3,2,1,0:T(8,128)(2,1)}, u32[]{:S(2)}) copy-start(bf16[3,3,192,192]{3,2,1,0:T(8,128)(2,1)} %c1.3) | copy-start | bytes 1990660
  8.5 3.3 %copy-start.2 = (bf16[3,3,192,192]{3,2,1,0:T(8,128)(2,1)S(1)}, bf16[3,3,192,192]{3,2,1,0:T(8,128)(2,1)}, u32[]{:S(2)}) copy-start(bf16[3,3,192,192]{3,2,1,0:T(8,128)(2,1)} %c2.3) | copy-start | bytes 1990660
  9.1 2.6 %collective-permute-start.2 = (bf16[32,64]{1,0:T(8,128)(2,1)S(1)}, bf16[32,64]{1,0:T(8,128)(2,1)S(1)}, u32[]{:S(2)}, u32[]{:S(2)}) collective-permute-start(bf16[32,64]{1,0:T(8,128)(2,1)S(1)} %get-tuple-element.40), channel_id=1, source_target_pairs={{0,1},{2,3},{4,5},{6,7},{8,9},{10,11},{12,13},{14,15},{1,0},{3,2},... | collective-permute-start | bytes 12296 | tf_op jit(solution)/shard_map/ppermute | solution.py:479
  10.5 1.2 collective-permute-start.3
  11.7 34.3 %copy-start.3 = (s32[1,16384]{1,0:T(1,128)S(1)}, s32[1,16384]{1,0:T(1,128)}, u32[]{:S(2)}) copy-start(s32[1,16384]{1,0:T(1,128)} %param.18) | copy-start | bytes 196612
  11.7 34.3 %copy-start.4 = (f32[6,2048]{1,0:T(8,128)S(1)}, f32[6,2048]{1,0:T(8,128)}, u32[]{:S(2)}) copy-start(f32[6,2048]{1,0:T(8,128)} %target.1) | copy-start | bytes 147460
  72.7 2.7 %collective-permute-start.4 = (f32[16,128]{1,0:T(8,128)S(1)}, f32[16,128]{1,0:T(8,128)S(1)}, u32[]{:S(2)}, u32[]{:S(2)}) collective-permute-start(f32[16,128]{1,0:T(8,128)S(1)} %get-tuple-element.46), channel_id=1, source_target_pairs={{0,16},{32,48},{64,80},{96,112},{16,0},{48,32},{80,64},{112,96},{1... | collective-permute-start | bytes 24584 | tf_op jit(solution)/shard_map/ppermute | solution.py:479
  73.3 5.1 %collective-permute-start.5 = (f32[16,128]{1,0:T(8,128)S(1)}, f32[16,128]{1,0:T(8,128)S(1)}, u32[]{:S(2)}, u32[]{:S(2)}) collective-permute-start(f32[16,128]{1,0:T(8,128)S(1)} %get-tuple-element.47), channel_id=1, source_target_pairs={{16,32},{48,64},{80,96},{32,16},{64,48},{96,80},{17,33},{49,65},{8... | collective-permute-start | bytes 24584 | tf_op jit(solution)/shard_map/ppermute | solution.py:479
  79.0 3.3 %collective-permute-start.6 = (f32[2,96]{1,0:T(2,128)S(1)}, f32[2,96]{1,0:T(2,128)S(1)}, u32[]{:S(2)}, u32[]{:S(2)}) collective-permute-start(f32[2,96]{1,0:T(2,128)S(1)} %get-tuple-element.49), channel_id=1, source_target_pairs={{0,1},{2,3},{4,5},{6,7},{8,9},{10,11},{12,13},{14,15},{1,0},{3,2},... | collective-permute-start | bytes 2312 | tf_op jit(solution)/shard_map/ppermute | solution.py:479
  79.4 2.9 %collective-permute-start.7 = (f32[2,96]{1,0:T(2,128)S(1)}, f32[2,96]{1,0:T(2,128)S(1)}, u32[]{:S(2)}, u32[]{:S(2)}) collective-permute-start(f32[2,96]{1,0:T(2,128)S(1)} %get-tuple-element.50), channel_id=1, source_target_pairs={{1,2},{3,4},{5,6},{7,8},{9,10},{11,12},{13,14},{2,1},{4,3},{6,5},{... | collective-permute-start | bytes 2312 | tf_op jit(solution)/shard_map/ppermute | solution.py:479
  90.0 2.4 %collective-permute-start.8 = (bf16[3072,128]{1,0:T(8,128)(2,1)S(1)}, bf16[3072,128]{1,0:T(8,128)(2,1)S(1)}, u32[]{:S(2)}, u32[]{:S(2)}) collective-permute-start(bf16[3072,128]{1,0:T(8,128)(2,1)S(1)} %slice.15), channel_id=1, source_target_pairs={{0,16},{16,0},{32,48},{48,32},{64,80},{80,64},{96,112},{112,96},{1... | collective-permute-start | bytes 2359304 | tf_op jit(solution)/shard_map/ppermute | solution.py:608
  135.5 4.8 %collective-permute-start.9 = (bf16[3072,128]{1,0:T(8,128)(2,1)S(1)}, bf16[3072,128]{1,0:T(8,128)(2,1)S(1)}, u32[]{:S(2)}, u32[]{:S(2)}) collective-permute-start(bf16[3072,128]{1,0:T(8,128)(2,1)S(1)} %bitcast.31), channel_id=1, source_target_pairs={{0,16},{16,0},{32,48},{48,32},{64,80},{80,64},{96,112},{112,96},{1... | collective-permute-start | bytes 2359304 | tf_op jit(solution)/shard_map/ppermute | solution.py:612

commit v7 on v6

--- a/solution.py
+++ b/solution.py
@@ -323,8 +323,8 @@
     lane = lax.broadcasted_iota(I32, (8, 128), 1)
 
     def owners(group, slot):
-        for q in range(2):
-            owners_eight(group * 2 + q, q * 4096, lefts[slot], rights[slot])
+        for q in range(4):
+            owners_eight(group * 4 + q, q * 4096, lefts[slot], rights[slot])
 
     def owners_eight(ob, start, left, right):
         rows = pl.ds(pl.multiple_of(ob * 8, 8), 8)
@@ -349,7 +349,7 @@
     def multiply(slot):
         total[...] += dot(lefts[slot][...], rights[slot][...], NT)
 
-    overlapped(8, owners, multiply)
+    overlapped(4, owners, multiply)
     out[...] = jnp.zeros_like(out)
     for r in range(8):
         even = total[pl.ds(2 * r, 6, stride=16), :]
@@ -577,11 +577,11 @@
         spread_kernel,
         [((64, 128), F32), ((16, 128), F32), ((16, 128), F32)],
         [
-            ((96, 8192), BF), ((96, 8192), BF), ((64, 8192), BF), ((64, 8192), BF),
+            ((96, 16384), BF), ((96, 16384), BF), ((64, 16384), BF), ((64, 16384), BF),
             ((96, 64), F32),
         ],
         flags, grads, cells, wts, cnt,
-        smem=1, vmem=16, flops=10**9,
+        smem=1, vmem=20, flops=10**9,
     )
     one, two = swaps(one, two, "ns")
     et, one, two = call(

time: 143 us -> 143 us (level)
  no operation moved by 1% of the time
where the time goes in v7:
time: 143 us
  blocking collectives  85 us (59%)
  Pallas kernels  32.4 us (23%)
  starting transfers between devices  13.4 us (9%)
  waiting for transfers between devices  8.16 us (6%)
    all_to_all x4, blocking collectives, exchange(): lax.all_to_all(rows, AXES, split_axis=0, concat_axis=0, tiled=True, axis_...  85 us
    pallas_call x9, Pallas kernels, call(): pl.pallas_call(kernel, out_shape=[jax.ShapeDtypeStruct(s, d) for s, d in...  32.4 us
    ppermute x8, starting transfers between devices, swaps(): lax.ppermute(x, axis, p + [(j, i) for i, j in p])  10.5 us
    ppermute x8, waiting for transfers between devices, swaps(): lax.ppermute(x, axis, p + [(j, i) for i, j in p])  3.97 us
    ppermute x1, starting transfers between devices, on_device(): other = lax.ppermute(mine, 'ns', pairs)  2.87 us
  transfers between devices with their start and end apart: 10, of which 5 were waited for; matrix products, arithmetic and copies ran while one was open for 0% of the time, Pallas kernels for 2%

profile of v7, /device:TPU:1, one launch (start us, length us, event | category | flops | bytes accessed | tf_op | source)
XLA Modules:
  0.0 142.8 jit_solution(16222371222927217112)
XLA Ops:
  0.6 1.1 broadcast_select_fusion
  1.7 1.5 %collective-permute-start = (bf16[128,128]{1,0:T(8,128)(2,1)S(1)}, bf16[128,128]{1,0:T(8,128)(2,1)S(1)}, u32[]{:S(2)}, u32[]{:S(2)}) collective-permute-start(bf16[128,128]{1,0:T(8,128)(2,1)S(1)} %bitcast.47), channel_id=1, source_target_pairs={{0,16},{32,48},{64,80},{96,112},{16,0},{48,32},{80,64},{112,96},{1... | collective-permute-start | bytes 98312 | tf_op jit(solution)/shard_map/ppermute | solution.py:479
  3.2 3.2 %collective-permute-start.1 = (bf16[128,128]{1,0:T(8,128)(2,1)S(1)}, bf16[128,128]{1,0:T(8,128)(2,1)S(1)}, u32[]{:S(2)}, u32[]{:S(2)}) collective-permute-start(bf16[128,128]{1,0:T(8,128)(2,1)S(1)} %bitcast.46), channel_id=1, source_target_pairs={{16,32},{48,64},{80,96},{32,16},{64,48},{96,80},{17,33},{49,65},{8... | collective-permute-start | bytes 98312 | tf_op jit(solution)/shard_map/ppermute | solution.py:479
  6.4 0.9 copy-done
  7.3 0.2 shard_map.153
  7.7 0.8 collective-permute-done.1.swap2
  8.5 0.7 shard_map.154
  9.1 1.4 collective-permute-start.2
  10.5 0.6 collective-permute-start.3
  11.2 0.1 copy.17.cnt
  11.4 0.3 collective-permute-done.2.swap1
  11.8 7.4 %shard_map.155 = (bf16[1024,128]{1,0:T(8,128)(2,1)S(1)}, bf16[1440,256]{1,0:T(8,128)(2,1)S(1)}, bf16[1440,256]{1,0:T(8,128)(2,1)S(1)}, bf16[1024,256]{1,0:T(8,128)(2,1)S(1)}) custom-call(f32[6]{0:T(128)S(1)} %convert_element_type.20.flags, bf16[1024,64]{1,0:T(8,128)(2,1)S(1)} %get-tuple-element.36.fto, bf16[512,64]{1,0:T(8,128)(2,1)S(1)} %get-tuple-element.39.ftr, ...), custom_call_target="tpu_custom_call" | custom-call | flops 2000000000 | bytes 4000000 | tf_op jit(solution)/shard_map/pallas_call | solution.py:491
  19.1 26.9 %all_to_all.32 = bf16[128,8,128]{2,1,0:T(8,128)(2,1)S(1)} all-to-all(bf16[128,8,128]{2,1,0:T(8,128)(2,1)S(1)} %bitcast.38), channel_id=1, replica_groups=mesh['ns'=8,'ew'=16] {'ns','ew'}, dimensions={0} | all-to-all | bytes 524288 | tf_op jit(solution)/shard_map/all_to_all | solution.py:484
  46.0 4.0 %shard_map.156 = (f32[6,2048]{1,0:T(8,128)}, f32[16,128]{1,0:T(8,128)S(1)}, bf16[1024,128]{1,0:T(8,128)(2,1)S(1)}) custom-call(bf16[1024,128]{1,0:T(8,128)(2,1)S(1)} %bitcast.39, s32[128,128]{1,0:T(8,128)S(1)} %bitcast.42, f32[6,2048]{1,0:T(8,128)S(1)} %copy-done.4), custom_call_target="tpu_custom_call" | custom-call | flops 1000000000 | bytes 4000000 | tf_op jit(solution)/shard_map/pallas_call | solution.py:491
  50.1 15.3 %all_to_all.33 = bf16[128,8,128]{2,1,0:T(8,128)(2,1)S(1)} all-to-all(bf16[128,8,128]{2,1,0:T(8,128)(2,1)S(1)} %bitcast.40), channel_id=1, replica_groups=mesh['ns'=8,'ew'=16] {'ns','ew'}, dimensions={0} | all-to-all | bytes 524288 | tf_op jit(solution)/shard_map/all_to_all | solution.py:484
  65.3 7.2 %shard_map.157 = (f32[64,128]{1,0:T(8,128)S(1)}, f32[16,128]{1,0:T(8,128)S(1)}, f32[16,128]{1,0:T(8,128)S(1)}) custom-call(f32[6]{0:T(128)S(1)} %convert_element_type.20.flags, bf16[1024,128]{1,0:T(8,128)(2,1)S(1)} %bitcast.37, s32[4,128,128]{2,1,0:T(8,128)S(1)} %bitcast.34, f32[4,128,128]{2,1,0:T(8,128)S(1)} %bitcast.36, s32[128,1]{1,0:T(8,128)S(1)} %copy.17.cnt), custom_call_target="tpu_custom_call" | custom-call | flops 1000000000 | bytes 4000000 | tf_op jit(solution)/shard_map/pallas_call | solution.py:491
  72.5 0.6 collective-permute-start.4
  73.1 2.2 %collective-permute-start.5 = (f32[16,128]{1,0:T(8,128)S(1)}, f32[16,128]{1,0:T(8,128)S(1)}, u32[]{:S(2)}, u32[]{:S(2)}) collective-permute-start(f32[16,128]{1,0:T(8,128)S(1)} %get-tuple-element.47), channel_id=1, source_target_pairs={{16,32},{48,64},{80,96},{32,16},{64,48},{96,80},{17,33},{49,65},{8... | collective-permute-start | bytes 24584 | tf_op jit(solution)/shard_map/ppermute | solution.py:479
  75.3 2.9 %collective-permute-done.5.swap2 = f32[16,128]{1,0:T(8,128)S(1)} collective-permute-done((f32[16,128]{1,0:T(8,128)S(1)}, f32[16,128]{1,0:T(8,128)S(1)}, u32[]{:S(2)}, u32[]{:S(2)}) %collective-permute-start.5) | collective-permute-done | bytes 8224 | tf_op jit(solution)/shard_map/ppermute | solution.py:479
  78.2 0.6 shard_map.158
  78.8 0.4 collective-permute-start.6
  79.2 0.6 collective-permute-start.7
  79.9 2.1 %shard_map.159 = (bf16[576,1280]{1,0:T(8,128)(2,1)S(1)}, bf16[576,1280]{1,0:T(8,128)(2,1)S(1)}) custom-call(f32[6]{0:T(128)S(1)} %convert_element_type.20.flags, bf16[1440,256]{1,0:T(8,128)(2,1)S(1)} %get-tuple-element.52.a1, bf16[1024,64]{1,0:T(8,128)(2,1)S(1)} %get-tuple-element.36.fto, bf16[512,64]{1,0:T(8,128)(2,1)S(1)} %get-tuple-element.39.ftr, ...), custom_call_target="tpu_custom_call" | custom-call | flops 1000000000 | bytes 4000000 | tf_op jit(solution)/shard_map/pallas_call | solution.py:491
  82.0 7.5 %shard_map.160 = (bf16[6144,128]{1,0:T(8,128)(2,1)S(1)}, f32[512,128]{1,0:T(8,128)}) custom-call(f32[6]{0:T(128)S(1)} %convert_element_type.20.flags, f32[64,128]{1,0:T(8,128)S(1)} %get-tuple-element.45.gf, f32[128,96]{1,0:T(8,128)S(1)} %get-tuple-element.48.et, f32[2,96]{1,0:T(2,128)S(1)} %collective-permute-done.6.swap1, ...), custom_call_target="tpu_custom_call" | custom-call | flops 2000000000 | bytes 4000000 | tf_op jit(solution)/shard_map/pallas_call | solution.py:491
  89.7 2.3 %collective-permute-done.8 = bf16[3072,128]{1,0:T(8,128)(2,1)S(1)} collective-permute-done((bf16[3072,128]{1,0:T(8,128)(2,1)S(1)}, bf16[3072,128]{1,0:T(8,128)(2,1)S(1)}, u32[]{:S(2)}, u32[]{:S(2)}) %collective-permute-start.8) | collective-permute-done | bytes 786464 | tf_op jit(solution)/shard_map/ppermute | solution.py:608
  92.0 0.2 add_convert_fusion
  92.2 24.3 %all_to_all.34 = bf16[64,48,128]{2,1,0:T(8,128)(2,1)S(1)} all-to-all(bf16[64,48,128]{2,1,0:T(8,128)(2,1)S(1)} %bitcast.43), channel_id=1, replica_groups={{0,1,2,3,4,5,6,7,8,9,10,11,12,13,14,15,32,33,34,35,36,37,38,39,40,41,42..., dimensions={0} | all-to-all | bytes 1572864 | tf_op jit(solution)/shard_map/all_to_all | solution.py:484
  116.4 0.1 reduce_sum.12
  116.7 18.6 %all_to_all.35 = bf16[64,48,128]{2,1,0:T(8,128)(2,1)S(1)} all-to-all(bf16[64,48,128]{2,1,0:T(8,128)(2,1)S(1)} %broadcast_in_dim.2), channel_id=1, replica_groups={{0,1,2,3,4,5,6,7,8,9,10,11,12,13,14,15,32,33,34,35,36,37,38,39,40,41,42..., dimensions={0} | all-to-all | bytes 1572864 | tf_op jit(solution)/shard_map/all_to_all | solution.py:484
  135.3 2.9 %collective-permute-start.9 = (bf16[3072,128]{1,0:T(8,128)(2,1)S(1)}, bf16[3072,128]{1,0:T(8,128)(2,1)S(1)}, u32[]{:S(2)}, u32[]{:S(2)}) collective-permute-start(bf16[3072,128]{1,0:T(8,128)(2,1)S(1)} %bitcast.31), channel_id=1, source_target_pairs={{0,16},{16,0},{32,48},{48,32},{64,80},{80,64},{96,112},{112,96},{1... | collective-permute-start | bytes 2359304 | tf_op jit(solution)/shard_map/ppermute | solution.py:612
  138.1 1.9 %collective-permute-done.9.other = bf16[3072,128]{1,0:T(8,128)(2,1)S(1)} collective-permute-done((bf16[3072,128]{1,0:T(8,128)(2,1)S(1)}, bf16[3072,128]{1,0:T(8,128)(2,1)S(1)}, u32[]{:S(2)}, u32[]{:S(2)}) %collective-permute-start.9) | collective-permute-done | bytes 786464 | tf_op jit(solution)/shard_map/ppermute | solution.py:612
  140.0 2.7 %shard_map.161 = (f32[3,3,192,192]{3,2,1,0:T(8,128)}, f32[3,3,192,192]{3,2,1,0:T(8,128)}, f32[64,192]{1,0:T(8,128)}, f32[6,192]{1,0:T(8,128)}, f32[1,1]{1,0:T(1,128)}) custom-call(f32[6]{0:T(128)S(1)} %convert_element_type.20.flags, bf16[3072,128]{1,0:T(8,128)(2,1)S(1)} %bitcast.32, bf16[3072,128]{1,0:T(8,128)(2,1)S(1)} %collective-permute-done.9.other), custom_call_target="tpu_custom_call" | custom-call | bytes 4000000 | tf_op jit(solution)/shard_map/pallas_call | solution.py:491
  (33 shorter events, 0.5 us)
Async XLA Ops:
  1.7 6.0 %collective-permute-start = (bf16[128,128]{1,0:T(8,128)(2,1)S(1)}, bf16[128,128]{1,0:T(8,128)(2,1)S(1)}, u32[]{:S(2)}, u32[]{:S(2)}) collective-permute-start(bf16[128,128]{1,0:T(8,128)(2,1)S(1)} %bitcast.47), channel_id=1, source_target_pairs={{0,16},{32,48},{64,80},{96,112},{16,0},{48,32},{80,64},{112,96},{1... | collective-permute-start | bytes 98312 | tf_op jit(solution)/shard_map/ppermute | solution.py:479
  3.2 5.2 %collective-permute-start.1 = (bf16[128,128]{1,0:T(8,128)(2,1)S(1)}, bf16[128,128]{1,0:T(8,128)(2,1)S(1)}, u32[]{:S(2)}, u32[]{:S(2)}) collective-permute-start(bf16[128,128]{1,0:T(8,128)(2,1)S(1)} %bitcast.46), channel_id=1, source_target_pairs={{16,32},{48,64},{80,96},{32,16},{64,48},{96,80},{17,33},{49,65},{8... | collective-permute-start | bytes 98312 | tf_op jit(solution)/shard_map/ppermute | solution.py:479
  6.4 0.9 copy-start
  8.4 2.8 %copy-start.7 = (bf16[64,192]{1,0:T(8,128)(2,1)S(1)}, bf16[64,192]{1,0:T(8,128)(2,1)}, u32[]{:S(2)}) copy-start(bf16[64,192]{1,0:T(8,128)(2,1)} %param.11) | copy-start | bytes 73732
  8.4 2.8 %copy-start.8 = (bf16[192,6]{0,1:T(8,128)(2,1)S(1)}, bf16[192,6]{0,1:T(8,128)(2,1)}, u32[]{:S(2)}) copy-start(bf16[192,6]{0,1:T(8,128)(2,1)} %param.14) | copy-start | bytes 6916
  8.4 2.8 %copy-start.9 = (s32[1,128]{1,0:T(1,128)S(1)}, s32[1,128]{1,0:T(1,128)}, u32[]{:S(2)}) copy-start(s32[1,128]{1,0:T(1,128)} %param.17) | copy-start | bytes 1540
  8.4 2.9 %copy-start.5 = (s32[1,4,16384]{2,1,0:T(4,128)S(1)}, s32[1,4,16384]{2,1,0:T(4,128)}, u32[]{:S(2)}) copy-start(s32[1,4,16384]{2,1,0:T(4,128)} %param.15) | copy-start | bytes 786436
  8.4 2.9 %copy-start.6 = (f32[1,4,16384]{2,1,0:T(4,128)S(1)}, f32[1,4,16384]{2,1,0:T(4,128)}, u32[]{:S(2)}) copy-start(f32[1,4,16384]{2,1,0:T(4,128)} %param.16) | copy-start | bytes 786436
  8.4 3.3 %copy-start.1 = (bf16[3,3,192,192]{3,2,1,0:T(8,128)(2,1)S(1)}, bf16[3,3,192,192]{3,2,1,0:T(8,128)(2,1)}, u32[]{:S(2)}) copy-start(bf16[3,3,192,192]{3,2,1,0:T(8,128)(2,1)} %c1.3) | copy-start | bytes 1990660
  8.5 3.3 %copy-start.2 = (bf16[3,3,192,192]{3,2,1,0:T(8,128)(2,1)S(1)}, bf16[3,3,192,192]{3,2,1,0:T(8,128)(2,1)}, u32[]{:S(2)}) copy-start(bf16[3,3,192,192]{3,2,1,0:T(8,128)(2,1)} %c2.3) | copy-start | bytes 1990660
  9.1 2.6 %collective-permute-start.2 = (bf16[32,64]{1,0:T(8,128)(2,1)S(1)}, bf16[32,64]{1,0:T(8,128)(2,1)S(1)}, u32[]{:S(2)}, u32[]{:S(2)}) collective-permute-start(bf16[32,64]{1,0:T(8,128)(2,1)S(1)} %get-tuple-element.40), channel_id=1, source_target_pairs={{0,1},{2,3},{4,5},{6,7},{8,9},{10,11},{12,13},{14,15},{1,0},{3,2},... | collective-permute-start | bytes 12296 | tf_op jit(solution)/shard_map/ppermute | solution.py:479
  10.5 1.2 collective-permute-start.3
  11.7 34.3 %copy-start.3 = (s32[1,16384]{1,0:T(1,128)S(1)}, s32[1,16384]{1,0:T(1,128)}, u32[]{:S(2)}) copy-start(s32[1,16384]{1,0:T(1,128)} %param.18) | copy-start | bytes 196612
  11.7 34.3 %copy-start.4 = (f32[6,2048]{1,0:T(8,128)S(1)}, f32[6,2048]{1,0:T(8,128)}, u32[]{:S(2)}) copy-start(f32[6,2048]{1,0:T(8,128)} %target.1) | copy-start | bytes 147460
  72.5 2.7 %collective-permute-start.4 = (f32[16,128]{1,0:T(8,128)S(1)}, f32[16,128]{1,0:T(8,128)S(1)}, u32[]{:S(2)}, u32[]{:S(2)}) collective-permute-start(f32[16,128]{1,0:T(8,128)S(1)} %get-tuple-element.46), channel_id=1, source_target_pairs={{0,16},{32,48},{64,80},{96,112},{16,0},{48,32},{80,64},{112,96},{1... | collective-permute-start | bytes 24584 | tf_op jit(solution)/shard_map/ppermute | solution.py:479
  73.1 5.1 %collective-permute-start.5 = (f32[16,128]{1,0:T(8,128)S(1)}, f32[16,128]{1,0:T(8,128)S(1)}, u32[]{:S(2)}, u32[]{:S(2)}) collective-permute-start(f32[16,128]{1,0:T(8,128)S(1)} %get-tuple-element.47), channel_id=1, source_target_pairs={{16,32},{48,64},{80,96},{32,16},{64,48},{96,80},{17,33},{49,65},{8... | collective-permute-start | bytes 24584 | tf_op jit(solution)/shard_map/ppermute | solution.py:479
  78.8 3.2 %collective-permute-start.6 = (f32[2,96]{1,0:T(2,128)S(1)}, f32[2,96]{1,0:T(2,128)S(1)}, u32[]{:S(2)}, u32[]{:S(2)}) collective-permute-start(f32[2,96]{1,0:T(2,128)S(1)} %get-tuple-element.49), channel_id=1, source_target_pairs={{0,1},{2,3},{4,5},{6,7},{8,9},{10,11},{12,13},{14,15},{1,0},{3,2},... | collective-permute-start | bytes 2312 | tf_op jit(solution)/shard_map/ppermute | solution.py:479
  79.2 2.8 %collective-permute-start.7 = (f32[2,96]{1,0:T(2,128)S(1)}, f32[2,96]{1,0:T(2,128)S(1)}, u32[]{:S(2)}, u32[]{:S(2)}) collective-permute-start(f32[2,96]{1,0:T(2,128)S(1)} %get-tuple-element.50), channel_id=1, source_target_pairs={{1,2},{3,4},{5,6},{7,8},{9,10},{11,12},{13,14},{2,1},{4,3},{6,5},{... | collective-permute-start | bytes 2312 | tf_op jit(solution)/shard_map/ppermute | solution.py:479
  89.6 2.4 %collective-permute-start.8 = (bf16[3072,128]{1,0:T(8,128)(2,1)S(1)}, bf16[3072,128]{1,0:T(8,128)(2,1)S(1)}, u32[]{:S(2)}, u32[]{:S(2)}) collective-permute-start(bf16[3072,128]{1,0:T(8,128)(2,1)S(1)} %slice.15), channel_id=1, source_target_pairs={{0,16},{16,0},{32,48},{48,32},{64,80},{80,64},{96,112},{112,96},{1... | collective-permute-start | bytes 2359304 | tf_op jit(solution)/shard_map/ppermute | solution.py:608
  135.3 4.8 %collective-permute-start.9 = (bf16[3072,128]{1,0:T(8,128)(2,1)S(1)}, bf16[3072,128]{1,0:T(8,128)(2,1)S(1)}, u32[]{:S(2)}, u32[]{:S(2)}) collective-permute-start(bf16[3072,128]{1,0:T(8,128)(2,1)S(1)} %bitcast.31), channel_id=1, source_target_pairs={{0,16},{16,0},{32,48},{48,32},{64,80},{80,64},{96,112},{112,96},{1... | collective-permute-start | bytes 2359304 | tf_op jit(solution)/shard_map/ppermute | solution.py:612
